TPU v7x, 256 devices: a whole 4x4x8 slice. The times are simulated.
256 devices in a mesh: lon: 4 (over x), lat: 64 (over z, y, core).
Axes of the slice: x: 4, y: 4, z: 8, core: 2. Of those that a mesh axis runs over, the one named last changes fastest.
Arguments:
- grid_latent: bfloat16 [196608, 256], P(('lon', 'lat')), may hold values from -6 to 6
- mesh_latent: bfloat16 [8192, 256], P('lon'), may hold values from -6 to 6
- edge_latent: bfloat16 [524288, 256], P(('lon', 'lat')), may hold values from -6 to 6
- mesh_cotangent: bfloat16 [8192, 256], P('lon'), may hold values from -6 to 6
- edge_senders: int32 [524288], P(('lon', 'lat')), may hold values from 0 to 191
- edge_receivers: int32 [524288], P(('lon', 'lat')), may hold values from 0 to 2047
- send_rows: int32 [256, 192], P(('lon', 'lat')), may hold values from 0 to 767
- edge_count: int32 [256], P(('lon', 'lat')), may hold values from 1 to 2048, 393216 in all
- edge_first: bfloat16 [768, 256], replicated, may hold values from -0.21875 to 0.21875
- edge_second: bfloat16 [256, 256], replicated, may hold values from -0.375 to 0.375
- edge_gain: float32 [256], replicated, may hold values from 0.5 to 1.5
- node_first: bfloat16 [512, 256], replicated, may hold values from -0.25 to 0.25
- node_second: bfloat16 [256, 256], replicated, may hold values from -0.375 to 0.375
- node_gain: float32 [256], replicated, may hold values from 0.5 to 1.5
Outputs:
- mesh_out: bfloat16 [8192, 256], P(('lon', 'lat'))
- grid_grad: bfloat16 [196608, 256], P(('lon', 'lat'))
- mesh_grad: bfloat16 [8192, 256], P(('lon', 'lat'))
- edge_grad: bfloat16 [524288, 256], P(('lon', 'lat'))
Inputs may be any that keep to these rules, and one draw needn't show every extreme that they name: `edge_count`: the live slots of a block come first; some block is full.
All inputs are finite; a program needn't handle non-finite values.
Results may differ from a plain program's by a relative error of at most 0.015.
Values may be sent and summed in bfloat16 or wider, within the bound.
No kernel may reach another device: no remote copies, remote signals or barrier semaphores. Data moves between devices by JAX's collectives and lax.ppermute only.
A program may use at most 64 MiB of HBM per device.

v0:
```python
import jax
import jax.numpy as jnp
from jax import lax
from jax.sharding import PartitionSpec as P

eps = 1e-05


def with_halo(block, sides, width):
    for axis, dim in sides:
        count = lax.axis_size(axis)
        forward = [(i, i + 1) for i in range(count - 1)]
        forward.append((count - 1, 0))
        backward = [(target, source) for source, target in forward]
        low = lax.ppermute(
            lax.slice_in_dim(block, block.shape[dim] - width, None, axis=dim), axis, forward
        )
        high = lax.ppermute(lax.slice_in_dim(block, 0, width, axis=dim), axis, backward)
        block = jnp.concatenate([low, block, high], axis=dim)
    return block


def swish_grad(value):
    sigma = jax.nn.sigmoid(value)
    return sigma * (1.0 + value * (1.0 - sigma))


def norm_forward(value, gain):
    center = value - jnp.mean(value, axis=-1, keepdims=True)
    factor = lax.rsqrt(jnp.mean(center * center, axis=-1, keepdims=True) + eps)
    return center * factor * gain


def norm_backward(value, gain, upstream):
    center = value - jnp.mean(value, axis=-1, keepdims=True)
    factor = lax.rsqrt(jnp.mean(center * center, axis=-1, keepdims=True) + eps)
    normed = center * factor
    scaled = upstream * gain
    return factor * (
        scaled
        - jnp.mean(scaled, axis=-1, keepdims=True)
        - normed * jnp.mean(scaled * normed, axis=-1, keepdims=True)
    )


def node_pass(mesh_rows, aggregate, cotangent_rows, node_first, node_second, node_gain):
    width = mesh_rows.shape[1]
    agg_low = aggregate.astype(jnp.bfloat16)
    node_pre = jnp.dot(mesh_rows, node_first[0:width], preferred_element_type=jnp.float32)
    node_pre = node_pre + jnp.dot(
        agg_low, node_first[width : 2 * width], preferred_element_type=jnp.float32
    )
    node_act = jax.nn.silu(node_pre).astype(jnp.bfloat16)
    node_post = jnp.dot(node_act, node_second, preferred_element_type=jnp.float32)
    updated = (mesh_rows.astype(jnp.float32) + norm_forward(node_post, node_gain)).astype(
        jnp.bfloat16
    )
    cotangent = cotangent_rows.astype(jnp.float32)
    d_post = norm_backward(node_post, node_gain, cotangent).astype(jnp.bfloat16)
    d_pre = (
        jnp.dot(d_post, node_second.T, preferred_element_type=jnp.float32) * swish_grad(node_pre)
    ).astype(jnp.bfloat16)
    d_agg = jnp.dot(
        d_pre, node_first[width : 2 * width].T, preferred_element_type=jnp.float32
    ).astype(jnp.bfloat16)
    direct = cotangent + jnp.dot(d_pre, node_first[0:width].T, preferred_element_type=jnp.float32)
    return (updated, d_agg, direct)


def shards(
    grid_latent,
    mesh_latent,
    edge_latent,
    mesh_cotangent,
    edge_senders,
    edge_receivers,
    send_rows,
    edge_count,
    edge_first,
    edge_second,
    edge_gain,
    node_first,
    node_second,
    node_gain,
):
    width = grid_latent.shape[1]
    lat_count = lax.axis_size("lat")
    lat_pos = lax.axis_index("lat")
    listed = send_rows.shape[1]
    per_side = listed // 3
    patch_rows = mesh_latent.shape[0]
    own_rows = patch_rows // lat_count
    edges_dev = edge_latent.shape[0]
    w_edge = edge_first[0:width]
    w_grid = edge_first[width : 2 * width]
    w_mesh = edge_first[2 * width : 3 * width]
    row_list = send_rows.reshape(-1)
    outgoing = jnp.take(grid_latent, row_list, axis=0)
    outer = jnp.concatenate([outgoing[0:per_side], outgoing[2 * per_side :]], axis=0)
    padded = with_halo(outer, (("lon", 0),), per_side)
    arrived = jnp.concatenate(
        [
            padded[0:per_side],
            outgoing[per_side : 2 * per_side],
            padded[3 * per_side : 4 * per_side],
        ],
        axis=0,
    )
    projected = jnp.dot(arrived, w_grid, preferred_element_type=jnp.float32)
    patch_proj = jnp.dot(mesh_latent, w_mesh, preferred_element_type=jnp.float32)
    first = jnp.dot(edge_latent, w_edge, preferred_element_type=jnp.float32)
    first = first + jnp.take(patch_proj, edge_receivers, axis=0)
    first = first + jnp.take(projected, edge_senders, axis=0)
    live = (jnp.arange(edges_dev, dtype=jnp.int32) < edge_count[0]).astype(jnp.float32)[:, None]
    act = jax.nn.silu(first).astype(jnp.bfloat16)
    second = jnp.dot(act, edge_second, preferred_element_type=jnp.float32)
    fresh = live * norm_forward(second, edge_gain)
    partial_agg = jax.ops.segment_sum(fresh, edge_receivers, num_segments=patch_rows)
    own_start = lat_pos * own_rows
    aggregate = lax.psum_scatter(partial_agg, "lat", scatter_dimension=0, tiled=True)
    own_mesh = lax.dynamic_slice_in_dim(mesh_latent, own_start, own_rows, 0)
    own_cot = lax.dynamic_slice_in_dim(mesh_cotangent, own_start, own_rows, 0)
    mesh_out, own_d_agg, direct = node_pass(
        own_mesh, aggregate, own_cot, node_first, node_second, node_gain
    )
    d_agg = lax.all_gather(own_d_agg, "lat", axis=0, tiled=True)
    upstream = live * jnp.take(d_agg, edge_receivers, axis=0).astype(jnp.float32)
    d_second = norm_backward(second, edge_gain, upstream).astype(jnp.bfloat16)
    d_first = (
        jnp.dot(d_second, edge_second.T, preferred_element_type=jnp.float32) * swish_grad(first)
    ).astype(jnp.bfloat16)
    edge_grad = jnp.dot(d_first, w_edge.T, preferred_element_type=jnp.float32).astype(jnp.bfloat16)
    mesh_terms = jax.ops.segment_sum(
        jnp.dot(d_first, w_mesh.T, preferred_element_type=jnp.float32),
        edge_receivers,
        num_segments=patch_rows,
    )
    received = lax.psum_scatter(mesh_terms, "lat", scatter_dimension=0, tiled=True)
    mesh_grad = (direct + received).astype(jnp.bfloat16)
    slot_sums = jax.ops.segment_sum(
        jnp.dot(d_first, w_grid.T, preferred_element_type=jnp.float32),
        edge_senders,
        num_segments=listed,
    )
    back_outer = jnp.concatenate([slot_sums[0:per_side], slot_sums[2 * per_side :]], axis=0)
    back_padded = with_halo(back_outer.astype(jnp.bfloat16), (("lon", 0),), per_side).astype(
        back_outer.dtype
    )
    returned = jnp.concatenate(
        [
            back_padded[0:per_side],
            slot_sums[per_side : 2 * per_side],
            back_padded[3 * per_side : 4 * per_side],
        ],
        axis=0,
    )
    collected = jax.ops.segment_sum(returned, row_list, num_segments=grid_latent.shape[0])
    grid_grad = collected.astype(jnp.bfloat16)
    return (mesh_out, grid_grad, mesh_grad, edge_grad)


def solution(mesh):
    placed = (
        P(("lon", "lat"), None),
        P("lon", None),
        P(("lon", "lat"), None),
        P("lon", None),
        P(("lon", "lat")),
        P(("lon", "lat")),
        P(("lon", "lat"), None),
        P(("lon", "lat")),
        P(),
        P(),
        P(),
        P(),
        P(),
        P(),
    )
    return jax.shard_map(
        shards,
        mesh=mesh,
        in_specs=placed,
        out_specs=(
            P(("lon", "lat"), None),
            P(("lon", "lat"), None),
            P(("lon", "lat"), None),
            P(("lon", "lat"), None),
        ),
        check_vma=False,
    )
```

profile of v0, /device:TPU:1, one launch (start us, length us, event | category | flops | bytes accessed | tf_op | source)
XLA Modules:
  0.0 463.2 jit_solution(7793095055937622556)
XLA Ops:
  8.7 1.9 gather_fusion.1
  10.7 2.1 collective-permute-start
  17.7 1.7 fusion.37
  19.3 8.6 %gather_fusion = f32[2048,256]{1,0:T(8,128)} fusion(f32[2048,256]{1,0:T(8,128)S(1)} %fusion.37, s32[2048]{0:T(1024)S(1)} %fusion.71), kind=kCustom, calls=%fused_computation | custom fusion | bytes 4202496 | tf_op jit(solution)/shard_map/jit(_take)/gather | solution.py:112
  27.9 1.9 convolution_add_fusion
  31.1 8.6 %gather_fusion.2 = f32[2048,256]{1,0:T(8,128)} fusion(f32[192,256]{1,0:T(8,128)S(1)} %fusion.33, s32[2048]{0:T(1024)S(1)} %fusion.72), kind=kCustom, calls=%fused_computation.2 | custom fusion | bytes 4202496 | tf_op jit(solution)/shard_map/jit(_take)/gather | solution.py:113
  39.6 3.9 fusion.81
  43.5 1.9 copy.19
  46.1 14.5 %scatter_custom_fusion = f32[2048,256]{1,0:T(8,128)} fusion(s32[2048]{0:T(1024)} %param.19, f32[2048,256]{1,0:T(8,128)S(1)} %copy.19, f32[256]{0:T(256)S(1)} %copy-done.13, f32[2048]{0:T(1024)S(1)} %add_rsqrt_fusion, f32[2048]{0:T(1024)S(1)} %broadcast_multiply_fusion.2, f32[2048]{0:T(1024)S(1)} %fusion.70, f32[]{:T(128)} %constant.59.clone.1), kind=kCustom, calls=%fused_computation.16 | custom fusion | flops 2621440 | bytes 4220416 | tf_op jit(solution)/shard_map/scatter-add | solution.py:118
  62.4 136.4 %reduce-scatter.3.cloned.1.call-done = f32[32,256]{1,0:T(8,128)} async-done(((f32[2048,256]{1,0:T(8,128)}), f32[32,256]{1,0:T(8,128)}) %reduce-scatter.3.cloned.1.call-update) | async-done | bytes 32784 | tf_op jit(solution)/shard_map/reduce_scatter | solution.py:120
  201.2 1.5 fusion.53
  204.9 80.1 %all-gather.2.cloned.1.call-done = bf16[2048,256]{1,0:T(8,128)(2,1)} async-done(((bf16[32,256]{1,0:T(8,128)(2,1)}), bf16[2048,256]{1,0:T(8,128)(2,1)}) %all-gather.2.cloned.1.call-update) | async-done | bytes 1048592 | tf_op jit(solution)/shard_map/all_gather | solution.py:126
  285.0 9.9 %gather_fusion.3 = bf16[2048,256]{1,0:T(8,128)(2,1)} fusion(bf16[2048,256]{1,0:T(8,128)(2,1)} %all-gather.2.cloned.1.call-done, s32[2048]{0:T(1024)S(1)} %fusion.71), kind=kCustom, calls=%fused_computation.3 | custom fusion | bytes 2105344 | tf_op jit(solution)/shard_map/jit(_take)/gather | solution.py:127
  294.9 3.9 fusion.1
  298.9 6.9 %fusion = bf16[2048,256]{1,0:T(8,128)(2,1)S(1)} fusion(bf16[256,256]{1,0:T(8,128)(2,1)} %param.23, f32[2048,256]{1,0:T(8,128)S(1)} %copy.19, f32[2048]{0:T(1024)S(1)} %broadcast_multiply_fusion, f32[2048]{0:T(1024)S(1)} %broadcast_multiply_fusion.1, f32[256]{0:T(256)S(1)} %copy-done.14, f32[2048]{0:T(1024)} %copy-done.9, ...), kind=kOutput, calls=%fused_computation.10 | convolution fusion | flops 279969792 | bytes 8565760 | tf_op jit(solution)/shard_map/dot_general | solution.py:130
  306.8 1.8 fusion.35
  308.5 13.5 %scatter_custom_fusion.3 = f32[2048,256]{1,0:T(8,128)} fusion(s32[2048]{0:T(1024)} %param.19, f32[2048,256]{1,0:T(8,128)} %fusion.35, f32[]{:T(128)} %constant.59.clone.1), kind=kCustom, calls=%fused_computation.41 | custom fusion | flops 524288 | bytes 2097664 | tf_op jit(solution)/shard_map/scatter-add | solution.py:133
  322.0 1.8 fusion.31
  323.8 12.0 %scatter_custom_fusion.1 = f32[192,256]{1,0:T(8,128)S(1)} fusion(s32[2048]{0:T(1024)} %param.18, f32[2048,256]{1,0:T(8,128)} %fusion.31, f32[]{:T(128)} %constant.59.clone.1), kind=kCustom, calls=%fused_computation.73 | custom fusion | flops 524288 | bytes 197120 | tf_op jit(solution)/shard_map/scatter-add | solution.py:140
  337.1 1.5 collective-permute-start.3
  338.6 1.4 convolution_convert_fusion
  340.1 2.0 scatter_custom_fusion.2
  342.8 112.3 %reduce-scatter.5.cloned.1.call-done = f32[32,256]{1,0:T(8,128)} async-done(((f32[2048,256]{1,0:T(8,128)}), f32[32,256]{1,0:T(8,128)}) %reduce-scatter.5.cloned.1.call-update) | async-done | bytes 32784 | tf_op jit(solution)/shard_map/reduce_scatter | solution.py:138
  455.1 1.6 fusion.7
  (78 shorter events, 17.0 us)
Async XLA Ops:
  7.2 20.7 %copy-start = (bf16[2048,256]{1,0:T(8,128)(2,1)S(1)}, bf16[2048,256]{1,0:T(8,128)(2,1)}, u32[]{:S(2)}) copy-start(bf16[2048,256]{1,0:T(8,128)(2,1)} %param.16) | copy-start | bytes 3145732
  7.2 191.7 %reduce-scatter.3.cloned.1.call-start = ((), (), s32[]{:S(2)}) async-start(), calls=%async_computation.2 | async-start | bytes 2129920 | tf_op jit(solution)/shard_map/reduce_scatter | solution.py:120
  10.7 19.1 %collective-permute-start = (bf16[64,256]{1,0:T(8,128)(2,1)S(1)}, bf16[64,256]{1,0:T(8,128)(2,1)S(1)}, u32[]{:S(2)}, u32[]{:S(2)}) collective-permute-start(bf16[64,256]{1,0:T(8,128)(2,1)S(1)} %get-tuple-element.12), channel_id=1, source_target_pairs={{0,64},{64,128},{128,192},{192,0},{1,65},{65,129},{129,193},{193,1... | collective-permute-start | bytes 98312 | tf_op jit(solution)/shard_map/ppermute | solution.py:15
  12.8 17.0 %collective-permute-start.1 = (bf16[64,256]{1,0:T(8,128)(2,1)S(1)}, bf16[64,256]{1,0:T(8,128)(2,1)S(1)}, u32[]{:S(2)}, u32[]{:S(2)}) collective-permute-start(bf16[64,256]{1,0:T(8,128)(2,1)S(1)} %get-tuple-element.13), channel_id=1, source_target_pairs={{64,0},{128,64},{192,128},{0,192},{65,1},{129,65},{193,129},{1,193... | collective-permute-start | bytes 98312 | tf_op jit(solution)/shard_map/ppermute | solution.py:18
  14.9 280.0 %copy-start.12 = (pred[2048]{0:T(1024)(128)(4,1)}, pred[2048]{0:T(1024)(128)(4,1)S(1)}, u32[]{:S(2)}) copy-start(pred[2048]{0:T(1024)(128)(4,1)S(1)} %compare_and_fusion.1) | copy-start | bytes 6148
  17.0 22.6 %copy-start.15 = (pred[2048]{0:T(1024)(128)(4,1)}, pred[2048]{0:T(1024)(128)(4,1)S(1)}, u32[]{:S(2)}) copy-start(pred[2048]{0:T(1024)(128)(4,1)S(1)} %compare_and_fusion) | copy-start | bytes 6148
  29.8 9.9 %copy-start.4 = (f32[2048,256]{1,0:T(8,128)}, f32[2048,256]{1,0:T(8,128)S(1)}, u32[]{:S(2)}) copy-start(f32[2048,256]{1,0:T(8,128)S(1)} %convolution_add_fusion) | copy-start | bytes 6291460
  46.1 248.7 %copy-start.9 = (f32[2048]{0:T(1024)}, f32[2048]{0:T(1024)S(1)}, u32[]{:S(2)}) copy-start(f32[2048]{0:T(1024)S(1)} %add_rsqrt_fusion) | copy-start | bytes 24580
  60.6 0.9 copy-start.7
  60.6 140.5 %copy-start.17 = (f32[256]{0:T(256)S(1)}, f32[256]{0:T(256)}, u32[]{:S(2)}) copy-start(f32[256]{0:T(256)} %param.27) | copy-start | bytes 3076
  60.7 224.3 %all-gather.2.cloned.1.call-start = ((), (), s32[]{:S(2)}) async-start(), calls=%async_computation.3 | async-start | bytes 1064960 | tf_op jit(solution)/shard_map/all_gather | solution.py:126
  203.8 91.0 %copy-start.10 = (bf16[32,256]{1,0:T(8,128)(2,1)}, bf16[32,256]{1,0:T(8,128)(2,1)S(1)}, u32[]{:S(2)}) copy-start(bf16[32,256]{1,0:T(8,128)(2,1)S(1)} %fusion.6) | copy-start | bytes 49156
  204.7 250.4 %reduce-scatter.5.cloned.1.call-start = ((), (), s32[]{:S(2)}) async-start(), calls=%async_computation.4 | async-start | bytes 2129920 | tf_op jit(solution)/shard_map/reduce_scatter | solution.py:138
  294.9 4.0 copy-start.3
  294.9 4.0 copy-start.5
  294.9 4.0 copy-start.14
  294.9 4.0 copy-start.16
  298.9 7.9 %copy-start.6 = (bf16[768,256]{1,0:T(8,128)(2,1)S(1)}, bf16[768,256]{1,0:T(8,128)(2,1)}, u32[]{:S(2)}) copy-start(bf16[768,256]{1,0:T(8,128)(2,1)} %param.22) | copy-start | bytes 1179652
  305.8 1.0 copy-start.1
  308.5 13.5 %copy-start.2 = (bf16[2048,256]{1,0:T(8,128)(2,1)S(1)}, bf16[2048,256]{1,0:T(8,128)(2,1)}, u32[]{:S(2)}) copy-start(bf16[2048,256]{1,0:T(8,128)(2,1)} %copy-done.1) | copy-start | bytes 3145732
  335.8 4.2 collective-permute-start.2
  337.1 118.0 %copy-start.8 = (bf16[512,256]{1,0:T(8,128)(2,1)S(1)}, bf16[512,256]{1,0:T(8,128)(2,1)}, u32[]{:S(2)}) copy-start(bf16[512,256]{1,0:T(8,128)(2,1)} %param.25) | copy-start | bytes 786436
  337.1 118.0 %copy-start.11 = (bf16[32,256]{1,0:T(8,128)(2,1)S(1)}, bf16[32,256]{1,0:T(8,128)(2,1)}, u32[]{:S(2)}) copy-start(bf16[32,256]{1,0:T(8,128)(2,1)} %copy-done.10) | copy-start | bytes 49156
  337.1 2.9 collective-permute-start.3
  (1 other events, 0.7 us)
Sparse Core Ops, SparseCore 0:
  60.8 138.0 reduce-scatter.2
  204.8 80.1 all-gather.1
  322.1 132.9 reduce-scatter.4
where the time goes:
time: 468 us; the launch traced here: 463 us
  waiting for transfers between devices  329 us (70%)
  other arithmetic  53.4 us (11%)
  local copies, waits for them, and re-layouts  32.8 us (7%)
  matrix products  26.9 us (6%)
  between operations  14.7 us (3%)
  starting transfers between devices  6.53 us (1%)
    reduce_scatter x1, waiting for transfers between devices, shards(): lax.psum_scatter(partial_agg, 'lat', scatter_dimension=0, tiled=True)  136 us
    reduce_scatter x1, waiting for transfers between devices, shards(): lax.psum_scatter(mesh_terms, 'lat', scatter_dimension=0, tiled=True)  112 us
    all_gather x1, waiting for transfers between devices, shards(): d_agg = lax.all_gather(own_d_agg, 'lat', axis=0, tiled=True)  80.1 us
    scatter-add x1, other arithmetic, shards(): jax.ops.segment_sum(fresh, edge_receivers, num_segments=patch_rows)  14.5 us
    scatter-add x1, other arithmetic, shards(): jax.ops.segment_sum(jnp.dot(d_first, w_mesh.T, preferred_element_type=jnp...  13.5 us
    scatter-add x1, other arithmetic, shards(): jax.ops.segment_sum(jnp.dot(d_first, w_grid.T, preferred_element_type=jnp...  12 us
    gather x1, local copies, waits for them, and re-layouts, shards(): jnp.take(d_agg, edge_receivers, axis=0).astype(jnp.float32)  9.86 us
  transfers between devices with their start and end apart: 7, of which 3 were waited for; matrix products, arithmetic and copies ran while one was open for 7% of the time, Pallas kernels for 0%

commit v1 on v0

v1 whole, which is shorter than its diff:
```python
import jax
import jax.numpy as jnp
from jax import lax
from jax.experimental import pallas as pl
from jax.experimental.pallas import tpu as pltpu
from jax.sharding import Mesh
from jax.sharding import PartitionSpec as P

eps = 1e-05
f32 = jnp.float32
bf16 = jnp.bfloat16
i32 = jnp.int32

LANES = 128
CHUNK = 256
MIB = 1 << 20


def dot(a, b):
    return lax.dot_general(a, b, (((1,), (0,)), ((), ())), preferred_element_type=f32)


def dot_nt(a, b):
    return lax.dot_general(a, b, (((1,), (1,)), ((), ())), preferred_element_type=f32)


def dot_tn(a, b):
    return lax.dot_general(a, b, (((0,), (0,)), ((), ())), preferred_element_type=f32)


def split_dot_nt(a, b):
    high = a.astype(bf16)
    low = (a - high.astype(f32)).astype(bf16)
    return dot_nt(high, b) + dot_nt(low, b)


def one_hot(mask):
    return jnp.where(mask, 1.0, 0.0).astype(bf16)


def call(kernel, outs, args, smem=(), scratch=(), limit=48, flops=0, nbytes=0):
    specs = [
        pl.BlockSpec(memory_space=pltpu.SMEM if i in smem else pltpu.VMEM)
        for i in range(len(args))
    ]
    return pl.pallas_call(
        kernel,
        out_shape=[jax.ShapeDtypeStruct(s, d) for s, d in outs],
        in_specs=specs,
        out_specs=[pl.BlockSpec(memory_space=pltpu.VMEM) for _ in outs],
        scratch_shapes=list(scratch),
        compiler_params=pltpu.CompilerParams(vmem_limit_bytes=limit * MIB),
        cost_estimate=pl.CostEstimate(flops=flops, bytes_accessed=nbytes, transcendentals=0),
    )(*args)


def columns(rows_ref):
    return jnp.transpose(rows_ref[...])


def pair_column(cols, i):
    return jnp.concatenate([cols[:, 2 * i : 2 * i + 1], cols[:, 2 * i + 1 : 2 * i + 2]], axis=0)


def live_rows(rows_ref, count):
    rows = rows_ref[...]
    slot = lax.broadcasted_iota(i32, rows.shape, 0) * LANES + lax.broadcasted_iota(
        i32, rows.shape, 1
    )
    return jnp.where(slot < count, rows, -1)


def halo_rows_kernel(list_ref, grid_ref, low_ref, own_ref, high_ref):
    n = list_ref.shape[1]
    g = grid_ref.shape[0]
    hot = one_hot(lax.broadcasted_iota(i32, (g, n), 0) == list_ref[...])
    rows = dot_tn(hot, grid_ref[...]).astype(bf16)
    side = n // 3
    low_ref[...] = rows[0:side]
    own_ref[...] = rows[side : 2 * side]
    high_ref[...] = rows[2 * side :]


def mesh_rows_kernel(recv_ref, mesh_ref, out_ref):
    m = mesh_ref.shape[0]
    cols = columns(recv_ref)
    for i in range(out_ref.shape[0] // CHUNK):
        col = pair_column(cols, i)
        hot = one_hot(lax.broadcasted_iota(i32, (CHUNK, m), 1) == col)
        out_ref[i * CHUNK : (i + 1) * CHUNK, :] = dot(hot, mesh_ref[...]).astype(bf16)


def edge_forward_kernel(
    send_ref, edge_ref, mesh_rows_ref, low_ref, own_ref, high_ref, first_ref, second_ref,
    normed_ref, slope_ref,
):
    width = edge_ref.shape[1]
    listed = jnp.concatenate([low_ref[...], own_ref[...], high_ref[...]], axis=0)
    n = listed.shape[0]
    cols = columns(send_ref)
    for i in range(edge_ref.shape[0] // CHUNK):
        at = slice(i * CHUNK, (i + 1) * CHUNK)
        hot = one_hot(lax.broadcasted_iota(i32, (CHUNK, n), 1) == pair_column(cols, i))
        source = dot(hot, listed).astype(bf16)
        first = dot(edge_ref[at, :], first_ref[0:width, :])
        first = first + dot(source, first_ref[width : 2 * width, :])
        first = first + dot(mesh_rows_ref[at, :], first_ref[2 * width :, :])
        sigma = jax.nn.sigmoid(first)
        act = (first * sigma).astype(bf16)
        second = dot(act, second_ref[...])
        center = second - jnp.mean(second, axis=-1, keepdims=True)
        factor = lax.rsqrt(jnp.mean(center * center, axis=-1, keepdims=True) + eps)
        normed_ref[at, :] = (center * factor).astype(bf16)
        slope_ref[at, :] = (factor * (sigma * (1.0 + first * (1.0 - sigma)))).astype(bf16)


def half_row(i, core, own):
    return (i // own) * (2 * own) + core * own + i % own


def half_sum_kernel(own_rows, core_ref, count_ref, recv_ref, value_ref, out_ref):
    half = out_ref.shape[0]
    live = live_rows(recv_ref, count_ref[0])
    core = core_ref[0]
    step = CHUNK
    for j in range(half // step):
        row = half_row(
            lax.broadcasted_iota(i32, (step, LANES), 0) + j * step, core, own_rows
        )
        total = jnp.zeros((step, value_ref.shape[1]), f32)
        for i in range(value_ref.shape[0] // CHUNK):
            hot = jnp.concatenate(
                [
                    one_hot(row == live[2 * i : 2 * i + 1, :]),
                    one_hot(row == live[2 * i + 1 : 2 * i + 2, :]),
                ],
                axis=1,
            )
            total = total + dot(hot, value_ref[i * CHUNK : (i + 1) * CHUNK, :])
        out_ref[j * step : (j + 1) * step, :] = total.astype(bf16)


def norm(value):
    center = value - jnp.mean(value, axis=-1, keepdims=True)
    factor = lax.rsqrt(jnp.mean(center * center, axis=-1, keepdims=True) + eps)
    return center * factor, factor


def node_kernel(
    at_ref, parts_ref, mesh_ref, cot_ref, first_ref, second_ref, node_gain_ref, edge_gain_ref,
    out_ref, grad_ref, direct_ref,
):
    width = mesh_ref.shape[1]
    aggregate = jnp.sum(parts_ref[...].astype(f32), axis=0)
    agg_low = (aggregate * edge_gain_ref[...]).astype(bf16)
    mesh = mesh_ref[...]
    gain = node_gain_ref[...]
    pre = dot(mesh, first_ref[0:width, :]) + dot(agg_low, first_ref[width : 2 * width, :])
    sigma = jax.nn.sigmoid(pre)
    act = (pre * sigma).astype(bf16)
    post = dot(act, second_ref[...])
    normed, factor = norm(post)
    out_ref[...] = (mesh.astype(f32) + normed * gain).astype(bf16)
    cotangent = cot_ref[...].astype(f32)
    scaled = cotangent * gain
    d_post = factor * (
        scaled
        - jnp.mean(scaled, axis=-1, keepdims=True)
        - normed * jnp.mean(scaled * normed, axis=-1, keepdims=True)
    )
    d_pre = dot_nt(d_post.astype(bf16), second_ref[...]) * (sigma * (1.0 + pre * (1.0 - sigma)))
    d_pre = d_pre.astype(bf16)
    grad = dot_nt(d_pre, first_ref[width : 2 * width, :]).astype(bf16)
    grad_ref[...] = jnp.broadcast_to(grad[None], grad_ref.shape)
    direct_ref[...] = cotangent + dot_nt(d_pre, first_ref[0:width, :])


def edge_backward_kernel(
    own_rows, core_ref, count_ref, recv_ref, near_ref, far_ref, normed_ref, slope_ref, second_ref,
    gain_ref, out_ref,
):
    half = near_ref.shape[0]
    live = live_rows(recv_ref, count_ref[0])
    core = (live // own_rows) % 2
    place = (live // (2 * own_rows)) * own_rows + live % own_rows
    place = jnp.where(live < 0, -1, place + jnp.where(core == core_ref[0], 0, half))
    cols = jnp.transpose(place)
    gain = gain_ref[...]
    for i in range(out_ref.shape[0] // CHUNK):
        at = slice(i * CHUNK, (i + 1) * CHUNK)
        col = pair_column(cols, i)
        spot = lax.broadcasted_iota(i32, (CHUNK, half), 1)
        upstream = dot(one_hot(spot == col), near_ref[...])
        upstream = upstream + dot(one_hot(spot == col - half), far_ref[...])
        scaled = upstream * gain
        normed = normed_ref[at, :].astype(f32)
        inner = (
            scaled
            - jnp.mean(scaled, axis=-1, keepdims=True)
            - normed * jnp.mean(scaled * normed, axis=-1, keepdims=True)
        ).astype(bf16)
        out_ref[at, :] = (dot_nt(inner, second_ref[...]) * slope_ref[at, :].astype(f32)).astype(bf16)


def slot_sum_kernel(send_ref, d_first_ref, first_ref, low_ref, own_ref, high_ref):
    width = d_first_ref.shape[1]
    side = low_ref.shape[0]
    slots = 3 * side
    spot = lax.broadcasted_iota(i32, (slots, LANES), 0)
    total = jnp.zeros((slots, width), f32)
    for i in range(d_first_ref.shape[0] // CHUNK):
        hot = jnp.concatenate(
            [
                one_hot(spot == send_ref[2 * i : 2 * i + 1, :]),
                one_hot(spot == send_ref[2 * i + 1 : 2 * i + 2, :]),
            ],
            axis=1,
        )
        total = total + dot(hot, d_first_ref[i * CHUNK : (i + 1) * CHUNK, :])
    terms = split_dot_nt(total, first_ref[width : 2 * width, :]).astype(bf16)
    low_ref[...] = terms[0:side]
    own_ref[...] = terms[side : 2 * side]
    high_ref[...] = terms[2 * side :]


def edge_grad_kernel(d_first_ref, first_ref, out_ref):
    width = d_first_ref.shape[1]
    for i in range(out_ref.shape[0] // CHUNK):
        at = slice(i * CHUNK, (i + 1) * CHUNK)
        out_ref[at, :] = dot_nt(d_first_ref[at, :], first_ref[0:width, :]).astype(bf16)


def grid_grad_kernel(list_ref, low_ref, own_ref, high_ref, out_ref):
    terms = jnp.concatenate([low_ref[...], own_ref[...], high_ref[...]], axis=0)
    spot = lax.broadcasted_iota(i32, (out_ref.shape[0], terms.shape[0]), 0)
    out_ref[...] = dot(one_hot(spot == list_ref[...]), terms).astype(bf16)


def mesh_grad_kernel(parts_ref, direct_ref, first_ref, out_ref):
    width = direct_ref.shape[1]
    total = jnp.sum(parts_ref[...].astype(f32), axis=0)
    out_ref[...] = (
        direct_ref[...] + split_dot_nt(total, first_ref[2 * width : 3 * width, :])
    ).astype(bf16)


def ring(count, shift):
    return [(i, (i + shift) % count) for i in range(count)]


def shards(
    grid_latent,
    mesh_latent,
    edge_latent,
    mesh_cotangent,
    edge_senders,
    edge_receivers,
    send_rows,
    edge_count,
    edge_first,
    edge_second,
    edge_gain,
    node_first,
    node_second,
    node_gain,
):
    width = grid_latent.shape[1]
    zy = ("z", "y")
    lon_count = lax.axis_size("lon")
    owners = lax.axis_size("z") * lax.axis_size("y")
    core = lax.axis_index("core").astype(i32).reshape(1)
    other = 1 - core
    lat_pos = lax.axis_index(("z", "y", "core")).astype(i32).reshape(1)
    listed = send_rows.shape[1]
    side = listed // 3
    patch = mesh_latent.shape[0]
    own = patch // (2 * owners)
    half = patch // 2
    edges = edge_latent.shape[0]
    grid_rows = grid_latent.shape[0]
    recv = edge_receivers.reshape(edges // LANES, LANES)
    send = edge_senders.reshape(edges // LANES, LANES)
    swap = [(0, 1), (1, 0)]
    big = 2 * edges * patch * width
    dense = 2 * edges * width * width

    to_low, stay, to_high = call(
        halo_rows_kernel, [((side, width), bf16)] * 3, (send_rows, grid_latent),
        flops=2 * listed * grid_rows * width,
    )
    from_low = lax.ppermute(to_high, "lon", ring(lon_count, 1))
    from_high = lax.ppermute(to_low, "lon", ring(lon_count, -1))
    (mesh_rows,) = call(
        mesh_rows_kernel, [((edges, width), bf16)], (recv, mesh_latent), flops=big
    )
    normed, slope = call(
        edge_forward_kernel,
        [((edges, width), bf16)] * 2,
        (send, edge_latent, mesh_rows, from_low, stay, from_high, edge_first, edge_second),
        flops=5 * dense,
    )

    def half_sum(which, value):
        return call(
            lambda *refs: half_sum_kernel(own, *refs),
            [((half, width), bf16)],
            (which, edge_count, recv, value),
            smem=(0, 1),
            flops=big // 2,
        )[0]

    def to_owners(value):
        away = lax.ppermute(half_sum(other, value), "core", swap)
        here = half_sum(core, value)
        both = (here.astype(f32) + away.astype(f32)).astype(bf16)
        return lax.all_to_all(both.reshape(owners, own, width), zy, 0, 0, tiled=True)

    parts = to_owners(normed)

    def whole(*shape):
        return pl.BlockSpec(shape, lambda i, at: (0,) * len(shape))

    mesh_out, grad_copies, direct = pl.pallas_call(
        node_kernel,
        grid_spec=pltpu.PrefetchScalarGridSpec(
            num_scalar_prefetch=1,
            grid=(1,),
            in_specs=[
                whole(owners, own, width),
                pl.BlockSpec((own, width), lambda i, at: (at[0], 0)),
                pl.BlockSpec((own, width), lambda i, at: (at[0], 0)),
                whole(2 * width, width),
                whole(width, width),
                whole(1, width),
                whole(1, width),
            ],
            out_specs=[whole(own, width), whole(owners, own, width), whole(own, width)],
        ),
        out_shape=[
            jax.ShapeDtypeStruct((own, width), bf16),
            jax.ShapeDtypeStruct((owners, own, width), bf16),
            jax.ShapeDtypeStruct((own, width), f32),
        ],
        compiler_params=pltpu.CompilerParams(vmem_limit_bytes=32 * MIB),
    )(
        lat_pos, parts, mesh_latent, mesh_cotangent, node_first, node_second,
        node_gain.reshape(1, width), edge_gain.reshape(1, width),
    )
    near = lax.all_to_all(grad_copies, zy, 0, 0, tiled=True).reshape(half, width)
    far = lax.ppermute(near, "core", swap)
    (d_first,) = call(
        lambda *refs: edge_backward_kernel(own, *refs),
        [((edges, width), bf16)],
        (core, edge_count, recv, near, far, normed, slope, edge_second, edge_gain.reshape(1, width)),
        smem=(0, 1),
        flops=big + dense,
    )
    back_low, back_own, back_high = call(
        slot_sum_kernel, [((side, width), bf16)] * 3, (send, d_first, edge_first), flops=dense
    )
    got_low = lax.ppermute(back_high, "lon", ring(lon_count, 1))
    got_high = lax.ppermute(back_low, "lon", ring(lon_count, -1))
    mesh_parts = to_owners(d_first)
    (edge_grad,) = call(
        edge_grad_kernel, [((edges, width), bf16)], (d_first, edge_first), flops=dense
    )
    (grid_grad,) = call(
        grid_grad_kernel,
        [((grid_rows, width), bf16)],
        (send_rows, got_low, back_own, got_high),
        flops=2 * listed * grid_rows * width,
    )
    (mesh_grad,) = call(
        mesh_grad_kernel, [((own, width), bf16)], (mesh_parts, direct, edge_first)
    )
    return (mesh_out, grid_grad, mesh_grad, edge_grad)


def solution(mesh):
    fine = Mesh(mesh.devices.reshape(mesh.shape["lon"], 8, 4, 2), ("lon", "z", "y", "core"))
    every = ("lon", "z", "y", "core")
    rows = P(every, None)
    flat = P(every)
    patch = P("lon", None)
    return jax.shard_map(
        shards,
        mesh=fine,
        in_specs=(rows, patch, rows, patch, flat, flat, rows, flat) + (P(),) * 6,
        out_specs=(rows, rows, rows, rows),
        check_vma=False,
    )
```

time: 468 us -> 109 us (0.23)
  waiting for transfers between devices: 329 us -> 28.9 us
  other arithmetic: 53.4 us -> 1.89 us
  local copies, waits for them, and re-layouts: 32.8 us -> 5.1 us
  matrix products: 26.9 us -> 0 us
  Pallas kernels: 0 us -> 23.5 us
  starting transfers between devices: 6.53 us -> 27.3 us
  blocking collectives: 0 us -> 20.2 us
  between operations: 14.7 us -> 1.52 us
    reduce_scatter x2 -> x0, waiting for transfers between devices: 249 us -> none  [the longest x1 136 us: shards(): lax.psum_scatter(partial_agg, 'lat', scatter_dimension=0, tiled=True)]
    all_gather x1 -> x0, waiting for transfers between devices: 80.1 us -> none  [shards(): d_agg = lax.all_gather(own_d_agg, 'lat', axis=0, tiled=True)]
    scatter-add x4 -> x0, other arithmetic: 41.9 us -> none  [the longest x1 14.5 us: shards(): jax.ops.segment_sum(fresh, edge_receivers, num_segments=patch_rows)]
    gather x4 -> x0, local copies, waits for them, and re-layouts: 28.9 us -> none  [the longest x1 9.86 us: shards(): jnp.take(d_agg, edge_receivers, axis=0).astype(jnp.float32)]
    dot_general x14 -> x0, matrix products: 26.9 us -> none  [the longest x1 6.89 us: shards(): jnp.dot(d_second, edge_second.T, preferred_element_type=jnp.float32)]
    all_to_all x0 -> x2, waiting for transfers between devices: none -> 26.6 us  [to_owners(): lax.all_to_all(both.reshape(owners, own, width), zy, 0, 0, tiled=True)]
    pallas_call x0 -> x13, Pallas kernels: none -> 23.5 us  [the longest x12 22.2 us: call(): pl.pallas_call(kernel, out_shape=[jax.ShapeDtypeStruct(s, d) for s, d in...]
    all_to_all x0 -> x1, blocking collectives: none -> 20.2 us  [shards(): lax.all_to_all(grad_copies, zy, 0, 0, tiled=True).reshape(half, width)]
  transfers between devices with their start and end apart: 7 -> 9, of which waited for: 3 -> 6; matrix products, arithmetic and copies ran while one was open for 7% -> 0% of each run, Pallas kernels for 0% -> 7%
where the time goes in v1:
time: 109 us; the launch traced here: 108 us
  waiting for transfers between devices  28.9 us (27%)
  starting transfers between devices  27.3 us (25%)
  Pallas kernels  23.5 us (22%)
  blocking collectives  20.2 us (19%)
  local copies, waits for them, and re-layouts  5.1 us (5%)
  other arithmetic  1.89 us (2%)
  between operations  1.52 us (1%)
    all_to_all x2, waiting for transfers between devices, to_owners(): lax.all_to_all(both.reshape(owners, own, width), zy, 0, 0, tiled=True)  26.6 us
    pallas_call x12, Pallas kernels, call(): pl.pallas_call(kernel, out_shape=[jax.ShapeDtypeStruct(s, d) for s, d in...  22.2 us
    all_to_all x1, blocking collectives, shards(): lax.all_to_all(grad_copies, zy, 0, 0, tiled=True).reshape(half, width)  20.2 us
    all_to_all x2, starting transfers between devices, to_owners(): lax.all_to_all(both.reshape(owners, own, width), zy, 0, 0, tiled=True)  13.9 us
    unnamed x46, local copies, waits for them, and re-layouts  5.1 us
    ppermute x2, starting transfers between devices, to_owners(): away = lax.ppermute(half_sum(other, value), 'core', swap)  3.63 us
    ppermute x1, starting transfers between devices, shards(): far = lax.ppermute(near, 'core', swap)  3.57 us
    ppermute x1, starting transfers between devices, shards(): got_high = lax.ppermute(back_low, 'lon', ring(lon_count, -1))  2.66 us
  transfers between devices with their start and end apart: 9, of which 6 were waited for; matrix products, arithmetic and copies ran while one was open for 0% of the time, Pallas kernels for 7%

profile of v1, /device:TPU:1, one launch (start us, length us, event | category | flops | bytes accessed | tf_op | source)
XLA Modules:
  0.0 108.3 jit_solution(5070487470059004789)
XLA Ops:
  0.6 1.0 copy-done.4
  2.6 2.1 %collective-permute-start = (bf16[64,256]{1,0:T(8,128)(2,1)S(1)}, bf16[64,256]{1,0:T(8,128)(2,1)S(1)}, u32[]{:S(2)}, u32[]{:S(2)}) collective-permute-start(bf16[64,256]{1,0:T(8,128)(2,1)S(1)} %get-tuple-element.15), channel_id=1, source_target_pairs={{0,64},{64,128},{128,192},{192,0},{1,65},{65,129},{129,193},{193,1... | collective-permute-start | bytes 98312 | tf_op jit(solution)/shard_map/ppermute | solution.py:291
  4.7 1.4 %collective-permute-start.1 = (bf16[64,256]{1,0:T(8,128)(2,1)S(1)}, bf16[64,256]{1,0:T(8,128)(2,1)S(1)}, u32[]{:S(2)}, u32[]{:S(2)}) collective-permute-start(bf16[64,256]{1,0:T(8,128)(2,1)S(1)} %get-tuple-element.17), channel_id=1, source_target_pairs={{0,192},{64,0},{128,64},{192,128},{1,193},{65,1},{129,65},{193,129... | collective-permute-start | bytes 98312 | tf_op jit(solution)/shard_map/ppermute | solution.py:292
  6.1 1.2 %copy-done.1 = bf16[2048,256]{1,0:T(8,128)(2,1)S(1)} copy-done((bf16[2048,256]{1,0:T(8,128)(2,1)S(1)}, bf16[2048,256]{1,0:T(8,128)(2,1)}, u32[]{:S(2)}) %copy-start.1) | copy-done | bytes 1048600
  7.3 2.5 %shard_map.165.mesh_rows_ref = bf16[2048,256]{1,0:T(8,128)(2,1)S(1)} custom-call(s32[16,128]{1,0:T(8,128)S(1)} %bitcast.16, bf16[2048,256]{1,0:T(8,128)(2,1)S(1)} %copy-done.1), custom_call_target="tpu_custom_call" | custom-call | flops 2147483648 | tf_op jit(solution)/shard_map/pallas_call | solution.py:46
  10.6 4.1 %shard_map.167 = (bf16[2048,256]{1,0:T(8,128)(2,1)S(1)}, bf16[2048,256]{1,0:T(8,128)(2,1)S(1)}) custom-call(s32[16,128]{1,0:T(8,128)S(1)} %bitcast.11, bf16[2048,256]{1,0:T(8,128)(2,1)S(1)} %copy-done.14, bf16[2048,256]{1,0:T(8,128)(2,1)S(1)} %shard_map.165.mesh_rows_ref, bf16[64,256]{1,0:T(8,128)(2,1)S(1)} %collective-permute-done.low_ref, ...), custom_call_target="tpu_custom_call" | custom-call | flops 1342177280 | tf_op jit(solution)/shard_map/pallas_call | solution.py:46
  14.7 1.0 copy-done.21
  15.7 1.2 %shard_map.169 = bf16[1024,256]{1,0:T(8,128)(2,1)S(1)} custom-call(s32[1]{0:T(128)S(6)} %sub.3.refs_0_, s32[1]{0:T(128)S(6)} %copy.18.refs_1_, s32[16,128]{1,0:T(8,128)S(1)} %bitcast.17, bf16[2048,256]{1,0:T(8,128)(2,1)S(1)} %get-tuple-element.18.refs_3_.refs_5_), custom_call_target="tpu_custom_call" | custom-call | flops 1073741824 | tf_op jit(solution)/shard_map/pallas_call | solution.py:46
  16.9 3.2 %collective-permute-start.2 = (bf16[1024,256]{1,0:T(8,128)(2,1)S(1)}, bf16[1024,256]{1,0:T(8,128)(2,1)S(1)}, u32[]{:S(2)}, u32[]{:S(2)}) collective-permute-start(bf16[1024,256]{1,0:T(8,128)(2,1)S(1)} %shard_map.169), channel_id=1, source_target_pairs={{0,1},{1,0},{2,3},{3,2},{4,5},{5,4},{6,7},{7,6},{8,9},{9,8},{10,11... | collective-permute-start | bytes 1572872 | tf_op jit(solution)/shard_map/ppermute | solution.py:313
  20.1 1.2 %shard_map.168 = bf16[1024,256]{1,0:T(8,128)(2,1)S(1)} custom-call(s32[1]{0:T(128)} %bitcast.1.refs_0_, s32[1]{0:T(128)S(6)} %copy.18.refs_1_, s32[16,128]{1,0:T(8,128)S(1)} %bitcast.18, bf16[2048,256]{1,0:T(8,128)(2,1)S(1)} %get-tuple-element.18.refs_3_.refs_5_), custom_call_target="tpu_custom_call" | custom-call | flops 1073741824 | tf_op jit(solution)/shard_map/pallas_call | solution.py:46
  22.6 9.6 %all-to-all-start = ((bf16[32,32,256]{2,1,0:T(8,128)(2,1)}), bf16[32,32,256]{2,1,0:T(8,128)(2,1)S(1)}, u32[]{:S(2)}, u32[]{:S(2)}) async-start(bf16[32,32,256]{2,1,0:T(8,128)(2,1)} %bitcast.22), calls=%async_computation | async-start | bytes 1048576 | tf_op jit(solution)/shard_map/all_to_all | solution.py:316
  32.2 16.6 %all-to-all-done.parts_ref = bf16[32,32,256]{2,1,0:T(8,128)(2,1)S(1)} async-done(((bf16[32,32,256]{2,1,0:T(8,128)(2,1)}), bf16[32,32,256]{2,1,0:T(8,128)(2,1)S(1)}, u32[]{:S(2)}, u32[]{:S(2)}) %all-to-all-start) | async-done | bytes 524320 | tf_op jit(solution)/shard_map/all_to_all | solution.py:316
  49.4 1.2 %shard_map.170 = (bf16[32,256]{1,0:T(8,128)(2,1)}, bf16[32,32,256]{2,1,0:T(8,128)(2,1)S(1)}, f32[32,256]{1,0:T(8,128)S(1)}) custom-call(s32[1]{0:T(128)} %bitcast.at_ref, bf16[32,32,256]{2,1,0:T(8,128)(2,1)S(1)} %all-to-all-done.parts_ref, bf16[2048,256]{1,0:T(8,128)(2,1)S(1)} %copy-done.2, bf16[2048,256]{1,0:T(8,128)(2,1)S(1)} %copy-done.3, ...), custom_call_target="tpu_custom_call" | custom-call | tf_op jit(solution)/shard_map/pallas_call | solution.py:323
  50.7 20.2 %all_to_all.15 = bf16[32,32,256]{2,1,0:T(8,128)(2,1)S(1)} all-to-all(bf16[32,32,256]{2,1,0:T(8,128)(2,1)S(1)} %get-tuple-element.20), channel_id=1, replica_groups=mesh['lon'=4,'z'=8,'y'=4,'core'=2] {'z','y'}, dimensions={0} | all-to-all | bytes 1048576 | tf_op jit(solution)/shard_map/all_to_all | solution.py:349
  70.8 3.6 %collective-permute-start.3 = (bf16[1024,256]{1,0:T(8,128)(2,1)S(1)}, bf16[1024,256]{1,0:T(8,128)(2,1)S(1)}, u32[]{:S(2)}, u32[]{:S(2)}) collective-permute-start(bf16[1024,256]{1,0:T(8,128)(2,1)S(1)} %bitcast.9), channel_id=1, source_target_pairs={{0,1},{1,0},{2,3},{3,2},{4,5},{5,4},{6,7},{7,6},{8,9},{9,8},{10,11... | collective-permute-start | bytes 1572872 | tf_op jit(solution)/shard_map/ppermute | solution.py:350
  74.4 1.5 %collective-permute-done.3.refs_4_ = bf16[1024,256]{1,0:T(8,128)(2,1)S(1)} collective-permute-done((bf16[1024,256]{1,0:T(8,128)(2,1)S(1)}, bf16[1024,256]{1,0:T(8,128)(2,1)S(1)}, u32[]{:S(2)}, u32[]{:S(2)}) %collective-permute-start.3) | collective-permute-done | bytes 524320 | tf_op jit(solution)/shard_map/ppermute | solution.py:350
  76.0 6.4 %shard_map.171.d_first_ref.refs_3_ = bf16[2048,256]{1,0:T(8,128)(2,1)S(1)} custom-call(s32[1]{0:T(128)} %bitcast.1.refs_0_, s32[1]{0:T(128)S(6)} %copy.18.refs_1_, s32[16,128]{1,0:T(8,128)S(1)} %bitcast.19, bf16[1024,256]{1,0:T(8,128)(2,1)S(1)} %bitcast.10, bf16[1024,256]{1,0:T(8,128)(2,1)S(1)} %collective-permute-done.3.refs_4_, ...), custom_call_target="tpu_custom_call" | custom-call | flops 2415919104 | tf_op jit(solution)/shard_map/pallas_call | solution.py:46
  82.4 1.3 %shard_map.175 = bf16[1024,256]{1,0:T(8,128)(2,1)S(1)} custom-call(s32[1]{0:T(128)S(6)} %sub.3.refs_0_, s32[1]{0:T(128)S(6)} %copy.18.refs_1_, s32[16,128]{1,0:T(8,128)S(1)} %bitcast.20, bf16[2048,256]{1,0:T(8,128)(2,1)S(1)} %shard_map.171.d_first_ref.refs_3_), custom_call_target="tpu_custom_call" | custom-call | flops 1073741824 | tf_op jit(solution)/shard_map/pallas_call | solution.py:46
  84.1 1.2 %shard_map.174 = bf16[1024,256]{1,0:T(8,128)(2,1)S(1)} custom-call(s32[1]{0:T(128)} %bitcast.1.refs_0_, s32[1]{0:T(128)S(6)} %copy.18.refs_1_, s32[16,128]{1,0:T(8,128)S(1)} %bitcast.21, bf16[2048,256]{1,0:T(8,128)(2,1)S(1)} %shard_map.171.d_first_ref.refs_3_), custom_call_target="tpu_custom_call" | custom-call | flops 1073741824 | tf_op jit(solution)/shard_map/pallas_call | solution.py:46
  86.6 4.3 %all-to-all-start.2 = ((bf16[32,32,256]{2,1,0:T(8,128)(2,1)}), bf16[32,32,256]{2,1,0:T(8,128)(2,1)S(1)}, u32[]{:S(2)}, u32[]{:S(2)}) async-start(bf16[32,32,256]{2,1,0:T(8,128)(2,1)} %bitcast.8), calls=%async_computation.2 | async-start | bytes 1048576 | tf_op jit(solution)/shard_map/all_to_all | solution.py:316
  91.6 2.7 %collective-permute-start.5 = (bf16[64,256]{1,0:T(8,128)(2,1)S(1)}, bf16[64,256]{1,0:T(8,128)(2,1)S(1)}, u32[]{:S(2)}, u32[]{:S(2)}) collective-permute-start(bf16[64,256]{1,0:T(8,128)(2,1)S(1)} %get-tuple-element.24), channel_id=1, source_target_pairs={{0,192},{64,0},{128,64},{192,128},{1,193},{65,1},{129,65},{193,129... | collective-permute-start | bytes 98312 | tf_op jit(solution)/shard_map/ppermute | solution.py:362
  94.3 1.4 %shard_map.177 = bf16[2048,256]{1,0:T(8,128)(2,1)} custom-call(bf16[2048,256]{1,0:T(8,128)(2,1)S(1)} %shard_map.171.d_first_ref.refs_3_, bf16[768,256]{1,0:T(8,128)(2,1)S(1)} %copy-done), custom_call_target="tpu_custom_call" | custom-call | flops 268435456 | tf_op jit(solution)/shard_map/pallas_call | solution.py:46
  96.4 1.0 shard_map.173
  97.4 10.1 %all-to-all-done.2.parts_ref = bf16[32,32,256]{2,1,0:T(8,128)(2,1)S(1)} async-done(((bf16[32,32,256]{2,1,0:T(8,128)(2,1)}), bf16[32,32,256]{2,1,0:T(8,128)(2,1)S(1)}, u32[]{:S(2)}, u32[]{:S(2)}) %all-to-all-start.2) | async-done | bytes 524320 | tf_op jit(solution)/shard_map/all_to_all | solution.py:316
  (56 shorter events, 6.8 us)
Async XLA Ops:
  2.3 3.8 %copy-start.17 = (s32[2048]{0:T(1024)S(1)}, s32[2048]{0:T(1024)}, u32[]{:S(2)}) copy-start(s32[2048]{0:T(1024)} %param.19) | copy-start | bytes 24580
  2.6 7.9 %collective-permute-start = (bf16[64,256]{1,0:T(8,128)(2,1)S(1)}, bf16[64,256]{1,0:T(8,128)(2,1)S(1)}, u32[]{:S(2)}, u32[]{:S(2)}) collective-permute-start(bf16[64,256]{1,0:T(8,128)(2,1)S(1)} %get-tuple-element.15), channel_id=1, source_target_pairs={{0,64},{64,128},{128,192},{192,0},{1,65},{65,129},{129,193},{193,1... | collective-permute-start | bytes 98312 | tf_op jit(solution)/shard_map/ppermute | solution.py:291
  4.7 5.8 %collective-permute-start.1 = (bf16[64,256]{1,0:T(8,128)(2,1)S(1)}, bf16[64,256]{1,0:T(8,128)(2,1)S(1)}, u32[]{:S(2)}, u32[]{:S(2)}) collective-permute-start(bf16[64,256]{1,0:T(8,128)(2,1)S(1)} %get-tuple-element.17), channel_id=1, source_target_pairs={{0,192},{64,0},{128,64},{192,128},{1,193},{65,1},{129,65},{193,129... | collective-permute-start | bytes 98312 | tf_op jit(solution)/shard_map/ppermute | solution.py:292
  7.3 3.2 %copy-start.14 = (bf16[2048,256]{1,0:T(8,128)(2,1)S(1)}, bf16[2048,256]{1,0:T(8,128)(2,1)}, u32[]{:S(2)}) copy-start(bf16[2048,256]{1,0:T(8,128)(2,1)} %edge_ref.1) | copy-start | bytes 3145732
  7.3 3.3 %copy-start.15 = (bf16[256,256]{1,0:T(8,128)(2,1)S(1)}, bf16[256,256]{1,0:T(8,128)(2,1)}, u32[]{:S(2)}) copy-start(bf16[256,256]{1,0:T(8,128)(2,1)} %refs_7_.1) | copy-start | bytes 393220
  15.7 4.4 %copy-start.19 = (bf16[2048,256]{1,0:T(8,128)(2,1)}, bf16[2048,256]{1,0:T(8,128)(2,1)S(1)}, u32[]{:S(2)}) copy-start(bf16[2048,256]{1,0:T(8,128)(2,1)S(1)} %get-tuple-element.18.refs_3_.refs_5_) | copy-start | bytes 3145732
  16.9 4.7 %collective-permute-start.2 = (bf16[1024,256]{1,0:T(8,128)(2,1)S(1)}, bf16[1024,256]{1,0:T(8,128)(2,1)S(1)}, u32[]{:S(2)}, u32[]{:S(2)}) collective-permute-start(bf16[1024,256]{1,0:T(8,128)(2,1)S(1)} %shard_map.169), channel_id=1, source_target_pairs={{0,1},{1,0},{2,3},{3,2},{4,5},{5,4},{6,7},{7,6},{8,9},{9,8},{10,11... | collective-permute-start | bytes 1572872 | tf_op jit(solution)/shard_map/ppermute | solution.py:313
  21.3 27.4 %copy-start.2 = (bf16[2048,256]{1,0:T(8,128)(2,1)S(1)}, bf16[2048,256]{1,0:T(8,128)(2,1)}, u32[]{:S(2)}) copy-start(bf16[2048,256]{1,0:T(8,128)(2,1)} %mesh_ref.3) | copy-start | bytes 3145732
  21.4 27.4 %copy-start.3 = (bf16[2048,256]{1,0:T(8,128)(2,1)S(1)}, bf16[2048,256]{1,0:T(8,128)(2,1)}, u32[]{:S(2)}) copy-start(bf16[2048,256]{1,0:T(8,128)(2,1)} %cot_ref.1) | copy-start | bytes 3145732
  22.6 26.2 %copy-start.5 = (bf16[512,256]{1,0:T(8,128)(2,1)S(1)}, bf16[512,256]{1,0:T(8,128)(2,1)}, u32[]{:S(2)}) copy-start(bf16[512,256]{1,0:T(8,128)(2,1)} %first_ref.6) | copy-start | bytes 786436
  22.6 26.2 %copy-start.6 = (bf16[256,256]{1,0:T(8,128)(2,1)S(1)}, bf16[256,256]{1,0:T(8,128)(2,1)}, u32[]{:S(2)}) copy-start(bf16[256,256]{1,0:T(8,128)(2,1)} %second_ref.3) | copy-start | bytes 393220
  22.6 26.2 %copy-start.13 = (f32[256]{0:T(256)S(1)}, f32[256]{0:T(256)}, u32[]{:S(2)}) copy-start(f32[256]{0:T(256)} %param.24) | copy-start | bytes 3076
  22.6 26.2 %all-to-all-start = ((bf16[32,32,256]{2,1,0:T(8,128)(2,1)}), bf16[32,32,256]{2,1,0:T(8,128)(2,1)S(1)}, u32[]{:S(2)}, u32[]{:S(2)}) async-start(bf16[32,32,256]{2,1,0:T(8,128)(2,1)} %bitcast.22), calls=%async_computation | async-start | bytes 1048576 | tf_op jit(solution)/shard_map/all_to_all | solution.py:316
  49.4 26.5 %copy-start.20 = (bf16[2048,256]{1,0:T(8,128)(2,1)S(1)}, bf16[2048,256]{1,0:T(8,128)(2,1)}, u32[]{:S(2)}) copy-start(bf16[2048,256]{1,0:T(8,128)(2,1)} %copy-done.19) | copy-start | bytes 3145732
  49.4 26.5 %copy-start.22 = (bf16[2048,256]{1,0:T(8,128)(2,1)S(1)}, bf16[2048,256]{1,0:T(8,128)(2,1)}, u32[]{:S(2)}) copy-start(bf16[2048,256]{1,0:T(8,128)(2,1)} %copy-done.21) | copy-start | bytes 3145732
  50.7 20.2 %copy-start.7 = (f32[32,256]{1,0:T(8,128)}, f32[32,256]{1,0:T(8,128)S(1)}, u32[]{:S(2)}) copy-start(f32[32,256]{1,0:T(8,128)S(1)} %get-tuple-element.25.direct_ref) | copy-start | bytes 98308
  50.7 25.3 %copy-start.16 = (bf16[256,256]{1,0:T(8,128)(2,1)S(1)}, bf16[256,256]{1,0:T(8,128)(2,1)}, u32[]{:S(2)}) copy-start(bf16[256,256]{1,0:T(8,128)(2,1)} %refs_7_.1) | copy-start | bytes 393220
  50.7 25.3 %copy-start.18 = (s32[2048]{0:T(1024)S(1)}, s32[2048]{0:T(1024)}, u32[]{:S(2)}) copy-start(s32[2048]{0:T(1024)} %param.19) | copy-start | bytes 24580
  70.8 5.1 %collective-permute-start.3 = (bf16[1024,256]{1,0:T(8,128)(2,1)S(1)}, bf16[1024,256]{1,0:T(8,128)(2,1)S(1)}, u32[]{:S(2)}, u32[]{:S(2)}) collective-permute-start(bf16[1024,256]{1,0:T(8,128)(2,1)S(1)} %bitcast.9), channel_id=1, source_target_pairs={{0,1},{1,0},{2,3},{3,2},{4,5},{5,4},{6,7},{7,6},{8,9},{9,8},{10,11... | collective-permute-start | bytes 1572872 | tf_op jit(solution)/shard_map/ppermute | solution.py:350
  83.7 2.0 %collective-permute-start.6 = (bf16[1024,256]{1,0:T(8,128)(2,1)S(1)}, bf16[1024,256]{1,0:T(8,128)(2,1)S(1)}, u32[]{:S(2)}, u32[]{:S(2)}) collective-permute-start(bf16[1024,256]{1,0:T(8,128)(2,1)S(1)} %shard_map.175), channel_id=1, source_target_pairs={{0,1},{1,0},{2,3},{3,2},{4,5},{5,4},{6,7},{7,6},{8,9},{9,8},{10,11... | collective-permute-start | bytes 1572872 | tf_op jit(solution)/shard_map/ppermute | solution.py:313
  86.6 20.8 %all-to-all-start.2 = ((bf16[32,32,256]{2,1,0:T(8,128)(2,1)}), bf16[32,32,256]{2,1,0:T(8,128)(2,1)S(1)}, u32[]{:S(2)}, u32[]{:S(2)}) async-start(bf16[32,32,256]{2,1,0:T(8,128)(2,1)} %bitcast.8), calls=%async_computation.2 | async-start | bytes 1048576 | tf_op jit(solution)/shard_map/all_to_all | solution.py:316
  91.5 4.3 %collective-permute-start.4 = (bf16[64,256]{1,0:T(8,128)(2,1)S(1)}, bf16[64,256]{1,0:T(8,128)(2,1)S(1)}, u32[]{:S(2)}, u32[]{:S(2)}) collective-permute-start(bf16[64,256]{1,0:T(8,128)(2,1)S(1)} %get-tuple-element.22), channel_id=1, source_target_pairs={{0,64},{64,128},{128,192},{192,0},{1,65},{65,129},{129,193},{193,1... | collective-permute-start | bytes 98312 | tf_op jit(solution)/shard_map/ppermute | solution.py:361
  91.6 4.3 %collective-permute-start.5 = (bf16[64,256]{1,0:T(8,128)(2,1)S(1)}, bf16[64,256]{1,0:T(8,128)(2,1)S(1)}, u32[]{:S(2)}, u32[]{:S(2)}) collective-permute-start(bf16[64,256]{1,0:T(8,128)(2,1)S(1)} %get-tuple-element.24), channel_id=1, source_target_pairs={{0,192},{64,0},{128,64},{192,128},{1,193},{65,1},{129,65},{193,129... | collective-permute-start | bytes 98312 | tf_op jit(solution)/shard_map/ppermute | solution.py:362
  96.4 11.1 %copy-start.8 = (f32[32,256]{1,0:T(8,128)S(1)}, f32[32,256]{1,0:T(8,128)}, u32[]{:S(2)}) copy-start(f32[32,256]{1,0:T(8,128)} %copy-done.7) | copy-start | bytes 98308
  (8 other events, 9.2 us)

commit v2 on v1

v2 whole, which is shorter than its diff:
```python
import jax
import jax.numpy as jnp
from jax import lax
from jax.experimental import pallas as pl
from jax.experimental.pallas import tpu as pltpu
from jax.sharding import Mesh
from jax.sharding import PartitionSpec as P

eps = 1e-05
f32 = jnp.float32
bf16 = jnp.bfloat16
i32 = jnp.int32

LANES = 128
CHUNK = 256
MIB = 1 << 20


def dot(a, b):
    return lax.dot_general(a, b, (((1,), (0,)), ((), ())), preferred_element_type=f32)


def dot_nt(a, b):
    return lax.dot_general(a, b, (((1,), (1,)), ((), ())), preferred_element_type=f32)


def dot_tn(a, b):
    return lax.dot_general(a, b, (((0,), (0,)), ((), ())), preferred_element_type=f32)


def split_dot_nt(a, b):
    high = a.astype(bf16)
    low = (a - high.astype(f32)).astype(bf16)
    return dot_nt(high, b) + dot_nt(low, b)


def one_hot(mask):
    return jnp.where(mask, 1.0, 0.0).astype(bf16)


def call(kernel, outs, args, smem=(), hbm=(), scratch=(), limit=16, flops=0, name=None):
    def space(i):
        if i in smem:
            return pltpu.SMEM
        return pltpu.HBM if i in hbm else pltpu.VMEM

    return pl.pallas_call(
        kernel,
        out_shape=[jax.ShapeDtypeStruct(s, d) for s, d in outs],
        in_specs=[pl.BlockSpec(memory_space=space(i)) for i in range(len(args))],
        out_specs=[pl.BlockSpec(memory_space=pltpu.VMEM) for _ in outs],
        scratch_shapes=list(scratch),
        compiler_params=pltpu.CompilerParams(vmem_limit_bytes=limit * MIB),
        cost_estimate=pl.CostEstimate(flops=flops, bytes_accessed=0, transcendentals=0),
        name=name,
    )(*args)


def column(cols, start, size):
    parts = [cols[:, j : j + 1] for j in range(start // LANES, (start + size) // LANES)]
    return parts[0] if len(parts) == 1 else jnp.concatenate(parts, axis=0)


def row_hot(spot, rows, start, size):
    parts = [one_hot(spot == rows[j : j + 1, :]) for j in range(start // LANES, (start + size) // LANES)]
    return jnp.concatenate(parts, axis=1)


def chunks(rows, size):
    return [(at, slice(at, at + size)) for at in range(0, rows, size)]


def live_rows(rows_ref, count):
    rows = rows_ref[...]
    slot = lax.broadcasted_iota(i32, rows.shape, 0) * LANES + lax.broadcasted_iota(
        i32, rows.shape, 1
    )
    return jnp.where(slot < count, rows, -1)


def halo_rows_kernel(list_ref, grid_ref, low_ref, own_ref, high_ref):
    n = list_ref.shape[1]
    g = grid_ref.shape[0]
    hot = one_hot(lax.broadcasted_iota(i32, (g, n), 0) == list_ref[...])
    rows = dot_tn(hot, grid_ref[...]).astype(bf16)
    side = n // 3
    low_ref[...] = rows[0:side]
    own_ref[...] = rows[side : 2 * side]
    high_ref[...] = rows[2 * side :]


def mesh_rows_kernel(recv_ref, mesh_ref, out_ref, own_ref):
    own = own_ref.shape[0]
    own_ref[...] = mesh_ref[pl.ds(pl.multiple_of(my_block() * own, own), own), :]
    m = mesh_ref.shape[0]
    cols = jnp.transpose(recv_ref[...])
    for start, at in chunks(out_ref.shape[0], LANES):
        hot = one_hot(lax.broadcasted_iota(i32, (LANES, m), 1) == column(cols, start, LANES))
        out_ref[at, :] = dot(hot, mesh_ref[...]).astype(bf16)


def edge_forward_kernel(
    send_ref, edge_ref, mesh_rows_ref, low_ref, own_ref, high_ref, first_ref, second_ref,
    cot_ref, node_gain_ref, edge_gain_ref, normed_ref, slope_ref, own_cot_ref, gains_ref,
    work_ref, post_ref,
):
    own = own_cot_ref.shape[0]
    own_cot_ref[...] = cot_ref[pl.ds(pl.multiple_of(my_block() * own, own), own), :]
    gains_ref[0:1, :] = node_gain_ref[...]
    gains_ref[1:2, :] = edge_gain_ref[...]
    listed = jnp.concatenate([low_ref[...], own_ref[...], high_ref[...]], axis=0)
    n = listed.shape[0]
    cols = jnp.transpose(send_ref[...])
    parts = chunks(edge_ref.shape[0], CHUNK)
    for start, at in parts:
        hot = one_hot(lax.broadcasted_iota(i32, (CHUNK, n), 1) == column(cols, start, CHUNK))
        source = dot(hot, listed).astype(bf16)
        given = jnp.concatenate([edge_ref[at, :], source, mesh_rows_ref[at, :]], axis=1)
        work_ref[at, :] = dot(given, first_ref[...])
    for _, at in parts:
        first = work_ref[at, :]
        sigma = jax.nn.sigmoid(first)
        act = first * sigma
        work_ref[at, :] = sigma + act * (1.0 - sigma)
        post_ref[at, :] = dot(act.astype(bf16), second_ref[...])
    for _, at in parts:
        normed, factor = norm(post_ref[at, :])
        normed_ref[at, :] = normed.astype(bf16)
        slope_ref[at, :] = (factor * work_ref[at, :]).astype(bf16)


def my_core():
    return lax.axis_index("core").astype(i32)


def my_block():
    return (lax.axis_index("z") * 8 + lax.axis_index("y") * 2 + lax.axis_index("core")).astype(i32)


def half_row(i, core, own):
    return (i // own) * (2 * own) + core * own + i % own


def half_rows(own, core, live, value_ref, start):
    spot = half_row(lax.broadcasted_iota(i32, (CHUNK, LANES), 0) + start, core, own)
    total = jnp.zeros((CHUNK, value_ref.shape[1]), f32)
    for begin, at in chunks(value_ref.shape[0], CHUNK):
        total = total + dot(row_hot(spot, live, begin, CHUNK), value_ref[at, :])
    return total


def half_sum_kernel(own, here, count_ref, recv_ref, value_ref, out_ref):
    live = live_rows(recv_ref, count_ref[0])
    core = my_core() if here else 1 - my_core()
    for start, at in chunks(out_ref.shape[0], CHUNK):
        out_ref[at, :] = half_rows(own, core, live, value_ref, start).astype(out_ref.dtype)


def half_total_kernel(own, count_ref, recv_ref, value_ref, begun_ref, away_ref, out_ref):
    done = begun_ref.shape[0]
    live = live_rows(recv_ref, count_ref[0])
    for start, at in chunks(out_ref.shape[0], CHUNK):
        if start < done:
            here = begun_ref[at, :]
        else:
            here = half_rows(own, my_core(), live, value_ref, start)
        out_ref[at, :] = (here + away_ref[at, :].astype(f32)).astype(bf16)


def norm(value):
    center = value - jnp.mean(value, axis=-1, keepdims=True)
    factor = lax.rsqrt(jnp.mean(center * center, axis=-1, keepdims=True) + eps)
    return center * factor, factor


def node_kernel(
    parts_ref, mesh_ref, cot_ref, first_ref, second_ref, gains_ref, out_ref, grad_ref, direct_ref,
):
    width = mesh_ref.shape[1]
    aggregate = jnp.sum(parts_ref[...].astype(f32), axis=0)
    agg_low = (aggregate * gains_ref[1:2, :]).astype(bf16)
    mesh = mesh_ref[...]
    gain = gains_ref[0:1, :]
    pre = dot(mesh, first_ref[0:width, :]) + dot(agg_low, first_ref[width : 2 * width, :])
    sigma = jax.nn.sigmoid(pre)
    act = (pre * sigma).astype(bf16)
    post = dot(act, second_ref[...])
    normed, factor = norm(post)
    out_ref[...] = (mesh.astype(f32) + normed * gain).astype(bf16)
    cotangent = cot_ref[...].astype(f32)
    scaled = cotangent * gain
    d_post = factor * (
        scaled
        - jnp.mean(scaled, axis=-1, keepdims=True)
        - normed * jnp.mean(scaled * normed, axis=-1, keepdims=True)
    )
    d_pre = dot_nt(d_post.astype(bf16), second_ref[...]) * (sigma * (1.0 + pre * (1.0 - sigma)))
    d_pre = d_pre.astype(bf16)
    grad = dot_nt(d_pre, first_ref[width : 2 * width, :]).astype(bf16)
    grad_ref[...] = jnp.broadcast_to(grad[None], grad_ref.shape)
    direct_ref[...] = cotangent + dot_nt(d_pre, first_ref[0:width, :])


def half_place(own, core, live):
    place = (live // (2 * own)) * own + live % own
    return jnp.where((live // own) % 2 == core, place, -1)


def near_rows_kernel(own, count_ref, recv_ref, near_ref, out_ref):
    half = near_ref.shape[0]
    place = half_place(own, my_core(), live_rows(recv_ref, count_ref[0]))
    cols = jnp.transpose(place)
    for start, at in chunks(out_ref.shape[0], LANES):
        hot = one_hot(lax.broadcasted_iota(i32, (LANES, half), 1) == column(cols, start, LANES))
        out_ref[at, :] = dot(hot, near_ref[...]).astype(bf16)


def edge_backward_kernel(
    own, count_ref, recv_ref, near_rows_ref, far_ref, normed_ref, slope_ref, second_ref,
    gains_ref, out_ref, work_ref,
):
    half = far_ref.shape[0]
    place = half_place(own, 1 - my_core(), live_rows(recv_ref, count_ref[0]))
    cols = jnp.transpose(place)
    for start, at in chunks(out_ref.shape[0], LANES):
        hot = one_hot(lax.broadcasted_iota(i32, (LANES, half), 1) == column(cols, start, LANES))
        work_ref[at, :] = dot(hot, far_ref[...]) + near_rows_ref[at, :].astype(f32)
    gain = gains_ref[1:2, :]
    for _, at in chunks(out_ref.shape[0], CHUNK):
        scaled = work_ref[at, :] * gain
        normed = normed_ref[at, :].astype(f32)
        inner = (
            scaled
            - jnp.mean(scaled, axis=-1, keepdims=True)
            - normed * jnp.mean(scaled * normed, axis=-1, keepdims=True)
        ).astype(bf16)
        out_ref[at, :] = (dot_nt(inner, second_ref[...]) * slope_ref[at, :].astype(f32)).astype(bf16)


def slot_sum_kernel(send_ref, d_first_ref, first_ref, low_ref, own_ref, high_ref):
    width = d_first_ref.shape[1]
    side = low_ref.shape[0]
    spot = lax.broadcasted_iota(i32, (3 * side, LANES), 0)
    total = jnp.zeros((3 * side, width), f32)
    for start, at in chunks(d_first_ref.shape[0], CHUNK):
        total = total + dot(row_hot(spot, send_ref, start, CHUNK), d_first_ref[at, :])
    terms = split_dot_nt(total, first_ref[width : 2 * width, :]).astype(bf16)
    low_ref[...] = terms[0:side]
    own_ref[...] = terms[side : 2 * side]
    high_ref[...] = terms[2 * side :]


def edge_grad_kernel(d_first_ref, first_ref, out_ref):
    width = d_first_ref.shape[1]
    for i in range(out_ref.shape[0] // CHUNK):
        at = slice(i * CHUNK, (i + 1) * CHUNK)
        out_ref[at, :] = dot_nt(d_first_ref[at, :], first_ref[0:width, :]).astype(bf16)


def grid_grad_kernel(list_ref, low_ref, own_ref, high_ref, out_ref):
    terms = jnp.concatenate([low_ref[...], own_ref[...], high_ref[...]], axis=0)
    spot = lax.broadcasted_iota(i32, (out_ref.shape[0], terms.shape[0]), 0)
    out_ref[...] = dot(one_hot(spot == list_ref[...]), terms).astype(bf16)


def mesh_grad_kernel(parts_ref, direct_ref, first_ref, out_ref):
    width = direct_ref.shape[1]
    total = jnp.sum(parts_ref[...].astype(f32), axis=0)
    out_ref[...] = (
        direct_ref[...] + split_dot_nt(total, first_ref[2 * width : 3 * width, :])
    ).astype(bf16)


def ring(count, shift):
    return [(i, (i + shift) % count) for i in range(count)]


def shards(
    grid_latent,
    mesh_latent,
    edge_latent,
    mesh_cotangent,
    edge_senders,
    edge_receivers,
    send_rows,
    edge_count,
    edge_first,
    edge_second,
    edge_gain,
    node_first,
    node_second,
    node_gain,
):
    width = grid_latent.shape[1]
    zy = ("z", "y")
    lon_count = lax.axis_size("lon")
    owners = lax.axis_size("z") * lax.axis_size("y")
    listed = send_rows.shape[1]
    side = listed // 3
    patch = mesh_latent.shape[0]
    own = patch // (2 * owners)
    half = patch // 2
    edges = edge_latent.shape[0]
    grid_rows = grid_latent.shape[0]
    recv = edge_receivers.reshape(edges // LANES, LANES)
    send = edge_senders.reshape(edges // LANES, LANES)
    swap = [(0, 1), (1, 0)]
    big = 2 * edges * patch * width
    dense = 2 * edges * width * width

    vm = pltpu.VMEM
    to_low, stay, to_high = call(
        halo_rows_kernel,
        [((side, width), bf16)] * 3,
        (send_rows, grid_latent),
        flops=2 * listed * grid_rows * width,
        name="halo_rows",
    )
    from_low = lax.ppermute(to_high, "lon", ring(lon_count, 1))
    from_high = lax.ppermute(to_low, "lon", ring(lon_count, -1))
    mesh_rows, own_mesh = call(
        mesh_rows_kernel, [((edges, width), bf16), ((own, width), bf16)], (recv, mesh_latent),
        flops=big,
        name="mesh_rows",
    )
    normed, slope, own_cot, gains = call(
        edge_forward_kernel,
        [((edges, width), bf16)] * 2 + [((own, width), bf16), ((2, width), f32)],
        (
            send, edge_latent, mesh_rows, from_low, stay, from_high, edge_first, edge_second,
            mesh_cotangent, node_gain.reshape(1, width), edge_gain.reshape(1, width),
        ),
        scratch=[vm((edges, width), f32)] * 2,
        flops=5 * dense,
        name="edge_forward",
    )

    def to_owners(value):
        shape = (half, width)
        begun = half - CHUNK
        (out,) = call(
            lambda *refs: half_sum_kernel(own, False, *refs), [(shape, bf16)],
            (edge_count, recv, value), smem=(0,), flops=big // 2, name="half_away",
        )
        away = lax.ppermute(out, "core", swap)
        (here,) = call(
            lambda *refs: half_sum_kernel(own, True, *refs), [((begun, width), f32)],
            (edge_count, recv, value), smem=(0,), flops=big // 2, name="half_here",
        )
        (both,) = call(
            lambda *refs: half_total_kernel(own, *refs), [(shape, bf16)],
            (edge_count, recv, value, here, away), smem=(0,), flops=big // 8,
            name="half_total",
        )
        return lax.all_to_all(both.reshape(owners, own, width), zy, 0, 0, tiled=True)

    parts = to_owners(normed)

    mesh_out, grad_copies, direct = call(
        node_kernel,
        [((own, width), bf16), ((owners, own, width), bf16), ((own, width), f32)],
        (parts, own_mesh, own_cot, node_first, node_second, gains),
        flops=2 * own * width * width * 7,
        name="node",
    )
    near = lax.all_to_all(grad_copies, zy, 0, 0, tiled=True).reshape(half, width)
    far = lax.ppermute(near, "core", swap)
    (near_rows,) = call(
        lambda *refs: near_rows_kernel(own, *refs), [((edges, width), bf16)],
        (edge_count, recv, near), smem=(0,), flops=big // 2, name="near_rows",
    )
    (d_first,) = call(
        lambda *refs: edge_backward_kernel(own, *refs),
        [((edges, width), bf16)],
        (
            edge_count, recv, near_rows, far, normed, slope, edge_second,
            gains,
        ),
        smem=(0,),
        scratch=[vm((edges, width), f32)],
        flops=big // 2 + dense,
        name="edge_backward",
    )
    back_low, back_own, back_high = call(
        slot_sum_kernel, [((side, width), bf16)] * 3, (send, d_first, edge_first), flops=dense, name="slot_sum"
    )
    got_low = lax.ppermute(back_high, "lon", ring(lon_count, 1))
    got_high = lax.ppermute(back_low, "lon", ring(lon_count, -1))
    mesh_parts = to_owners(d_first)
    (edge_grad,) = call(
        edge_grad_kernel, [((edges, width), bf16)], (d_first, edge_first), flops=dense, name="edge_grad"
    )
    (grid_grad,) = call(
        grid_grad_kernel,
        [((grid_rows, width), bf16)],
        (send_rows, got_low, back_own, got_high),
        flops=2 * listed * grid_rows * width,
        name="grid_grad",
    )
    (mesh_grad,) = call(
        mesh_grad_kernel, [((own, width), bf16)], (mesh_parts, direct, edge_first), name="mesh_grad"
    )
    return (mesh_out, grid_grad, mesh_grad, edge_grad)


def solution(mesh):
    fine = Mesh(mesh.devices.reshape(mesh.shape["lon"], 8, 4, 2), ("lon", "z", "y", "core"))
    every = ("lon", "z", "y", "core")
    rows = P(every, None)
    flat = P(every)
    patch = P("lon", None)
    return jax.shard_map(
        shards,
        mesh=fine,
        in_specs=(rows, patch, rows, patch, flat, flat, rows, flat) + (P(),) * 6,
        out_specs=(rows, rows, rows, rows),
        check_vma=False,
    )
```

time: 109 us -> 101 us (0.927)
  blocking collectives: 20.2 us -> 46 us
  waiting for transfers between devices: 28.9 us -> 11.4 us
  starting transfers between devices: 27.3 us -> 17.7 us
  Pallas kernels: 23.5 us -> 19.9 us
  other arithmetic: 1.89 us -> 0 us
    all_to_all x0 -> x1, blocking collectives: none -> 26 us  [to_owners(): lax.all_to_all(both.reshape(owners, own, width), zy, 0, 0, tiled=True)]
    all_to_all x2 -> x1, waiting for transfers between devices: 26.6 us -> 10.1 us  [to_owners(): lax.all_to_all(both.reshape(owners, own, width), zy, 0, 0, tiled=True)]
    all_to_all x2 -> x1, starting transfers between devices: 13.9 us -> 4.26 us  [to_owners(): lax.all_to_all(both.reshape(owners, own, width), zy, 0, 0, tiled=True)]
    pallas_call x12 -> x16, Pallas kernels: 22.2 us -> 19.9 us  [call(): pl.pallas_call(kernel, out_shape=[jax.ShapeDtypeStruct(s, d) for s, d in...]
    convert_element_type x2 -> x0, other arithmetic: 1.89 us -> none  [to_owners(): both = (here.astype(f32) + away.astype(f32)).astype(bf16)]
    ppermute x1, waiting for transfers between devices: 1.54 us -> 0.09 us  [shards(): far = lax.ppermute(near, 'core', swap)]
    pallas_call x1 -> x0, Pallas kernels: 1.21 us -> none  [shards(): pl.pallas_call(node_kernel, grid_spec=pltpu.PrefetchScalarGridSpec(num_sc...]
    unnamed x46 -> x28, local copies, waits for them, and re-layouts: 5.1 us -> 4.08 us
  transfers between devices with their start and end apart: 9 -> 8, of which waited for: 6 -> 5; matrix products, arithmetic and copies ran while one was open for 0% -> 0% of each run, Pallas kernels for 7% -> 9%
where the time goes in v2:
time: 101 us
  blocking collectives  46 us (46%)
  Pallas kernels  19.9 us (20%)
  starting transfers between devices  17.7 us (18%)
  waiting for transfers between devices  11.4 us (11%)
  local copies, waits for them, and re-layouts  4.08 us (4%)
  between operations  1.51 us (1%)
    all_to_all x1, blocking collectives, to_owners(): lax.all_to_all(both.reshape(owners, own, width), zy, 0, 0, tiled=True)  26 us
    all_to_all x1, blocking collectives, shards(): lax.all_to_all(grad_copies, zy, 0, 0, tiled=True).reshape(half, width)  20 us
    pallas_call x16, Pallas kernels, call(): pl.pallas_call(kernel, out_shape=[jax.ShapeDtypeStruct(s, d) for s, d in...  19.9 us
    all_to_all x1, waiting for transfers between devices, to_owners(): lax.all_to_all(both.reshape(owners, own, width), zy, 0, 0, tiled=True)  10.1 us
    all_to_all x1, starting transfers between devices, to_owners(): lax.all_to_all(both.reshape(owners, own, width), zy, 0, 0, tiled=True)  4.26 us
    unnamed x28, local copies, waits for them, and re-layouts  4.08 us
    ppermute x2, starting transfers between devices, to_owners(): away = lax.ppermute(out, 'core', swap)  3.62 us
    ppermute x1, starting transfers between devices, shards(): far = lax.ppermute(near, 'core', swap)  3.57 us
  transfers between devices with their start and end apart: 8, of which 5 were waited for; matrix products, arithmetic and copies ran while one was open for 0% of the time, Pallas kernels for 9%

profile of v2, /device:TPU:1, one launch (start us, length us, event | category | flops | bytes accessed | tf_op | source)
XLA Modules:
  0.0 100.6 jit_solution(15012318442060194533)
XLA Ops:
  0.6 1.0 copy-done.1
  2.6 2.1 %collective-permute-start = (bf16[64,256]{1,0:T(8,128)(2,1)S(1)}, bf16[64,256]{1,0:T(8,128)(2,1)S(1)}, u32[]{:S(2)}, u32[]{:S(2)}) collective-permute-start(bf16[64,256]{1,0:T(8,128)(2,1)S(1)} %get-tuple-element.20), channel_id=1, source_target_pairs={{0,64},{64,128},{128,192},{192,0},{1,65},{65,129},{129,193},{193,1... | collective-permute-start | bytes 98312 | tf_op jit(solution)/shard_map/ppermute | solution.py:319
  4.7 1.4 %collective-permute-start.1 = (bf16[64,256]{1,0:T(8,128)(2,1)S(1)}, bf16[64,256]{1,0:T(8,128)(2,1)S(1)}, u32[]{:S(2)}, u32[]{:S(2)}) collective-permute-start(bf16[64,256]{1,0:T(8,128)(2,1)S(1)} %get-tuple-element.22), channel_id=1, source_target_pairs={{0,192},{64,0},{128,64},{192,128},{1,193},{65,1},{129,65},{193,129... | collective-permute-start | bytes 98312 | tf_op jit(solution)/shard_map/ppermute | solution.py:320
  6.1 1.2 %copy-done.8 = bf16[2048,256]{1,0:T(8,128)(2,1)S(1)} copy-done((bf16[2048,256]{1,0:T(8,128)(2,1)S(1)}, bf16[2048,256]{1,0:T(8,128)(2,1)}, u32[]{:S(2)}) %copy-start.8) | copy-done | bytes 1048600
  7.3 2.5 %mesh_rows.1 = (bf16[2048,256]{1,0:T(8,128)(2,1)S(1)}, bf16[32,256]{1,0:T(8,128)(2,1)S(1)}) custom-call(s32[16,128]{1,0:T(8,128)S(1)} %bitcast.10, bf16[2048,256]{1,0:T(8,128)(2,1)S(1)} %copy-done.8), custom_call_target="tpu_custom_call" | custom-call | flops 2147483648 | tf_op jit(solution)/shard_map/mesh_rows/pallas_call | solution.py:47
  11.2 2.2 %edge_forward.1 = (bf16[2048,256]{1,0:T(8,128)(2,1)S(1)}, bf16[2048,256]{1,0:T(8,128)(2,1)S(1)}, bf16[32,256]{1,0:T(8,128)(2,1)S(1)}, f32[2,256]{1,0:T(2,128)S(1)}) custom-call(s32[16,128]{1,0:T(8,128)S(1)} %bitcast.19, bf16[2048,256]{1,0:T(8,128)(2,1)S(1)} %copy-done.9, bf16[2048,256]{1,0:T(8,128)(2,1)S(1)} %get-tuple-element.19.mesh_rows_ref, ...), custom_call_target="tpu_custom_call" | custom-call | flops 1342177280 | tf_op jit(solution)/shard_map/edge_forward/pallas_call | solution.py:47
  13.4 1.2 %half_away.2 = bf16[1024,256]{1,0:T(8,128)(2,1)S(1)} custom-call(s32[1]{0:T(128)S(6)} %copy.18.refs_0_, s32[16,128]{1,0:T(8,128)S(1)} %bitcast.11, bf16[2048,256]{1,0:T(8,128)(2,1)S(1)} %get-tuple-element.23.refs_2_.refs_4_), custom_call_target="tpu_custom_call" | custom-call | flops 1073741824 | tf_op jit(solution)/shard_map/half_away/pallas_call | solution.py:47
  14.7 3.2 %collective-permute-start.2 = (bf16[1024,256]{1,0:T(8,128)(2,1)S(1)}, bf16[1024,256]{1,0:T(8,128)(2,1)S(1)}, u32[]{:S(2)}, u32[]{:S(2)}) collective-permute-start(bf16[1024,256]{1,0:T(8,128)(2,1)S(1)} %half_away.2), channel_id=1, source_target_pairs={{0,1},{1,0},{2,3},{3,2},{4,5},{5,4},{6,7},{7,6},{8,9},{9,8},{10,11... | collective-permute-start | bytes 1572872 | tf_op jit(solution)/shard_map/ppermute | solution.py:345
  17.8 1.0 half_here.2.refs_3_
  19.8 26.0 %all_to_all.15.parts_ref = bf16[32,32,256]{2,1,0:T(8,128)(2,1)S(1)} all-to-all(bf16[32,32,256]{2,1,0:T(8,128)(2,1)S(1)} %bitcast.7), channel_id=1, replica_groups=mesh['lon'=4,'z'=8,'y'=4,'core'=2] {'z','y'}, dimensions={0} | all-to-all | bytes 1048576 | tf_op jit(solution)/shard_map/all_to_all | solution.py:355
  45.8 1.2 %node.1 = (bf16[32,256]{1,0:T(8,128)(2,1)}, bf16[32,32,256]{2,1,0:T(8,128)(2,1)S(1)}, f32[32,256]{1,0:T(8,128)S(1)}) custom-call(bf16[32,32,256]{2,1,0:T(8,128)(2,1)S(1)} %all_to_all.15.parts_ref, bf16[32,256]{1,0:T(8,128)(2,1)S(1)} %get-tuple-element.24.mesh_ref, bf16[32,256]{1,0:T(8,128)(2,1)S(1)} %get-tuple-element.25.cot_ref, ...), custom_call_target="tpu_custom_call" | custom-call | flops 29360128 | tf_op jit(solution)/shard_map/node/pallas_call | solution.py:47
  47.0 20.0 %all_to_all.16 = bf16[32,32,256]{2,1,0:T(8,128)(2,1)S(1)} all-to-all(bf16[32,32,256]{2,1,0:T(8,128)(2,1)S(1)} %get-tuple-element.28), channel_id=1, replica_groups=mesh['lon'=4,'z'=8,'y'=4,'core'=2] {'z','y'}, dimensions={0} | all-to-all | bytes 1048576 | tf_op jit(solution)/shard_map/all_to_all | solution.py:366
  67.1 3.6 %collective-permute-start.3 = (bf16[1024,256]{1,0:T(8,128)(2,1)S(1)}, bf16[1024,256]{1,0:T(8,128)(2,1)S(1)}, u32[]{:S(2)}, u32[]{:S(2)}) collective-permute-start(bf16[1024,256]{1,0:T(8,128)(2,1)S(1)} %bitcast.8), channel_id=1, source_target_pairs={{0,1},{1,0},{2,3},{3,2},{4,5},{5,4},{6,7},{7,6},{8,9},{9,8},{10,11... | collective-permute-start | bytes 1572872 | tf_op jit(solution)/shard_map/ppermute | solution.py:367
  70.7 1.4 %near_rows.1.refs_2_ = bf16[2048,256]{1,0:T(8,128)(2,1)S(1)} custom-call(s32[1]{0:T(128)S(6)} %copy.18.refs_0_, s32[16,128]{1,0:T(8,128)S(1)} %bitcast.14, bf16[1024,256]{1,0:T(8,128)(2,1)S(1)} %bitcast.9), custom_call_target="tpu_custom_call" | custom-call | flops 1073741824 | tf_op jit(solution)/shard_map/near_rows/pallas_call | solution.py:47
  72.2 2.2 %edge_backward.1.d_first_ref.refs_2_ = bf16[2048,256]{1,0:T(8,128)(2,1)S(1)} custom-call(s32[1]{0:T(128)S(6)} %copy.18.refs_0_, s32[16,128]{1,0:T(8,128)S(1)} %bitcast.15, bf16[2048,256]{1,0:T(8,128)(2,1)S(1)} %near_rows.1.refs_2_, bf16[1024,256]{1,0:T(8,128)(2,1)S(1)} %collective-permute-done.3.refs_3_, ...), custom_call_target="tpu_custom_call" | custom-call | flops 1342177280 | tf_op jit(solution)/shard_map/edge_backward/pallas_call | solution.py:47
  74.4 1.2 %half_away.3 = bf16[1024,256]{1,0:T(8,128)(2,1)S(1)} custom-call(s32[1]{0:T(128)S(6)} %copy.18.refs_0_, s32[16,128]{1,0:T(8,128)S(1)} %bitcast.16, bf16[2048,256]{1,0:T(8,128)(2,1)S(1)} %edge_backward.1.d_first_ref.refs_2_), custom_call_target="tpu_custom_call" | custom-call | flops 1073741824 | tf_op jit(solution)/shard_map/half_away/pallas_call | solution.py:47
  76.1 1.0 half_here.3.refs_3_
  77.6 1.3 %half_total.3 = bf16[1024,256]{1,0:T(8,128)(2,1)} custom-call(s32[1]{0:T(128)S(6)} %copy.18.refs_0_, s32[16,128]{1,0:T(8,128)S(1)} %bitcast.18, bf16[2048,256]{1,0:T(8,128)(2,1)S(1)} %edge_backward.1.d_first_ref.refs_2_, f32[768,256]{1,0:T(8,128)S(1)} %half_here.3.refs_3_, bf16[1024,256]{1,0:T(8,128)(2,1)S(1)} %collective-permute-done.6.refs_4_), custom_call_target="tpu_custom_call" | custom-call | flops 268435456 | tf_op jit(solution)/shard_map/half_total/pallas_call | solution.py:47
  78.9 4.3 %all-to-all-start.2 = ((bf16[32,32,256]{2,1,0:T(8,128)(2,1)}), bf16[32,32,256]{2,1,0:T(8,128)(2,1)S(1)}, u32[]{:S(2)}, u32[]{:S(2)}) async-start(bf16[32,32,256]{2,1,0:T(8,128)(2,1)} %bitcast.6), calls=%async_computation.2 | async-start | bytes 1048576 | tf_op jit(solution)/shard_map/all_to_all | solution.py:355
  83.9 2.7 %collective-permute-start.5 = (bf16[64,256]{1,0:T(8,128)(2,1)S(1)}, bf16[64,256]{1,0:T(8,128)(2,1)S(1)}, u32[]{:S(2)}, u32[]{:S(2)}) collective-permute-start(bf16[64,256]{1,0:T(8,128)(2,1)S(1)} %get-tuple-element.32), channel_id=1, source_target_pairs={{0,192},{64,0},{128,64},{192,128},{1,193},{65,1},{129,65},{193,129... | collective-permute-start | bytes 98312 | tf_op jit(solution)/shard_map/ppermute | solution.py:388
  86.6 1.4 %edge_grad.1 = bf16[2048,256]{1,0:T(8,128)(2,1)} custom-call(bf16[2048,256]{1,0:T(8,128)(2,1)S(1)} %edge_backward.1.d_first_ref.refs_2_, bf16[768,256]{1,0:T(8,128)(2,1)S(1)} %copy-done), custom_call_target="tpu_custom_call" | custom-call | flops 268435456 | tf_op jit(solution)/shard_map/edge_grad/pallas_call | solution.py:47
  88.7 1.0 grid_grad.1
  89.7 10.1 %all-to-all-done.2.parts_ref = bf16[32,32,256]{2,1,0:T(8,128)(2,1)S(1)} async-done(((bf16[32,32,256]{2,1,0:T(8,128)(2,1)}), bf16[32,32,256]{2,1,0:T(8,128)(2,1)S(1)}, u32[]{:S(2)}, u32[]{:S(2)}) %all-to-all-start.2) | async-done | bytes 524320 | tf_op jit(solution)/shard_map/all_to_all | solution.py:355
  99.8 0.8 mesh_grad.1
  (38 shorter events, 5.1 us)
Async XLA Ops:
  0.6 1.0 copy-start.1
  1.6 0.7 copy-start.6
  2.3 3.8 %copy-start.4 = (s32[2048]{0:T(1024)S(1)}, s32[2048]{0:T(1024)}, u32[]{:S(2)}) copy-start(s32[2048]{0:T(1024)} %param.19) | copy-start | bytes 24580
  2.6 7.9 %collective-permute-start = (bf16[64,256]{1,0:T(8,128)(2,1)S(1)}, bf16[64,256]{1,0:T(8,128)(2,1)S(1)}, u32[]{:S(2)}, u32[]{:S(2)}) collective-permute-start(bf16[64,256]{1,0:T(8,128)(2,1)S(1)} %get-tuple-element.20), channel_id=1, source_target_pairs={{0,64},{64,128},{128,192},{192,0},{1,65},{65,129},{129,193},{193,1... | collective-permute-start | bytes 98312 | tf_op jit(solution)/shard_map/ppermute | solution.py:319
  4.7 5.8 %collective-permute-start.1 = (bf16[64,256]{1,0:T(8,128)(2,1)S(1)}, bf16[64,256]{1,0:T(8,128)(2,1)S(1)}, u32[]{:S(2)}, u32[]{:S(2)}) collective-permute-start(bf16[64,256]{1,0:T(8,128)(2,1)S(1)} %get-tuple-element.22), channel_id=1, source_target_pairs={{0,192},{64,0},{128,64},{192,128},{1,193},{65,1},{129,65},{193,129... | collective-permute-start | bytes 98312 | tf_op jit(solution)/shard_map/ppermute | solution.py:320
  6.1 1.2 %copy-start.8 = (bf16[2048,256]{1,0:T(8,128)(2,1)S(1)}, bf16[2048,256]{1,0:T(8,128)(2,1)}, u32[]{:S(2)}) copy-start(bf16[2048,256]{1,0:T(8,128)(2,1)} %mesh_ref.1) | copy-start | bytes 3145732
  7.3 3.2 %copy-start = (bf16[768,256]{1,0:T(8,128)(2,1)S(1)}, bf16[768,256]{1,0:T(8,128)(2,1)}, u32[]{:S(2)}) copy-start(bf16[768,256]{1,0:T(8,128)(2,1)} %first_ref.9) | copy-start | bytes 1179652
  7.3 3.2 %copy-start.9 = (bf16[2048,256]{1,0:T(8,128)(2,1)S(1)}, bf16[2048,256]{1,0:T(8,128)(2,1)}, u32[]{:S(2)}) copy-start(bf16[2048,256]{1,0:T(8,128)(2,1)} %edge_ref.1) | copy-start | bytes 3145732
  7.3 3.2 %copy-start.10 = (bf16[2048,256]{1,0:T(8,128)(2,1)S(1)}, bf16[2048,256]{1,0:T(8,128)(2,1)}, u32[]{:S(2)}) copy-start(bf16[2048,256]{1,0:T(8,128)(2,1)} %cot_ref.1) | copy-start | bytes 3145732
  7.3 3.2 %copy-start.11 = (bf16[256,256]{1,0:T(8,128)(2,1)S(1)}, bf16[256,256]{1,0:T(8,128)(2,1)}, u32[]{:S(2)}) copy-start(bf16[256,256]{1,0:T(8,128)(2,1)} %refs_6_.1) | copy-start | bytes 393220
  7.3 3.2 %copy-start.13 = (f32[256]{0:T(256)S(1)}, f32[256]{0:T(256)}, u32[]{:S(2)}) copy-start(f32[256]{0:T(256)} %param.24) | copy-start | bytes 3076
  9.8 0.8 copy-start.5
  10.5 0.7 copy-start.12
  14.7 4.7 %collective-permute-start.2 = (bf16[1024,256]{1,0:T(8,128)(2,1)S(1)}, bf16[1024,256]{1,0:T(8,128)(2,1)S(1)}, u32[]{:S(2)}, u32[]{:S(2)}) collective-permute-start(bf16[1024,256]{1,0:T(8,128)(2,1)S(1)} %half_away.2), channel_id=1, source_target_pairs={{0,1},{1,0},{2,3},{3,2},{4,5},{5,4},{6,7},{7,6},{8,9},{9,8},{10,11... | collective-permute-start | bytes 1572872 | tf_op jit(solution)/shard_map/ppermute | solution.py:345
  19.8 26.0 %copy-start.2 = (bf16[512,256]{1,0:T(8,128)(2,1)S(1)}, bf16[512,256]{1,0:T(8,128)(2,1)}, u32[]{:S(2)}) copy-start(bf16[512,256]{1,0:T(8,128)(2,1)} %first_ref.6) | copy-start | bytes 786436
  19.8 26.0 %copy-start.3 = (bf16[256,256]{1,0:T(8,128)(2,1)S(1)}, bf16[256,256]{1,0:T(8,128)(2,1)}, u32[]{:S(2)}) copy-start(bf16[256,256]{1,0:T(8,128)(2,1)} %second_ref.3) | copy-start | bytes 393220
  67.1 5.1 %collective-permute-start.3 = (bf16[1024,256]{1,0:T(8,128)(2,1)S(1)}, bf16[1024,256]{1,0:T(8,128)(2,1)S(1)}, u32[]{:S(2)}, u32[]{:S(2)}) collective-permute-start(bf16[1024,256]{1,0:T(8,128)(2,1)S(1)} %bitcast.8), channel_id=1, source_target_pairs={{0,1},{1,0},{2,3},{3,2},{4,5},{5,4},{6,7},{7,6},{8,9},{9,8},{10,11... | collective-permute-start | bytes 1572872 | tf_op jit(solution)/shard_map/ppermute | solution.py:367
  75.6 2.0 %collective-permute-start.6 = (bf16[1024,256]{1,0:T(8,128)(2,1)S(1)}, bf16[1024,256]{1,0:T(8,128)(2,1)S(1)}, u32[]{:S(2)}, u32[]{:S(2)}) collective-permute-start(bf16[1024,256]{1,0:T(8,128)(2,1)S(1)} %half_away.3), channel_id=1, source_target_pairs={{0,1},{1,0},{2,3},{3,2},{4,5},{5,4},{6,7},{7,6},{8,9},{9,8},{10,11... | collective-permute-start | bytes 1572872 | tf_op jit(solution)/shard_map/ppermute | solution.py:345
  78.9 20.8 %all-to-all-start.2 = ((bf16[32,32,256]{2,1,0:T(8,128)(2,1)}), bf16[32,32,256]{2,1,0:T(8,128)(2,1)S(1)}, u32[]{:S(2)}, u32[]{:S(2)}) async-start(bf16[32,32,256]{2,1,0:T(8,128)(2,1)} %bitcast.6), calls=%async_computation.2 | async-start | bytes 1048576 | tf_op jit(solution)/shard_map/all_to_all | solution.py:355
  83.8 4.3 %collective-permute-start.4 = (bf16[64,256]{1,0:T(8,128)(2,1)S(1)}, bf16[64,256]{1,0:T(8,128)(2,1)S(1)}, u32[]{:S(2)}, u32[]{:S(2)}) collective-permute-start(bf16[64,256]{1,0:T(8,128)(2,1)S(1)} %get-tuple-element.30), channel_id=1, source_target_pairs={{0,64},{64,128},{128,192},{192,0},{1,65},{65,129},{129,193},{193,1... | collective-permute-start | bytes 98312 | tf_op jit(solution)/shard_map/ppermute | solution.py:387
  83.9 4.3 %collective-permute-start.5 = (bf16[64,256]{1,0:T(8,128)(2,1)S(1)}, bf16[64,256]{1,0:T(8,128)(2,1)S(1)}, u32[]{:S(2)}, u32[]{:S(2)}) collective-permute-start(bf16[64,256]{1,0:T(8,128)(2,1)S(1)} %get-tuple-element.32), channel_id=1, source_target_pairs={{0,192},{64,0},{128,64},{192,128},{1,193},{65,1},{129,65},{193,129... | collective-permute-start | bytes 98312 | tf_op jit(solution)/shard_map/ppermute | solution.py:388
  88.0 0.7 copy-start.7

commit v3 on v2

--- a/solution.py
+++ b/solution.py
@@ -89,11 +89,13 @@
     high_ref[...] = rows[2 * side :]
 
 
-def mesh_rows_kernel(recv_ref, mesh_ref, out_ref, own_ref):
+def mesh_rows_kernel(count_ref, recv_ref, mesh_ref, out_ref, own_ref, live_ref):
     own = own_ref.shape[0]
     own_ref[...] = mesh_ref[pl.ds(pl.multiple_of(my_block() * own, own), own), :]
     m = mesh_ref.shape[0]
-    cols = jnp.transpose(recv_ref[...])
+    live = live_rows(recv_ref, count_ref[...])
+    live_ref[...] = live
+    cols = jnp.transpose(live)
     for start, at in chunks(out_ref.shape[0], LANES):
         hot = one_hot(lax.broadcasted_iota(i32, (LANES, m), 1) == column(cols, start, LANES))
         out_ref[at, :] = dot(hot, mesh_ref[...]).astype(bf16)
@@ -101,13 +103,8 @@
 
 def edge_forward_kernel(
     send_ref, edge_ref, mesh_rows_ref, low_ref, own_ref, high_ref, first_ref, second_ref,
-    cot_ref, node_gain_ref, edge_gain_ref, normed_ref, slope_ref, own_cot_ref, gains_ref,
-    work_ref, post_ref,
+    normed_ref, slope_ref, work_ref, post_ref,
 ):
-    own = own_cot_ref.shape[0]
-    own_cot_ref[...] = cot_ref[pl.ds(pl.multiple_of(my_block() * own, own), own), :]
-    gains_ref[0:1, :] = node_gain_ref[...]
-    gains_ref[1:2, :] = edge_gain_ref[...]
     listed = jnp.concatenate([low_ref[...], own_ref[...], high_ref[...]], axis=0)
     n = listed.shape[0]
     cols = jnp.transpose(send_ref[...])
@@ -149,22 +146,31 @@
     return total
 
 
-def half_sum_kernel(own, here, count_ref, recv_ref, value_ref, out_ref):
-    live = live_rows(recv_ref, count_ref[0])
+def half_sum_kernel(own, here, live_ref, value_ref, out_ref):
+    live = live_ref[...]
     core = my_core() if here else 1 - my_core()
     for start, at in chunks(out_ref.shape[0], CHUNK):
         out_ref[at, :] = half_rows(own, core, live, value_ref, start).astype(out_ref.dtype)
 
 
-def half_total_kernel(own, count_ref, recv_ref, value_ref, begun_ref, away_ref, out_ref):
+def half_total_kernel(own, live_ref, value_ref, begun_ref, away_ref, out_ref):
     done = begun_ref.shape[0]
-    live = live_rows(recv_ref, count_ref[0])
+    live = live_ref[...]
     for start, at in chunks(out_ref.shape[0], CHUNK):
         if start < done:
             here = begun_ref[at, :]
         else:
             here = half_rows(own, my_core(), live, value_ref, start)
         out_ref[at, :] = (here + away_ref[at, :].astype(f32)).astype(bf16)
+
+
+def half_first_kernel(
+    own, live_ref, value_ref, cot_ref, node_gain_ref, edge_gain_ref, out_ref, own_cot_ref, gains_ref
+):
+    half_sum_kernel(own, True, live_ref, value_ref, out_ref)
+    own_cot_ref[...] = cot_ref[pl.ds(pl.multiple_of(my_block() * own, own), own), :]
+    gains_ref[0:1, :] = node_gain_ref[...]
+    gains_ref[1:2, :] = edge_gain_ref[...]
 
 
 def norm(value):
@@ -206,9 +212,9 @@
     return jnp.where((live // own) % 2 == core, place, -1)
 
 
-def near_rows_kernel(own, count_ref, recv_ref, near_ref, out_ref):
+def near_rows_kernel(own, live_ref, near_ref, out_ref):
     half = near_ref.shape[0]
-    place = half_place(own, my_core(), live_rows(recv_ref, count_ref[0]))
+    place = half_place(own, my_core(), live_ref[...])
     cols = jnp.transpose(place)
     for start, at in chunks(out_ref.shape[0], LANES):
         hot = one_hot(lax.broadcasted_iota(i32, (LANES, half), 1) == column(cols, start, LANES))
@@ -216,11 +222,11 @@
 
 
 def edge_backward_kernel(
-    own, count_ref, recv_ref, near_rows_ref, far_ref, normed_ref, slope_ref, second_ref,
+    own, live_ref, near_rows_ref, far_ref, normed_ref, slope_ref, second_ref,
     gains_ref, out_ref, work_ref,
 ):
     half = far_ref.shape[0]
-    place = half_place(own, 1 - my_core(), live_rows(recv_ref, count_ref[0]))
+    place = half_place(own, 1 - my_core(), live_ref[...])
     cols = jnp.transpose(place)
     for start, at in chunks(out_ref.shape[0], LANES):
         hot = one_hot(lax.broadcasted_iota(i32, (LANES, half), 1) == column(cols, start, LANES))
@@ -313,49 +319,54 @@
         halo_rows_kernel,
         [((side, width), bf16)] * 3,
         (send_rows, grid_latent),
-        flops=2 * listed * grid_rows * width,
+        flops=2 * big,
         name="halo_rows",
     )
     from_low = lax.ppermute(to_high, "lon", ring(lon_count, 1))
     from_high = lax.ppermute(to_low, "lon", ring(lon_count, -1))
-    mesh_rows, own_mesh = call(
-        mesh_rows_kernel, [((edges, width), bf16), ((own, width), bf16)], (recv, mesh_latent),
+    mesh_rows, own_mesh, live = call(
+        mesh_rows_kernel,
+        [((edges, width), bf16), ((own, width), bf16), (recv.shape, i32)],
+        (edge_count.reshape(1, 1), recv, mesh_latent),
         flops=big,
         name="mesh_rows",
     )
-    normed, slope, own_cot, gains = call(
+    normed, slope = call(
         edge_forward_kernel,
-        [((edges, width), bf16)] * 2 + [((own, width), bf16), ((2, width), f32)],
-        (
-            send, edge_latent, mesh_rows, from_low, stay, from_high, edge_first, edge_second,
-            mesh_cotangent, node_gain.reshape(1, width), edge_gain.reshape(1, width),
-        ),
+        [((edges, width), bf16)] * 2,
+        (send, edge_latent, mesh_rows, from_low, stay, from_high, edge_first, edge_second),
         scratch=[vm((edges, width), f32)] * 2,
         flops=5 * dense,
         name="edge_forward",
     )
 
-    def to_owners(value):
+    def to_owners(value, extras=(), extra_outs=()):
         shape = (half, width)
         begun = half - CHUNK
         (out,) = call(
             lambda *refs: half_sum_kernel(own, False, *refs), [(shape, bf16)],
-            (edge_count, recv, value), smem=(0,), flops=big // 2, name="half_away",
+            (live, value), flops=big // 2, name="half_away",
         )
         away = lax.ppermute(out, "core", swap)
-        (here,) = call(
-            lambda *refs: half_sum_kernel(own, True, *refs), [((begun, width), f32)],
-            (edge_count, recv, value), smem=(0,), flops=big // 2, name="half_here",
+        here = call(
+            (lambda *refs: half_first_kernel(own, *refs))
+            if extras
+            else (lambda *refs: half_sum_kernel(own, True, *refs)),
+            [((begun, width), f32)] + list(extra_outs),
+            (live, value) + tuple(extras), flops=big // 2, name="half_here",
         )
         (both,) = call(
             lambda *refs: half_total_kernel(own, *refs), [(shape, bf16)],
-            (edge_count, recv, value, here, away), smem=(0,), flops=big // 8,
-            name="half_total",
+            (live, value, here[0], away), flops=big // 8, name="half_total",
         )
-        return lax.all_to_all(both.reshape(owners, own, width), zy, 0, 0, tiled=True)
-
-    parts = to_owners(normed)
-
+        parts = lax.all_to_all(both.reshape(owners, own, width), zy, 0, 0, tiled=True)
+        return (parts,) + tuple(here[1:])
+
+    parts, own_cot, gains = to_owners(
+        normed,
+        (mesh_cotangent, node_gain.reshape(1, width), edge_gain.reshape(1, width)),
+        (((own, width), bf16), ((2, width), f32)),
+    )
     mesh_out, grad_copies, direct = call(
         node_kernel,
         [((own, width), bf16), ((owners, own, width), bf16), ((own, width), f32)],
@@ -367,16 +378,15 @@
     far = lax.ppermute(near, "core", swap)
     (near_rows,) = call(
         lambda *refs: near_rows_kernel(own, *refs), [((edges, width), bf16)],
-        (edge_count, recv, near), smem=(0,), flops=big // 2, name="near_rows",
+        (live, near), flops=big // 2, name="near_rows",
     )
     (d_first,) = call(
         lambda *refs: edge_backward_kernel(own, *refs),
         [((edges, width), bf16)],
         (
-            edge_count, recv, near_rows, far, normed, slope, edge_second,
+            live, near_rows, far, normed, slope, edge_second,
             gains,
         ),
-        smem=(0,),
         scratch=[vm((edges, width), f32)],
         flops=big // 2 + dense,
         name="edge_backward",
@@ -386,7 +396,7 @@
     )
     got_low = lax.ppermute(back_high, "lon", ring(lon_count, 1))
     got_high = lax.ppermute(back_low, "lon", ring(lon_count, -1))
-    mesh_parts = to_owners(d_first)
+    (mesh_parts,) = to_owners(d_first)
     (edge_grad,) = call(
         edge_grad_kernel, [((edges, width), bf16)], (d_first, edge_first), flops=dense, name="edge_grad"
     )

time: 101 us -> 99.3 us (0.983)
  local copies, waits for them, and re-layouts: 4.08 us -> 2.93 us
    unnamed x28, local copies, waits for them, and re-layouts: 4.08 us -> 2.93 us
  transfers between devices with their start and end apart: 8 -> 8, of which waited for: 5 -> 4; matrix products, arithmetic and copies ran while one was open for 0% -> 0% of each run, Pallas kernels for 9% -> 9%
where the time goes in v3:
time: 99.3 us; the launch traced here: 99 us
  blocking collectives  46.1 us (46%)
  Pallas kernels  19.9 us (20%)
  starting transfers between devices  17.7 us (18%)
  waiting for transfers between devices  10.9 us (11%)
  local copies, waits for them, and re-layouts  2.93 us (3%)
  between operations  1.54 us (2%)
    all_to_all x1, blocking collectives, to_owners(): lax.all_to_all(both.reshape(owners, own, width), zy, 0, 0, tiled=True)  26 us
    all_to_all x1, blocking collectives, shards(): lax.all_to_all(grad_copies, zy, 0, 0, tiled=True).reshape(half, width)  20 us
    pallas_call x16, Pallas kernels, call(): pl.pallas_call(kernel, out_shape=[jax.ShapeDtypeStruct(s, d) for s, d in...  19.9 us
    all_to_all x1, waiting for transfers between devices, to_owners(): lax.all_to_all(both.reshape(owners, own, width), zy, 0, 0, tiled=True)  10.1 us
    all_to_all x1, starting transfers between devices, to_owners(): lax.all_to_all(both.reshape(owners, own, width), zy, 0, 0, tiled=True)  4.26 us
    ppermute x2, starting transfers between devices, to_owners(): away = lax.ppermute(out, 'core', swap)  3.63 us
    ppermute x1, starting transfers between devices, shards(): far = lax.ppermute(near, 'core', swap)  3.55 us
    unnamed x28, local copies, waits for them, and re-layouts  2.93 us
  transfers between devices with their start and end apart: 8, of which 4 were waited for; matrix products, arithmetic and copies ran while one was open for 0% of the time, Pallas kernels for 9%

profile of v3, /device:TPU:1, one launch (start us, length us, event | category | flops | bytes accessed | tf_op | source)
XLA Modules:
  0.0 99.0 jit_solution(17094872320955541871)
XLA Ops:
  1.3 1.0 %copy-done.9 = bf16[768,256]{1,0:T(8,128)(2,1)S(1)} copy-done((bf16[768,256]{1,0:T(8,128)(2,1)S(1)}, bf16[768,256]{1,0:T(8,128)(2,1)}, u32[]{:S(2)}) %copy-start.9) | copy-done | bytes 393240
  2.6 2.1 %collective-permute-start = (bf16[64,256]{1,0:T(8,128)(2,1)S(1)}, bf16[64,256]{1,0:T(8,128)(2,1)S(1)}, u32[]{:S(2)}, u32[]{:S(2)}) collective-permute-start(bf16[64,256]{1,0:T(8,128)(2,1)S(1)} %get-tuple-element.23), channel_id=1, source_target_pairs={{0,64},{64,128},{128,192},{192,0},{1,65},{65,129},{129,193},{193,1... | collective-permute-start | bytes 98312 | tf_op jit(solution)/shard_map/ppermute | solution.py:325
  4.7 1.4 %collective-permute-start.1 = (bf16[64,256]{1,0:T(8,128)(2,1)S(1)}, bf16[64,256]{1,0:T(8,128)(2,1)S(1)}, u32[]{:S(2)}, u32[]{:S(2)}) collective-permute-start(bf16[64,256]{1,0:T(8,128)(2,1)S(1)} %get-tuple-element.25), channel_id=1, source_target_pairs={{0,192},{64,0},{128,64},{192,128},{1,193},{65,1},{129,65},{193,129... | collective-permute-start | bytes 98312 | tf_op jit(solution)/shard_map/ppermute | solution.py:326
  6.8 2.6 %mesh_rows.1 = (bf16[2048,256]{1,0:T(8,128)(2,1)S(1)}, bf16[32,256]{1,0:T(8,128)(2,1)S(1)}, s32[16,128]{1,0:T(8,128)S(1)}) custom-call(s32[1,1]{1,0:T(1,128)} %bitcast.8.count_ref, s32[16,128]{1,0:T(8,128)S(1)} %bitcast.14, bf16[2048,256]{1,0:T(8,128)(2,1)S(1)} %copy-done.6), custom_call_target="tpu_custom_call" | custom-call | flops 2147483648 | tf_op jit(solution)/shard_map/mesh_rows/pallas_call | solution.py:47
  9.5 2.2 %edge_forward.1 = (bf16[2048,256]{1,0:T(8,128)(2,1)S(1)}, bf16[2048,256]{1,0:T(8,128)(2,1)S(1)}) custom-call(s32[16,128]{1,0:T(8,128)S(1)} %bitcast.12, bf16[2048,256]{1,0:T(8,128)(2,1)S(1)} %copy-done.7, bf16[2048,256]{1,0:T(8,128)(2,1)S(1)} %get-tuple-element.22.mesh_rows_ref, bf16[64,256]{1,0:T(8,128)(2,1)S(1)} %collective-permute-done.low_ref, ...), custom_call_target="tpu_custom_call" | custom-call | flops 1342177280 | tf_op jit(solution)/shard_map/edge_forward/pallas_call | solution.py:47
  11.7 1.2 %half_away.2 = bf16[1024,256]{1,0:T(8,128)(2,1)S(1)} custom-call(s32[16,128]{1,0:T(8,128)S(1)} %get-tuple-element.21.refs_0_, bf16[2048,256]{1,0:T(8,128)(2,1)S(1)} %get-tuple-element.26.refs_1_.refs_3_), custom_call_target="tpu_custom_call" | custom-call | flops 1073741824 | tf_op jit(solution)/shard_map/half_away/pallas_call | solution.py:47
  12.9 3.2 %collective-permute-start.2 = (bf16[1024,256]{1,0:T(8,128)(2,1)S(1)}, bf16[1024,256]{1,0:T(8,128)(2,1)S(1)}, u32[]{:S(2)}, u32[]{:S(2)}) collective-permute-start(bf16[1024,256]{1,0:T(8,128)(2,1)S(1)} %half_away.2), channel_id=1, source_target_pairs={{0,1},{1,0},{2,3},{3,2},{4,5},{5,4},{6,7},{7,6},{8,9},{9,8},{10,11... | collective-permute-start | bytes 1572872 | tf_op jit(solution)/shard_map/ppermute | solution.py:350
  16.1 0.7 copy-done.12
  16.8 1.0 half_here.2
  18.2 26.0 %all_to_all.15.parts_ref = bf16[32,32,256]{2,1,0:T(8,128)(2,1)S(1)} all-to-all(bf16[32,32,256]{2,1,0:T(8,128)(2,1)S(1)} %bitcast.9), channel_id=1, replica_groups=mesh['lon'=4,'z'=8,'y'=4,'core'=2] {'z','y'}, dimensions={0} | all-to-all | bytes 1048576 | tf_op jit(solution)/shard_map/all_to_all | solution.py:362
  44.3 1.2 %node.1 = (bf16[32,256]{1,0:T(8,128)(2,1)}, bf16[32,32,256]{2,1,0:T(8,128)(2,1)S(1)}, f32[32,256]{1,0:T(8,128)S(1)}) custom-call(bf16[32,32,256]{2,1,0:T(8,128)(2,1)S(1)} %all_to_all.15.parts_ref, bf16[32,256]{1,0:T(8,128)(2,1)S(1)} %get-tuple-element.28.mesh_ref, bf16[32,256]{1,0:T(8,128)(2,1)S(1)} %get-tuple-element.29.cot_ref, ...), custom_call_target="tpu_custom_call" | custom-call | flops 29360128 | tf_op jit(solution)/shard_map/node/pallas_call | solution.py:47
  45.5 20.0 %all_to_all.16 = bf16[32,32,256]{2,1,0:T(8,128)(2,1)S(1)} all-to-all(bf16[32,32,256]{2,1,0:T(8,128)(2,1)S(1)} %get-tuple-element.32), channel_id=1, replica_groups=mesh['lon'=4,'z'=8,'y'=4,'core'=2] {'z','y'}, dimensions={0} | all-to-all | bytes 1048576 | tf_op jit(solution)/shard_map/all_to_all | solution.py:377
  65.5 3.5 %collective-permute-start.3 = (bf16[1024,256]{1,0:T(8,128)(2,1)S(1)}, bf16[1024,256]{1,0:T(8,128)(2,1)S(1)}, u32[]{:S(2)}, u32[]{:S(2)}) collective-permute-start(bf16[1024,256]{1,0:T(8,128)(2,1)S(1)} %bitcast.10), channel_id=1, source_target_pairs={{0,1},{1,0},{2,3},{3,2},{4,5},{5,4},{6,7},{7,6},{8,9},{9,8},{10,11... | collective-permute-start | bytes 1572872 | tf_op jit(solution)/shard_map/ppermute | solution.py:378
  69.1 1.4 %near_rows.1.refs_1_ = bf16[2048,256]{1,0:T(8,128)(2,1)S(1)} custom-call(s32[16,128]{1,0:T(8,128)S(1)} %get-tuple-element.21.refs_0_, bf16[1024,256]{1,0:T(8,128)(2,1)S(1)} %bitcast.11), custom_call_target="tpu_custom_call" | custom-call | flops 1073741824 | tf_op jit(solution)/shard_map/near_rows/pallas_call | solution.py:47
  70.6 2.1 %edge_backward.1.d_first_ref.refs_1_ = bf16[2048,256]{1,0:T(8,128)(2,1)S(1)} custom-call(s32[16,128]{1,0:T(8,128)S(1)} %get-tuple-element.21.refs_0_, bf16[2048,256]{1,0:T(8,128)(2,1)S(1)} %near_rows.1.refs_1_, bf16[1024,256]{1,0:T(8,128)(2,1)S(1)} %collective-permute-done.3.refs_2_, bf16[2048,256]{1,0:T(8,128)(2,1)S(1)} %get-tuple-element.26.refs_1_.refs_3_, ...), custom_call_target="tpu_custom_call" | custom-call | flops 1342177280 | tf_op jit(solution)/shard_map/edge_backward/pallas_call | solution.py:47
  72.7 1.2 %half_away.3 = bf16[1024,256]{1,0:T(8,128)(2,1)S(1)} custom-call(s32[16,128]{1,0:T(8,128)S(1)} %get-tuple-element.21.refs_0_, bf16[2048,256]{1,0:T(8,128)(2,1)S(1)} %edge_backward.1.d_first_ref.refs_1_), custom_call_target="tpu_custom_call" | custom-call | flops 1073741824 | tf_op jit(solution)/shard_map/half_away/pallas_call | solution.py:47
  74.5 1.0 half_here.3.refs_2_
  76.0 1.3 %half_total.3 = bf16[1024,256]{1,0:T(8,128)(2,1)} custom-call(s32[16,128]{1,0:T(8,128)S(1)} %get-tuple-element.21.refs_0_, bf16[2048,256]{1,0:T(8,128)(2,1)S(1)} %edge_backward.1.d_first_ref.refs_1_, f32[768,256]{1,0:T(8,128)S(1)} %half_here.3.refs_2_, bf16[1024,256]{1,0:T(8,128)(2,1)S(1)} %collective-permute-done.6.refs_3_), custom_call_target="tpu_custom_call" | custom-call | flops 268435456 | tf_op jit(solution)/shard_map/half_total/pallas_call | solution.py:47
  77.3 4.3 %all-to-all-start.2 = ((bf16[32,32,256]{2,1,0:T(8,128)(2,1)}), bf16[32,32,256]{2,1,0:T(8,128)(2,1)S(1)}, u32[]{:S(2)}, u32[]{:S(2)}) async-start(bf16[32,32,256]{2,1,0:T(8,128)(2,1)} %bitcast.7), calls=%async_computation.2 | async-start | bytes 1048576 | tf_op jit(solution)/shard_map/all_to_all | solution.py:362
  82.3 2.6 %collective-permute-start.5 = (bf16[64,256]{1,0:T(8,128)(2,1)S(1)}, bf16[64,256]{1,0:T(8,128)(2,1)S(1)}, u32[]{:S(2)}, u32[]{:S(2)}) collective-permute-start(bf16[64,256]{1,0:T(8,128)(2,1)S(1)} %get-tuple-element.36), channel_id=1, source_target_pairs={{0,192},{64,0},{128,64},{192,128},{1,193},{65,1},{129,65},{193,129... | collective-permute-start | bytes 98312 | tf_op jit(solution)/shard_map/ppermute | solution.py:398
  85.0 1.4 %edge_grad.1 = bf16[2048,256]{1,0:T(8,128)(2,1)} custom-call(bf16[2048,256]{1,0:T(8,128)(2,1)S(1)} %edge_backward.1.d_first_ref.refs_1_, bf16[768,256]{1,0:T(8,128)(2,1)S(1)} %copy-done), custom_call_target="tpu_custom_call" | custom-call | flops 268435456 | tf_op jit(solution)/shard_map/edge_grad/pallas_call | solution.py:47
  87.1 1.0 %grid_grad.1 = bf16[768,256]{1,0:T(8,128)(2,1)} custom-call(s32[1,192]{1,0:T(1,128)S(1)} %copy-done.5, bf16[64,256]{1,0:T(8,128)(2,1)S(1)} %collective-permute-done.4.low_ref, bf16[64,256]{1,0:T(8,128)(2,1)S(1)} %get-tuple-element.35.own_ref, bf16[64,256]{1,0:T(8,128)(2,1)S(1)} %collective-permute-done.5.high_ref), custom_call_target="tpu_custom_call" | custom-call | flops 75497472 | tf_op jit(solution)/shard_map/grid_grad/pallas_call | solution.py:47
  88.1 10.1 %all-to-all-done.2.parts_ref = bf16[32,32,256]{2,1,0:T(8,128)(2,1)S(1)} async-done(((bf16[32,32,256]{2,1,0:T(8,128)(2,1)}), bf16[32,32,256]{2,1,0:T(8,128)(2,1)S(1)}, u32[]{:S(2)}, u32[]{:S(2)}) %all-to-all-start.2) | async-done | bytes 524320 | tf_op jit(solution)/shard_map/all_to_all | solution.py:362
  98.2 0.8 mesh_grad.1
  (38 shorter events, 4.0 us)
Async XLA Ops:
  0.6 0.7 copy-start.4
  1.3 1.0 %copy-start.9 = (bf16[768,256]{1,0:T(8,128)(2,1)S(1)}, bf16[768,256]{1,0:T(8,128)(2,1)}, u32[]{:S(2)}) copy-start(bf16[768,256]{1,0:T(8,128)(2,1)} %grid_ref.1) | copy-start | bytes 1179652
  2.3 4.4 %copy-start.6 = (bf16[2048,256]{1,0:T(8,128)(2,1)S(1)}, bf16[2048,256]{1,0:T(8,128)(2,1)}, u32[]{:S(2)}) copy-start(bf16[2048,256]{1,0:T(8,128)(2,1)} %mesh_ref.1) | copy-start | bytes 3145732
  2.6 4.2 %copy-start.11 = (s32[2048]{0:T(1024)S(1)}, s32[2048]{0:T(1024)}, u32[]{:S(2)}) copy-start(s32[2048]{0:T(1024)} %param.19) | copy-start | bytes 24580
  2.6 6.8 %collective-permute-start = (bf16[64,256]{1,0:T(8,128)(2,1)S(1)}, bf16[64,256]{1,0:T(8,128)(2,1)S(1)}, u32[]{:S(2)}, u32[]{:S(2)}) collective-permute-start(bf16[64,256]{1,0:T(8,128)(2,1)S(1)} %get-tuple-element.23), channel_id=1, source_target_pairs={{0,64},{64,128},{128,192},{192,0},{1,65},{65,129},{129,193},{193,1... | collective-permute-start | bytes 98312 | tf_op jit(solution)/shard_map/ppermute | solution.py:325
  4.7 4.7 %collective-permute-start.1 = (bf16[64,256]{1,0:T(8,128)(2,1)S(1)}, bf16[64,256]{1,0:T(8,128)(2,1)S(1)}, u32[]{:S(2)}, u32[]{:S(2)}) collective-permute-start(bf16[64,256]{1,0:T(8,128)(2,1)S(1)} %get-tuple-element.25), channel_id=1, source_target_pairs={{0,192},{64,0},{128,64},{192,128},{1,193},{65,1},{129,65},{193,129... | collective-permute-start | bytes 98312 | tf_op jit(solution)/shard_map/ppermute | solution.py:326
  6.8 2.6 %copy-start = (bf16[768,256]{1,0:T(8,128)(2,1)S(1)}, bf16[768,256]{1,0:T(8,128)(2,1)}, u32[]{:S(2)}) copy-start(bf16[768,256]{1,0:T(8,128)(2,1)} %first_ref.9) | copy-start | bytes 1179652
  6.8 2.6 %copy-start.3 = (s32[2048]{0:T(1024)S(1)}, s32[2048]{0:T(1024)}, u32[]{:S(2)}) copy-start(s32[2048]{0:T(1024)} %param.18) | copy-start | bytes 24580
  6.8 2.6 %copy-start.7 = (bf16[2048,256]{1,0:T(8,128)(2,1)S(1)}, bf16[2048,256]{1,0:T(8,128)(2,1)}, u32[]{:S(2)}) copy-start(bf16[2048,256]{1,0:T(8,128)(2,1)} %edge_ref.1) | copy-start | bytes 3145732
  6.8 2.6 %copy-start.10 = (bf16[256,256]{1,0:T(8,128)(2,1)S(1)}, bf16[256,256]{1,0:T(8,128)(2,1)}, u32[]{:S(2)}) copy-start(bf16[256,256]{1,0:T(8,128)(2,1)} %refs_5_.1) | copy-start | bytes 393220
  11.6 4.5 %copy-start.8 = (bf16[2048,256]{1,0:T(8,128)(2,1)S(1)}, bf16[2048,256]{1,0:T(8,128)(2,1)}, u32[]{:S(2)}) copy-start(bf16[2048,256]{1,0:T(8,128)(2,1)} %refs_2_.1) | copy-start | bytes 3145732
  11.7 4.4 %copy-start.13 = (f32[256]{0:T(256)S(1)}, f32[256]{0:T(256)}, u32[]{:S(2)}) copy-start(f32[256]{0:T(256)} %param.24) | copy-start | bytes 3076
  12.9 4.8 %collective-permute-start.2 = (bf16[1024,256]{1,0:T(8,128)(2,1)S(1)}, bf16[1024,256]{1,0:T(8,128)(2,1)S(1)}, u32[]{:S(2)}, u32[]{:S(2)}) collective-permute-start(bf16[1024,256]{1,0:T(8,128)(2,1)S(1)} %half_away.2), channel_id=1, source_target_pairs={{0,1},{1,0},{2,3},{3,2},{4,5},{5,4},{6,7},{7,6},{8,9},{9,8},{10,11... | collective-permute-start | bytes 1572872 | tf_op jit(solution)/shard_map/ppermute | solution.py:350
  16.1 0.7 copy-start.12
  18.2 26.1 %copy-start.1 = (bf16[512,256]{1,0:T(8,128)(2,1)S(1)}, bf16[512,256]{1,0:T(8,128)(2,1)}, u32[]{:S(2)}) copy-start(bf16[512,256]{1,0:T(8,128)(2,1)} %first_ref.6) | copy-start | bytes 786436
  18.2 26.1 %copy-start.2 = (bf16[256,256]{1,0:T(8,128)(2,1)S(1)}, bf16[256,256]{1,0:T(8,128)(2,1)}, u32[]{:S(2)}) copy-start(bf16[256,256]{1,0:T(8,128)(2,1)} %second_ref.3) | copy-start | bytes 393220
  65.5 5.1 %collective-permute-start.3 = (bf16[1024,256]{1,0:T(8,128)(2,1)S(1)}, bf16[1024,256]{1,0:T(8,128)(2,1)S(1)}, u32[]{:S(2)}, u32[]{:S(2)}) collective-permute-start(bf16[1024,256]{1,0:T(8,128)(2,1)S(1)} %bitcast.10), channel_id=1, source_target_pairs={{0,1},{1,0},{2,3},{3,2},{4,5},{5,4},{6,7},{7,6},{8,9},{9,8},{10,11... | collective-permute-start | bytes 1572872 | tf_op jit(solution)/shard_map/ppermute | solution.py:378
  74.0 2.0 %collective-permute-start.6 = (bf16[1024,256]{1,0:T(8,128)(2,1)S(1)}, bf16[1024,256]{1,0:T(8,128)(2,1)S(1)}, u32[]{:S(2)}, u32[]{:S(2)}) collective-permute-start(bf16[1024,256]{1,0:T(8,128)(2,1)S(1)} %half_away.3), channel_id=1, source_target_pairs={{0,1},{1,0},{2,3},{3,2},{4,5},{5,4},{6,7},{7,6},{8,9},{9,8},{10,11... | collective-permute-start | bytes 1572872 | tf_op jit(solution)/shard_map/ppermute | solution.py:350
  77.3 20.9 %all-to-all-start.2 = ((bf16[32,32,256]{2,1,0:T(8,128)(2,1)}), bf16[32,32,256]{2,1,0:T(8,128)(2,1)S(1)}, u32[]{:S(2)}, u32[]{:S(2)}) async-start(bf16[32,32,256]{2,1,0:T(8,128)(2,1)} %bitcast.7), calls=%async_computation.2 | async-start | bytes 1048576 | tf_op jit(solution)/shard_map/all_to_all | solution.py:362
  82.2 4.3 %collective-permute-start.4 = (bf16[64,256]{1,0:T(8,128)(2,1)S(1)}, bf16[64,256]{1,0:T(8,128)(2,1)S(1)}, u32[]{:S(2)}, u32[]{:S(2)}) collective-permute-start(bf16[64,256]{1,0:T(8,128)(2,1)S(1)} %get-tuple-element.34), channel_id=1, source_target_pairs={{0,64},{64,128},{128,192},{192,0},{1,65},{65,129},{129,193},{193,1... | collective-permute-start | bytes 98312 | tf_op jit(solution)/shard_map/ppermute | solution.py:397
  82.3 4.2 %collective-permute-start.5 = (bf16[64,256]{1,0:T(8,128)(2,1)S(1)}, bf16[64,256]{1,0:T(8,128)(2,1)S(1)}, u32[]{:S(2)}, u32[]{:S(2)}) collective-permute-start(bf16[64,256]{1,0:T(8,128)(2,1)S(1)} %get-tuple-element.36), channel_id=1, source_target_pairs={{0,192},{64,0},{128,64},{192,128},{1,193},{65,1},{129,65},{193,129... | collective-permute-start | bytes 98312 | tf_op jit(solution)/shard_map/ppermute | solution.py:398
  86.4 0.7 copy-start.5

commit v4 on v3

--- a/solution.py
+++ b/solution.py
@@ -134,34 +134,30 @@
     return (lax.axis_index("z") * 8 + lax.axis_index("y") * 2 + lax.axis_index("core")).astype(i32)
 
 
-def half_row(i, core, own):
-    return (i // own) * (2 * own) + core * own + i % own
-
-
-def half_rows(own, core, live, value_ref, start):
-    spot = half_row(lax.broadcasted_iota(i32, (CHUNK, LANES), 0) + start, core, own)
-    total = jnp.zeros((CHUNK, value_ref.shape[1]), f32)
+def my_lane(shift):
+    return lax.rem(lax.axis_index("y").astype(i32) + shift, lax.axis_size("y"))
+
+
+def block_sum(own, y, core, live, value_ref):
+    lanes = lax.axis_size("y")
+    i = lax.broadcasted_iota(i32, (own * lax.axis_size("z"), LANES), 0)
+    spot = (i // own) * (2 * lanes * own) + (2 * y + core) * own + i % own
+    total = jnp.zeros((spot.shape[0], value_ref.shape[1]), f32)
     for begin, at in chunks(value_ref.shape[0], CHUNK):
         total = total + dot(row_hot(spot, live, begin, CHUNK), value_ref[at, :])
     return total
 
 
+SHIFTS = (2, 1, 3, 0)
+
+
 def half_sum_kernel(own, here, live_ref, value_ref, out_ref):
     live = live_ref[...]
     core = my_core() if here else 1 - my_core()
-    for start, at in chunks(out_ref.shape[0], CHUNK):
-        out_ref[at, :] = half_rows(own, core, live, value_ref, start).astype(out_ref.dtype)
-
-
-def half_total_kernel(own, live_ref, value_ref, begun_ref, away_ref, out_ref):
-    done = begun_ref.shape[0]
-    live = live_ref[...]
-    for start, at in chunks(out_ref.shape[0], CHUNK):
-        if start < done:
-            here = begun_ref[at, :]
-        else:
-            here = half_rows(own, my_core(), live, value_ref, start)
-        out_ref[at, :] = (here + away_ref[at, :].astype(f32)).astype(bf16)
+    size = out_ref.shape[0] // len(SHIFTS)
+    for n, shift in enumerate(SHIFTS):
+        total = block_sum(own, my_lane(shift), core, live, value_ref)
+        out_ref[n * size : (n + 1) * size, :] = total.astype(out_ref.dtype)
 
 
 def half_first_kernel(
@@ -171,6 +167,18 @@
     own_cot_ref[...] = cot_ref[pl.ds(pl.multiple_of(my_block() * own, own), own), :]
     gains_ref[0:1, :] = node_gain_ref[...]
     gains_ref[1:2, :] = edge_gain_ref[...]
+
+
+def pieces_kernel(here_ref, away_ref, *out_refs):
+    size = here_ref.shape[0] // len(out_refs)
+    for n, out_ref in enumerate(out_refs):
+        at = slice(n * size, (n + 1) * size)
+        out_ref[...] = (here_ref[at, :] + away_ref[at, :].astype(f32)).astype(out_ref.dtype)
+
+
+def total_kernel(a_ref, b_ref, c_ref, here_ref, out_ref):
+    far = a_ref[...].astype(f32) + (b_ref[...].astype(f32) + c_ref[...].astype(f32))
+    out_ref[...] = (here_ref[...] + far).astype(bf16).reshape(out_ref.shape)
 
 
 def norm(value):
@@ -340,11 +348,13 @@
         name="edge_forward",
     )
 
+    lanes = lax.axis_size("y")
+    columns = lax.axis_size("z")
+    piece = columns * own
+
     def to_owners(value, extras=(), extra_outs=()):
-        shape = (half, width)
-        begun = half - CHUNK
         (out,) = call(
-            lambda *refs: half_sum_kernel(own, False, *refs), [(shape, bf16)],
+            lambda *refs: half_sum_kernel(own, False, *refs), [((half, width), bf16)],
             (live, value), flops=big // 2, name="half_away",
         )
         away = lax.ppermute(out, "core", swap)
@@ -352,14 +362,20 @@
             (lambda *refs: half_first_kernel(own, *refs))
             if extras
             else (lambda *refs: half_sum_kernel(own, True, *refs)),
-            [((begun, width), f32)] + list(extra_outs),
+            [((half, width), f32)] + list(extra_outs),
             (live, value) + tuple(extras), flops=big // 2, name="half_here",
         )
-        (both,) = call(
-            lambda *refs: half_total_kernel(own, *refs), [(shape, bf16)],
-            (live, value, here[0], away), flops=big // 8, name="half_total",
+        sums = call(
+            pieces_kernel,
+            [((piece, width), bf16 if shift else f32) for shift in SHIFTS],
+            (here[0], away), name="pieces",
         )
-        parts = lax.all_to_all(both.reshape(owners, own, width), zy, 0, 0, tiled=True)
+        got = [
+            lax.ppermute(total, "y", ring(lanes, shift)) if shift else total
+            for shift, total in zip(SHIFTS, sums)
+        ]
+        (both,) = call(total_kernel, [((columns, own, width), bf16)], got, name="total")
+        parts = lax.all_to_all(both, "z", 0, 0, tiled=True)
         return (parts,) + tuple(here[1:])
 
     parts, own_cot, gains = to_owners(

time: 99.3 us -> 96.2 us (0.969)
  blocking collectives: 46.1 us -> 32.7 us
  starting transfers between devices: 17.7 us -> 26.3 us
  waiting for transfers between devices: 10.9 us -> 12.5 us
    all_to_all x1, blocking collectives: 26 us -> 14.1 us  [to_owners(): parts = lax.all_to_all(both, 'z', 0, 0, tiled=True)]
    ppermute x0 -> x6, waiting for transfers between devices: none -> 10.9 us  [to_owners(): lax.ppermute(total, 'y', ring(lanes, shift))]
    all_to_all x1, waiting for transfers between devices: 10.1 us -> 1.19 us  [to_owners(): parts = lax.all_to_all(both, 'z', 0, 0, tiled=True)]
    ppermute x0 -> x6, starting transfers between devices: none -> 8.53 us  [to_owners(): lax.ppermute(total, 'y', ring(lanes, shift))]
    all_to_all x1, blocking collectives: 20 us -> 18.5 us  [shards(): lax.all_to_all(grad_copies, zy, 0, 0, tiled=True).reshape(half, width)]
    ppermute x1, starting transfers between devices: 3.55 us -> 4.55 us  [shards(): far = lax.ppermute(near, 'core', swap)]
    pallas_call x16 -> x18, Pallas kernels: 19.9 us -> 19.7 us  [call(): pl.pallas_call(kernel, out_shape=[jax.ShapeDtypeStruct(s, d) for s, d in...]
  transfers between devices with their start and end apart: 8 -> 14, of which waited for: 4 -> 7; matrix products, arithmetic and copies ran while one was open for 0% -> 0% of each run, Pallas kernels for 9% -> 10%
where the time goes in v4:
time: 96.2 us; the launch traced here: 95.8 us
  blocking collectives  32.7 us (34%)
  starting transfers between devices  26.3 us (27%)
  Pallas kernels  19.7 us (20%)
  waiting for transfers between devices  12.5 us (13%)
  local copies, waits for them, and re-layouts  3.07 us (3%)
  between operations  1.54 us (2%)
    pallas_call x18, Pallas kernels, call(): pl.pallas_call(kernel, out_shape=[jax.ShapeDtypeStruct(s, d) for s, d in...  19.7 us
    all_to_all x1, blocking collectives, shards(): lax.all_to_all(grad_copies, zy, 0, 0, tiled=True).reshape(half, width)  18.5 us
    all_to_all x1, blocking collectives, to_owners(): parts = lax.all_to_all(both, 'z', 0, 0, tiled=True)  14.1 us
    ppermute x6, waiting for transfers between devices, to_owners(): lax.ppermute(total, 'y', ring(lanes, shift))  10.9 us
    ppermute x6, starting transfers between devices, to_owners(): lax.ppermute(total, 'y', ring(lanes, shift))  8.53 us
    ppermute x1, starting transfers between devices, shards(): far = lax.ppermute(near, 'core', swap)  4.55 us
    ppermute x2, starting transfers between devices, to_owners(): away = lax.ppermute(out, 'core', swap)  3.62 us
    all_to_all x1, starting transfers between devices, to_owners(): parts = lax.all_to_all(both, 'z', 0, 0, tiled=True)  3.37 us
  transfers between devices with their start and end apart: 14, of which 7 were waited for; matrix products, arithmetic and copies ran while one was open for 0% of the time, Pallas kernels for 10%

profile of v4, /device:TPU:1, one launch (start us, length us, event | category | flops | bytes accessed | tf_op | source)
XLA Modules:
  0.0 95.8 jit_solution(15627452313799403260)
XLA Ops:
  2.6 2.1 %collective-permute-start = (bf16[64,256]{1,0:T(8,128)(2,1)S(1)}, bf16[64,256]{1,0:T(8,128)(2,1)S(1)}, u32[]{:S(2)}, u32[]{:S(2)}) collective-permute-start(bf16[64,256]{1,0:T(8,128)(2,1)S(1)} %get-tuple-element.31), channel_id=1, source_target_pairs={{0,64},{64,128},{128,192},{192,0},{1,65},{65,129},{129,193},{193,1... | collective-permute-start | bytes 98312 | tf_op jit(solution)/shard_map/ppermute | solution.py:333
  4.7 1.4 %collective-permute-start.1 = (bf16[64,256]{1,0:T(8,128)(2,1)S(1)}, bf16[64,256]{1,0:T(8,128)(2,1)S(1)}, u32[]{:S(2)}, u32[]{:S(2)}) collective-permute-start(bf16[64,256]{1,0:T(8,128)(2,1)S(1)} %get-tuple-element.33), channel_id=1, source_target_pairs={{0,192},{64,0},{128,64},{192,128},{1,193},{65,1},{129,65},{193,129... | collective-permute-start | bytes 98312 | tf_op jit(solution)/shard_map/ppermute | solution.py:334
  6.8 2.6 %mesh_rows.1 = (bf16[2048,256]{1,0:T(8,128)(2,1)S(1)}, bf16[32,256]{1,0:T(8,128)(2,1)S(1)}, s32[16,128]{1,0:T(8,128)S(1)}) custom-call(s32[1,1]{1,0:T(1,128)} %bitcast.6.count_ref, s32[16,128]{1,0:T(8,128)S(1)} %bitcast.11, bf16[2048,256]{1,0:T(8,128)(2,1)S(1)} %copy-done.6), custom_call_target="tpu_custom_call" | custom-call | flops 2147483648 | tf_op jit(solution)/shard_map/mesh_rows/pallas_call | solution.py:47
  9.5 2.2 %edge_forward.1 = (bf16[2048,256]{1,0:T(8,128)(2,1)S(1)}, bf16[2048,256]{1,0:T(8,128)(2,1)S(1)}) custom-call(s32[16,128]{1,0:T(8,128)S(1)} %bitcast.9, bf16[2048,256]{1,0:T(8,128)(2,1)S(1)} %copy-done.7, bf16[2048,256]{1,0:T(8,128)(2,1)S(1)} %get-tuple-element.30.mesh_rows_ref, bf16[64,256]{1,0:T(8,128)(2,1)S(1)} %collective-permute-done.low_ref, ...), custom_call_target="tpu_custom_call" | custom-call | flops 1342177280 | tf_op jit(solution)/shard_map/edge_forward/pallas_call | solution.py:47
  11.7 1.3 %half_away.2 = bf16[1024,256]{1,0:T(8,128)(2,1)S(1)} custom-call(s32[16,128]{1,0:T(8,128)S(1)} %get-tuple-element.29.refs_0_, bf16[2048,256]{1,0:T(8,128)(2,1)S(1)} %get-tuple-element.34.refs_1_.refs_3_), custom_call_target="tpu_custom_call" | custom-call | flops 1073741824 | tf_op jit(solution)/shard_map/half_away/pallas_call | solution.py:47
  13.0 3.2 %collective-permute-start.2 = (bf16[1024,256]{1,0:T(8,128)(2,1)S(1)}, bf16[1024,256]{1,0:T(8,128)(2,1)S(1)}, u32[]{:S(2)}, u32[]{:S(2)}) collective-permute-start(bf16[1024,256]{1,0:T(8,128)(2,1)S(1)} %half_away.2), channel_id=1, source_target_pairs={{0,1},{1,0},{2,3},{3,2},{4,5},{5,4},{6,7},{7,6},{8,9},{9,8},{10,11... | collective-permute-start | bytes 1572872 | tf_op jit(solution)/shard_map/ppermute | solution.py:360
  16.8 1.2 %half_here.2 = (f32[1024,256]{1,0:T(8,128)S(1)}, bf16[32,256]{1,0:T(8,128)(2,1)S(1)}, f32[2,256]{1,0:T(2,128)S(1)}) custom-call(s32[16,128]{1,0:T(8,128)S(1)} %get-tuple-element.29.refs_0_, bf16[2048,256]{1,0:T(8,128)(2,1)S(1)} %get-tuple-element.34.refs_1_.refs_3_, bf16[2048,256]{1,0:T(8,128)(2,1)S(1)} %copy-done.8, f32[1,256]{1,0:T(1,128)S(1)} %bitcast.12, ...), custom_call_target="tpu_custom_call" | custom-call | flops 1073741824 | tf_op jit(solution)/shard_map/half_here/pallas_call | solution.py:47
  18.2 1.3 %collective-permute-start.3 = (bf16[256,256]{1,0:T(8,128)(2,1)S(1)}, bf16[256,256]{1,0:T(8,128)(2,1)S(1)}, u32[]{:S(2)}, u32[]{:S(2)}) collective-permute-start(bf16[256,256]{1,0:T(8,128)(2,1)S(1)} %get-tuple-element.36), channel_id=1, source_target_pairs={{0,4},{2,6},{4,0},{6,2},{1,5},{3,7},{5,1},{7,3},{8,12},{10,14},{12... | collective-permute-start | bytes 393224 | tf_op jit(solution)/shard_map/ppermute | solution.py:374
  19.8 2.3 %collective-permute-start.5 = (bf16[256,256]{1,0:T(8,128)(2,1)S(1)}, bf16[256,256]{1,0:T(8,128)(2,1)S(1)}, u32[]{:S(2)}, u32[]{:S(2)}) collective-permute-start(bf16[256,256]{1,0:T(8,128)(2,1)S(1)} %get-tuple-element.38), channel_id=1, source_target_pairs={{0,6},{2,0},{4,2},{6,4},{1,7},{3,1},{5,3},{7,5},{8,14},{10,8},{12,... | collective-permute-start | bytes 393224 | tf_op jit(solution)/shard_map/ppermute | solution.py:374
  22.1 2.8 %collective-permute-done.3.a_ref = bf16[256,256]{1,0:T(8,128)(2,1)S(1)} collective-permute-done((bf16[256,256]{1,0:T(8,128)(2,1)S(1)}, bf16[256,256]{1,0:T(8,128)(2,1)S(1)}, u32[]{:S(2)}, u32[]{:S(2)}) %collective-permute-start.3) | collective-permute-done | bytes 131104 | tf_op jit(solution)/shard_map/ppermute | solution.py:374
  24.9 3.1 %collective-permute-done.4.b_ref = bf16[256,256]{1,0:T(8,128)(2,1)S(1)} collective-permute-done((bf16[256,256]{1,0:T(8,128)(2,1)S(1)}, bf16[256,256]{1,0:T(8,128)(2,1)S(1)}, u32[]{:S(2)}, u32[]{:S(2)}) %collective-permute-start.4) | collective-permute-done | bytes 131104 | tf_op jit(solution)/shard_map/ppermute | solution.py:374
  28.1 14.1 %all_to_all.15.parts_ref = bf16[8,32,256]{2,1,0:T(8,128)(2,1)S(1)} all-to-all(bf16[8,32,256]{2,1,0:T(8,128)(2,1)S(1)} %total.2), channel_id=1, replica_groups=mesh['lon'=4,'z'=8,'y'=4,'core'=2] {'z'}, dimensions={0} | all-to-all | bytes 262144 | tf_op jit(solution)/shard_map/all_to_all | solution.py:378
  43.4 18.5 %all_to_all.16 = bf16[32,32,256]{2,1,0:T(8,128)(2,1)S(1)} all-to-all(bf16[32,32,256]{2,1,0:T(8,128)(2,1)S(1)} %get-tuple-element.44), channel_id=1, replica_groups=mesh['lon'=4,'z'=8,'y'=4,'core'=2] {'z','y'}, dimensions={0} | all-to-all | bytes 1048576 | tf_op jit(solution)/shard_map/all_to_all | solution.py:393
  61.9 4.5 %collective-permute-start.6 = (bf16[1024,256]{1,0:T(8,128)(2,1)S(1)}, bf16[1024,256]{1,0:T(8,128)(2,1)S(1)}, u32[]{:S(2)}, u32[]{:S(2)}) collective-permute-start(bf16[1024,256]{1,0:T(8,128)(2,1)S(1)} %bitcast.7), channel_id=1, source_target_pairs={{0,1},{1,0},{2,3},{3,2},{4,5},{5,4},{6,7},{7,6},{8,9},{9,8},{10,11... | collective-permute-start | bytes 1572872 | tf_op jit(solution)/shard_map/ppermute | solution.py:394
  66.5 1.4 %near_rows.1.refs_1_ = bf16[2048,256]{1,0:T(8,128)(2,1)S(1)} custom-call(s32[16,128]{1,0:T(8,128)S(1)} %get-tuple-element.29.refs_0_, bf16[1024,256]{1,0:T(8,128)(2,1)S(1)} %bitcast.8), custom_call_target="tpu_custom_call" | custom-call | flops 1073741824 | tf_op jit(solution)/shard_map/near_rows/pallas_call | solution.py:47
  68.0 2.2 %edge_backward.1.d_first_ref.refs_1_ = bf16[2048,256]{1,0:T(8,128)(2,1)S(1)} custom-call(s32[16,128]{1,0:T(8,128)S(1)} %get-tuple-element.29.refs_0_, bf16[2048,256]{1,0:T(8,128)(2,1)S(1)} %near_rows.1.refs_1_, bf16[1024,256]{1,0:T(8,128)(2,1)S(1)} %collective-permute-done.6.refs_2_, bf16[2048,256]{1,0:T(8,128)(2,1)S(1)} %get-tuple-element.34.refs_1_.refs_3_, ...), custom_call_target="tpu_custom_call" | custom-call | flops 1342177280 | tf_op jit(solution)/shard_map/edge_backward/pallas_call | solution.py:47
  70.3 1.2 %half_away.3 = bf16[1024,256]{1,0:T(8,128)(2,1)S(1)} custom-call(s32[16,128]{1,0:T(8,128)S(1)} %get-tuple-element.29.refs_0_, bf16[2048,256]{1,0:T(8,128)(2,1)S(1)} %edge_backward.1.d_first_ref.refs_1_), custom_call_target="tpu_custom_call" | custom-call | flops 1073741824 | tf_op jit(solution)/shard_map/half_away/pallas_call | solution.py:47
  73.6 1.9 %collective-permute-start.10 = (bf16[256,256]{1,0:T(8,128)(2,1)S(1)}, bf16[256,256]{1,0:T(8,128)(2,1)S(1)}, u32[]{:S(2)}, u32[]{:S(2)}) collective-permute-start(bf16[256,256]{1,0:T(8,128)(2,1)S(1)} %get-tuple-element.49), channel_id=1, source_target_pairs={{0,4},{2,6},{4,0},{6,2},{1,5},{3,7},{5,1},{7,3},{8,12},{10,14},{12... | collective-permute-start | bytes 393224 | tf_op jit(solution)/shard_map/ppermute | solution.py:374
  75.8 2.4 %collective-permute-start.12 = (bf16[256,256]{1,0:T(8,128)(2,1)S(1)}, bf16[256,256]{1,0:T(8,128)(2,1)S(1)}, u32[]{:S(2)}, u32[]{:S(2)}) collective-permute-start(bf16[256,256]{1,0:T(8,128)(2,1)S(1)} %get-tuple-element.51), channel_id=1, source_target_pairs={{0,6},{2,0},{4,2},{6,4},{1,7},{3,1},{5,3},{7,5},{8,14},{10,8},{12,... | collective-permute-start | bytes 393224 | tf_op jit(solution)/shard_map/ppermute | solution.py:374
  78.2 1.7 %collective-permute-done.10.a_ref = bf16[256,256]{1,0:T(8,128)(2,1)S(1)} collective-permute-done((bf16[256,256]{1,0:T(8,128)(2,1)S(1)}, bf16[256,256]{1,0:T(8,128)(2,1)S(1)}, u32[]{:S(2)}, u32[]{:S(2)}) %collective-permute-start.10) | collective-permute-done | bytes 131104 | tf_op jit(solution)/shard_map/ppermute | solution.py:374
  79.9 3.3 %collective-permute-done.11.b_ref = bf16[256,256]{1,0:T(8,128)(2,1)S(1)} collective-permute-done((bf16[256,256]{1,0:T(8,128)(2,1)S(1)}, bf16[256,256]{1,0:T(8,128)(2,1)S(1)}, u32[]{:S(2)}, u32[]{:S(2)}) %collective-permute-start.11) | collective-permute-done | bytes 131104 | tf_op jit(solution)/shard_map/ppermute | solution.py:374
  83.9 3.4 %all-to-all-start.2 = ((bf16[8,32,256]{2,1,0:T(8,128)(2,1)}), bf16[8,32,256]{2,1,0:T(8,128)(2,1)S(1)}, u32[]{:S(2)}, u32[]{:S(2)}) async-start(bf16[8,32,256]{2,1,0:T(8,128)(2,1)} %total.3), calls=%async_computation.2 | async-start | bytes 262144 | tf_op jit(solution)/shard_map/all_to_all | solution.py:378
  88.1 2.6 %collective-permute-start.8 = (bf16[64,256]{1,0:T(8,128)(2,1)S(1)}, bf16[64,256]{1,0:T(8,128)(2,1)S(1)}, u32[]{:S(2)}, u32[]{:S(2)}) collective-permute-start(bf16[64,256]{1,0:T(8,128)(2,1)S(1)} %get-tuple-element.48), channel_id=1, source_target_pairs={{0,192},{64,0},{128,64},{192,128},{1,193},{65,1},{129,65},{193,129... | collective-permute-start | bytes 98312 | tf_op jit(solution)/shard_map/ppermute | solution.py:414
  90.7 1.4 %edge_grad.1 = bf16[2048,256]{1,0:T(8,128)(2,1)} custom-call(bf16[2048,256]{1,0:T(8,128)(2,1)S(1)} %edge_backward.1.d_first_ref.refs_1_, bf16[768,256]{1,0:T(8,128)(2,1)S(1)} %copy-done), custom_call_target="tpu_custom_call" | custom-call | flops 268435456 | tf_op jit(solution)/shard_map/edge_grad/pallas_call | solution.py:47
  (52 shorter events, 12.0 us)
Async XLA Ops:
  2.3 4.4 %copy-start.6 = (bf16[2048,256]{1,0:T(8,128)(2,1)S(1)}, bf16[2048,256]{1,0:T(8,128)(2,1)}, u32[]{:S(2)}) copy-start(bf16[2048,256]{1,0:T(8,128)(2,1)} %mesh_ref.1) | copy-start | bytes 3145732
  2.6 4.2 %copy-start.11 = (s32[2048]{0:T(1024)S(1)}, s32[2048]{0:T(1024)}, u32[]{:S(2)}) copy-start(s32[2048]{0:T(1024)} %param.19) | copy-start | bytes 24580
  2.6 6.8 %collective-permute-start = (bf16[64,256]{1,0:T(8,128)(2,1)S(1)}, bf16[64,256]{1,0:T(8,128)(2,1)S(1)}, u32[]{:S(2)}, u32[]{:S(2)}) collective-permute-start(bf16[64,256]{1,0:T(8,128)(2,1)S(1)} %get-tuple-element.31), channel_id=1, source_target_pairs={{0,64},{64,128},{128,192},{192,0},{1,65},{65,129},{129,193},{193,1... | collective-permute-start | bytes 98312 | tf_op jit(solution)/shard_map/ppermute | solution.py:333
  4.7 4.7 %collective-permute-start.1 = (bf16[64,256]{1,0:T(8,128)(2,1)S(1)}, bf16[64,256]{1,0:T(8,128)(2,1)S(1)}, u32[]{:S(2)}, u32[]{:S(2)}) collective-permute-start(bf16[64,256]{1,0:T(8,128)(2,1)S(1)} %get-tuple-element.33), channel_id=1, source_target_pairs={{0,192},{64,0},{128,64},{192,128},{1,193},{65,1},{129,65},{193,129... | collective-permute-start | bytes 98312 | tf_op jit(solution)/shard_map/ppermute | solution.py:334
  6.8 2.6 %copy-start = (bf16[768,256]{1,0:T(8,128)(2,1)S(1)}, bf16[768,256]{1,0:T(8,128)(2,1)}, u32[]{:S(2)}) copy-start(bf16[768,256]{1,0:T(8,128)(2,1)} %first_ref.9) | copy-start | bytes 1179652
  6.8 2.6 %copy-start.3 = (s32[2048]{0:T(1024)S(1)}, s32[2048]{0:T(1024)}, u32[]{:S(2)}) copy-start(s32[2048]{0:T(1024)} %param.18) | copy-start | bytes 24580
  6.8 2.6 %copy-start.7 = (bf16[2048,256]{1,0:T(8,128)(2,1)S(1)}, bf16[2048,256]{1,0:T(8,128)(2,1)}, u32[]{:S(2)}) copy-start(bf16[2048,256]{1,0:T(8,128)(2,1)} %edge_ref.1) | copy-start | bytes 3145732
  6.8 2.6 %copy-start.10 = (bf16[256,256]{1,0:T(8,128)(2,1)S(1)}, bf16[256,256]{1,0:T(8,128)(2,1)}, u32[]{:S(2)}) copy-start(bf16[256,256]{1,0:T(8,128)(2,1)} %refs_5_.1) | copy-start | bytes 393220
  11.7 4.5 %copy-start.8 = (bf16[2048,256]{1,0:T(8,128)(2,1)S(1)}, bf16[2048,256]{1,0:T(8,128)(2,1)}, u32[]{:S(2)}) copy-start(bf16[2048,256]{1,0:T(8,128)(2,1)} %refs_2_.1) | copy-start | bytes 3145732
  11.7 4.4 %copy-start.13 = (f32[256]{0:T(256)S(1)}, f32[256]{0:T(256)}, u32[]{:S(2)}) copy-start(f32[256]{0:T(256)} %param.24) | copy-start | bytes 3076
  13.0 5.1 %collective-permute-start.2 = (bf16[1024,256]{1,0:T(8,128)(2,1)S(1)}, bf16[1024,256]{1,0:T(8,128)(2,1)S(1)}, u32[]{:S(2)}, u32[]{:S(2)}) collective-permute-start(bf16[1024,256]{1,0:T(8,128)(2,1)S(1)} %half_away.2), channel_id=1, source_target_pairs={{0,1},{1,0},{2,3},{3,2},{4,5},{5,4},{6,7},{7,6},{8,9},{9,8},{10,11... | collective-permute-start | bytes 1572872 | tf_op jit(solution)/shard_map/ppermute | solution.py:360
  18.2 6.7 %collective-permute-start.3 = (bf16[256,256]{1,0:T(8,128)(2,1)S(1)}, bf16[256,256]{1,0:T(8,128)(2,1)S(1)}, u32[]{:S(2)}, u32[]{:S(2)}) collective-permute-start(bf16[256,256]{1,0:T(8,128)(2,1)S(1)} %get-tuple-element.36), channel_id=1, source_target_pairs={{0,4},{2,6},{4,0},{6,2},{1,5},{3,7},{5,1},{7,3},{8,12},{10,14},{12... | collective-permute-start | bytes 393224 | tf_op jit(solution)/shard_map/ppermute | solution.py:374
  19.4 8.6 %collective-permute-start.4 = (bf16[256,256]{1,0:T(8,128)(2,1)S(1)}, bf16[256,256]{1,0:T(8,128)(2,1)S(1)}, u32[]{:S(2)}, u32[]{:S(2)}) collective-permute-start(bf16[256,256]{1,0:T(8,128)(2,1)S(1)} %get-tuple-element.37), channel_id=1, source_target_pairs={{0,2},{2,4},{4,6},{6,0},{1,3},{3,5},{5,7},{7,1},{8,10},{10,12},{12... | collective-permute-start | bytes 393224 | tf_op jit(solution)/shard_map/ppermute | solution.py:374
  19.8 8.2 %collective-permute-start.5 = (bf16[256,256]{1,0:T(8,128)(2,1)S(1)}, bf16[256,256]{1,0:T(8,128)(2,1)S(1)}, u32[]{:S(2)}, u32[]{:S(2)}) collective-permute-start(bf16[256,256]{1,0:T(8,128)(2,1)S(1)} %get-tuple-element.38), channel_id=1, source_target_pairs={{0,6},{2,0},{4,2},{6,4},{1,7},{3,1},{5,3},{7,5},{8,14},{10,8},{12,... | collective-permute-start | bytes 393224 | tf_op jit(solution)/shard_map/ppermute | solution.py:374
  28.0 14.2 %copy-start.2 = (bf16[256,256]{1,0:T(8,128)(2,1)S(1)}, bf16[256,256]{1,0:T(8,128)(2,1)}, u32[]{:S(2)}) copy-start(bf16[256,256]{1,0:T(8,128)(2,1)} %second_ref.3) | copy-start | bytes 393220
  28.1 14.2 %copy-start.1 = (bf16[512,256]{1,0:T(8,128)(2,1)S(1)}, bf16[512,256]{1,0:T(8,128)(2,1)}, u32[]{:S(2)}) copy-start(bf16[512,256]{1,0:T(8,128)(2,1)} %first_ref.6) | copy-start | bytes 786436
  61.9 6.1 %collective-permute-start.6 = (bf16[1024,256]{1,0:T(8,128)(2,1)S(1)}, bf16[1024,256]{1,0:T(8,128)(2,1)S(1)}, u32[]{:S(2)}, u32[]{:S(2)}) collective-permute-start(bf16[1024,256]{1,0:T(8,128)(2,1)S(1)} %bitcast.7), channel_id=1, source_target_pairs={{0,1},{1,0},{2,3},{3,2},{4,5},{5,4},{6,7},{7,6},{8,9},{9,8},{10,11... | collective-permute-start | bytes 1572872 | tf_op jit(solution)/shard_map/ppermute | solution.py:394
  71.5 2.0 %collective-permute-start.9 = (bf16[1024,256]{1,0:T(8,128)(2,1)S(1)}, bf16[1024,256]{1,0:T(8,128)(2,1)S(1)}, u32[]{:S(2)}, u32[]{:S(2)}) collective-permute-start(bf16[1024,256]{1,0:T(8,128)(2,1)S(1)} %half_away.3), channel_id=1, source_target_pairs={{0,1},{1,0},{2,3},{3,2},{4,5},{5,4},{6,7},{7,6},{8,9},{9,8},{10,11... | collective-permute-start | bytes 1572872 | tf_op jit(solution)/shard_map/ppermute | solution.py:360
  73.6 6.3 %collective-permute-start.10 = (bf16[256,256]{1,0:T(8,128)(2,1)S(1)}, bf16[256,256]{1,0:T(8,128)(2,1)S(1)}, u32[]{:S(2)}, u32[]{:S(2)}) collective-permute-start(bf16[256,256]{1,0:T(8,128)(2,1)S(1)} %get-tuple-element.49), channel_id=1, source_target_pairs={{0,4},{2,6},{4,0},{6,2},{1,5},{3,7},{5,1},{7,3},{8,12},{10,14},{12... | collective-permute-start | bytes 393224 | tf_op jit(solution)/shard_map/ppermute | solution.py:374
  75.5 7.7 %collective-permute-start.11 = (bf16[256,256]{1,0:T(8,128)(2,1)S(1)}, bf16[256,256]{1,0:T(8,128)(2,1)S(1)}, u32[]{:S(2)}, u32[]{:S(2)}) collective-permute-start(bf16[256,256]{1,0:T(8,128)(2,1)S(1)} %get-tuple-element.50), channel_id=1, source_target_pairs={{0,2},{2,4},{4,6},{6,0},{1,3},{3,5},{5,7},{7,1},{8,10},{10,12},{12... | collective-permute-start | bytes 393224 | tf_op jit(solution)/shard_map/ppermute | solution.py:374
  75.8 7.4 %collective-permute-start.12 = (bf16[256,256]{1,0:T(8,128)(2,1)S(1)}, bf16[256,256]{1,0:T(8,128)(2,1)S(1)}, u32[]{:S(2)}, u32[]{:S(2)}) collective-permute-start(bf16[256,256]{1,0:T(8,128)(2,1)S(1)} %get-tuple-element.51), channel_id=1, source_target_pairs={{0,6},{2,0},{4,2},{6,4},{1,7},{3,1},{5,3},{7,5},{8,14},{10,8},{12,... | collective-permute-start | bytes 393224 | tf_op jit(solution)/shard_map/ppermute | solution.py:374
  83.9 11.1 %all-to-all-start.2 = ((bf16[8,32,256]{2,1,0:T(8,128)(2,1)}), bf16[8,32,256]{2,1,0:T(8,128)(2,1)S(1)}, u32[]{:S(2)}, u32[]{:S(2)}) async-start(bf16[8,32,256]{2,1,0:T(8,128)(2,1)} %total.3), calls=%async_computation.2 | async-start | bytes 262144 | tf_op jit(solution)/shard_map/all_to_all | solution.py:378
  87.9 4.2 %collective-permute-start.7 = (bf16[64,256]{1,0:T(8,128)(2,1)S(1)}, bf16[64,256]{1,0:T(8,128)(2,1)S(1)}, u32[]{:S(2)}, u32[]{:S(2)}) collective-permute-start(bf16[64,256]{1,0:T(8,128)(2,1)S(1)} %get-tuple-element.46), channel_id=1, source_target_pairs={{0,64},{64,128},{128,192},{192,0},{1,65},{65,129},{129,193},{193,1... | collective-permute-start | bytes 98312 | tf_op jit(solution)/shard_map/ppermute | solution.py:413
  88.1 4.1 %collective-permute-start.8 = (bf16[64,256]{1,0:T(8,128)(2,1)S(1)}, bf16[64,256]{1,0:T(8,128)(2,1)S(1)}, u32[]{:S(2)}, u32[]{:S(2)}) collective-permute-start(bf16[64,256]{1,0:T(8,128)(2,1)S(1)} %get-tuple-element.48), channel_id=1, source_target_pairs={{0,192},{64,0},{128,64},{192,128},{1,193},{65,1},{129,65},{193,129... | collective-permute-start | bytes 98312 | tf_op jit(solution)/shard_map/ppermute | solution.py:414
  (4 other events, 3.0 us)

commit v5 on v4

--- a/solution.py
+++ b/solution.py
@@ -78,24 +78,27 @@
     return jnp.where(slot < count, rows, -1)
 
 
-def halo_rows_kernel(list_ref, grid_ref, low_ref, own_ref, high_ref):
-    n = list_ref.shape[1]
-    g = grid_ref.shape[0]
-    hot = one_hot(lax.broadcasted_iota(i32, (g, n), 0) == list_ref[...])
-    rows = dot_tn(hot, grid_ref[...]).astype(bf16)
-    side = n // 3
+def row_index_kernel(out_ref):
+    out_ref[...] = lax.broadcasted_iota(i32, out_ref.shape, 0)
+
+
+def halo_rows_kernel(
+    index_ref, list_ref, grid_ref, count_ref, recv_ref, low_ref, own_ref, high_ref, live_ref
+):
+    rows = dot_tn(one_hot(index_ref[...] == list_ref[...]), grid_ref[...]).astype(bf16)
+    side = rows.shape[0] // 3
     low_ref[...] = rows[0:side]
     own_ref[...] = rows[side : 2 * side]
     high_ref[...] = rows[2 * side :]
-
-
-def mesh_rows_kernel(count_ref, recv_ref, mesh_ref, out_ref, own_ref, live_ref):
+    live_ref[...] = live_rows(recv_ref, count_ref[...])
+
+
+def mesh_rows_kernel(live_ref, mesh_ref, gain_ref, out_ref, own_ref, gain_out_ref):
+    gain_out_ref[...] = gain_ref[...]
     own = own_ref.shape[0]
     own_ref[...] = mesh_ref[pl.ds(pl.multiple_of(my_block() * own, own), own), :]
     m = mesh_ref.shape[0]
-    live = live_rows(recv_ref, count_ref[...])
-    live_ref[...] = live
-    cols = jnp.transpose(live)
+    cols = jnp.transpose(live_ref[...])
     for start, at in chunks(out_ref.shape[0], LANES):
         hot = one_hot(lax.broadcasted_iota(i32, (LANES, m), 1) == column(cols, start, LANES))
         out_ref[at, :] = dot(hot, mesh_ref[...]).astype(bf16)
@@ -188,7 +191,7 @@
 
 
 def node_kernel(
-    parts_ref, mesh_ref, cot_ref, first_ref, second_ref, gains_ref, out_ref, grad_ref, direct_ref,
+    parts_ref, mesh_ref, cot_ref, first_ref, second_ref, gains_ref, grad_ref, normed_ref, d_pre_ref,
 ):
     width = mesh_ref.shape[1]
     aggregate = jnp.sum(parts_ref[...].astype(f32), axis=0)
@@ -200,9 +203,8 @@
     act = (pre * sigma).astype(bf16)
     post = dot(act, second_ref[...])
     normed, factor = norm(post)
-    out_ref[...] = (mesh.astype(f32) + normed * gain).astype(bf16)
-    cotangent = cot_ref[...].astype(f32)
-    scaled = cotangent * gain
+    normed_ref[...] = normed
+    scaled = cot_ref[...].astype(f32) * gain
     d_post = factor * (
         scaled
         - jnp.mean(scaled, axis=-1, keepdims=True)
@@ -212,7 +214,15 @@
     d_pre = d_pre.astype(bf16)
     grad = dot_nt(d_pre, first_ref[width : 2 * width, :]).astype(bf16)
     grad_ref[...] = jnp.broadcast_to(grad[None], grad_ref.shape)
-    direct_ref[...] = cotangent + dot_nt(d_pre, first_ref[0:width, :])
+    d_pre_ref[...] = d_pre
+
+
+def mesh_out_kernel(
+    mesh_ref, cot_ref, normed_ref, d_pre_ref, first_ref, gains_ref, out_ref, direct_ref
+):
+    width = mesh_ref.shape[1]
+    out_ref[...] = (mesh_ref[...].astype(f32) + normed_ref[...] * gains_ref[0:1, :]).astype(bf16)
+    direct_ref[...] = cot_ref[...].astype(f32) + dot_nt(d_pre_ref[...], first_ref[0:width, :])
 
 
 def half_place(own, core, live):
@@ -323,19 +333,22 @@
     dense = 2 * edges * width * width
 
     vm = pltpu.VMEM
-    to_low, stay, to_high = call(
+    (index,) = call(
+        row_index_kernel, [((grid_rows, listed), i32)], (), flops=2 * big, name="row_index"
+    )
+    to_low, stay, to_high, live = call(
         halo_rows_kernel,
-        [((side, width), bf16)] * 3,
-        (send_rows, grid_latent),
+        [((side, width), bf16)] * 3 + [(recv.shape, i32)],
+        (index, send_rows, grid_latent, edge_count.reshape(1, 1), recv),
         flops=2 * big,
         name="halo_rows",
     )
     from_low = lax.ppermute(to_high, "lon", ring(lon_count, 1))
     from_high = lax.ppermute(to_low, "lon", ring(lon_count, -1))
-    mesh_rows, own_mesh, live = call(
+    mesh_rows, own_mesh, node_gain_row = call(
         mesh_rows_kernel,
-        [((edges, width), bf16), ((own, width), bf16), (recv.shape, i32)],
-        (edge_count.reshape(1, 1), recv, mesh_latent),
+        [((edges, width), bf16), ((own, width), bf16), ((1, width), f32)],
+        (live, mesh_latent, node_gain.reshape(1, width)),
         flops=big,
         name="mesh_rows",
     )
@@ -352,7 +365,7 @@
     columns = lax.axis_size("z")
     piece = columns * own
 
-    def to_owners(value, extras=(), extra_outs=()):
+    def to_owners(value, extras=(), extra_outs=(), beside=None):
         (out,) = call(
             lambda *refs: half_sum_kernel(own, False, *refs), [((half, width), bf16)],
             (live, value), flops=big // 2, name="half_away",
@@ -374,18 +387,21 @@
             lax.ppermute(total, "y", ring(lanes, shift)) if shift else total
             for shift, total in zip(SHIFTS, sums)
         ]
+        done = ()
+        if beside is not None:
+            got[-1], *done = lax.optimization_barrier((got[-1], *beside()))
         (both,) = call(total_kernel, [((columns, own, width), bf16)], got, name="total")
         parts = lax.all_to_all(both, "z", 0, 0, tiled=True)
-        return (parts,) + tuple(here[1:])
+        return (parts,) + tuple(here[1:]) + tuple(done)
 
     parts, own_cot, gains = to_owners(
         normed,
-        (mesh_cotangent, node_gain.reshape(1, width), edge_gain.reshape(1, width)),
+        (mesh_cotangent, node_gain_row, edge_gain.reshape(1, width)),
         (((own, width), bf16), ((2, width), f32)),
     )
-    mesh_out, grad_copies, direct = call(
+    grad_copies, node_normed, d_pre = call(
         node_kernel,
-        [((own, width), bf16), ((owners, own, width), bf16), ((own, width), f32)],
+        [((owners, own, width), bf16), ((own, width), f32), ((own, width), bf16)],
         (parts, own_mesh, own_cot, node_first, node_second, gains),
         flops=2 * own * width * width * 7,
         name="node",
@@ -407,15 +423,29 @@
         flops=big // 2 + dense,
         name="edge_backward",
     )
-    back_low, back_own, back_high = call(
-        slot_sum_kernel, [((side, width), bf16)] * 3, (send, d_first, edge_first), flops=dense, name="slot_sum"
+    def other_work():
+        slots = call(
+            slot_sum_kernel, [((side, width), bf16)] * 3, (send, d_first, edge_first),
+            flops=dense, name="slot_sum",
+        )
+        grads = call(
+            edge_grad_kernel, [((edges, width), bf16)], (d_first, edge_first),
+            flops=dense, name="edge_grad",
+        )
+        late_normed, late_d_pre, _ = lax.optimization_barrier((node_normed, d_pre, d_first))
+        node_outs = call(
+            mesh_out_kernel,
+            [((own, width), bf16), ((own, width), f32)],
+            (own_mesh, own_cot, late_normed, late_d_pre, node_first, gains),
+            flops=2 * own * width * width, name="mesh_out",
+        )
+        return (*slots, *grads, *node_outs)
+
+    mesh_parts, back_low, back_own, back_high, edge_grad, mesh_out, direct = to_owners(
+        d_first, beside=other_work
     )
     got_low = lax.ppermute(back_high, "lon", ring(lon_count, 1))
     got_high = lax.ppermute(back_low, "lon", ring(lon_count, -1))
-    (mesh_parts,) = to_owners(d_first)
-    (edge_grad,) = call(
-        edge_grad_kernel, [((edges, width), bf16)], (d_first, edge_first), flops=dense, name="edge_grad"
-    )
     (grid_grad,) = call(
         grid_grad_kernel,
         [((grid_rows, width), bf16)],

time: 96.2 us -> 95.5 us (level)
  local copies, waits for them, and re-layouts: 3.07 us -> 2.09 us
    ppermute x6, waiting for transfers between devices: 10.9 us -> 8.23 us  [to_owners(): lax.ppermute(total, 'y', ring(lanes, shift))]
    all_to_all x1, waiting for transfers between devices: 1.19 us -> 2.63 us  [to_owners(): parts = lax.all_to_all(both, 'z', 0, 0, tiled=True)]
    ppermute x1, waiting for transfers between devices: 0.01 us -> 1.3 us  [shards(): got_low = lax.ppermute(back_high, 'lon', ring(lon_count, 1))]
    unnamed x28 -> x26, local copies, waits for them, and re-layouts: 3.07 us -> 2.09 us
    pallas_call x18 -> x20, Pallas kernels: 19.7 us -> 20 us  [call(): pl.pallas_call(kernel, out_shape=[jax.ShapeDtypeStruct(s, d) for s, d in...]
  transfers between devices with their start and end apart: 14 -> 14, of which waited for: 7 -> 7; matrix products, arithmetic and copies ran while one was open for 0% -> 0% of each run, Pallas kernels for 10% -> 11%
where the time goes in v5:
time: 95.5 us; the launch traced here: 95.1 us
  blocking collectives  32.7 us (34%)
  starting transfers between devices  26.3 us (28%)
  Pallas kernels  20 us (21%)
  waiting for transfers between devices  12.5 us (13%)
  local copies, waits for them, and re-layouts  2.09 us (2%)
  between operations  1.55 us (2%)
    pallas_call x20, Pallas kernels, call(): pl.pallas_call(kernel, out_shape=[jax.ShapeDtypeStruct(s, d) for s, d in...  20 us
    all_to_all x1, blocking collectives, shards(): lax.all_to_all(grad_copies, zy, 0, 0, tiled=True).reshape(half, width)  18.5 us
    all_to_all x1, blocking collectives, to_owners(): parts = lax.all_to_all(both, 'z', 0, 0, tiled=True)  14.1 us
    ppermute x6, starting transfers between devices, to_owners(): lax.ppermute(total, 'y', ring(lanes, shift))  8.52 us
    ppermute x6, waiting for transfers between devices, to_owners(): lax.ppermute(total, 'y', ring(lanes, shift))  8.23 us
    ppermute x1, starting transfers between devices, shards(): far = lax.ppermute(near, 'core', swap)  4.55 us
    ppermute x2, starting transfers between devices, to_owners(): away = lax.ppermute(out, 'core', swap)  3.63 us
    all_to_all x1, starting transfers between devices, to_owners(): parts = lax.all_to_all(both, 'z', 0, 0, tiled=True)  3.37 us
  transfers between devices with their start and end apart: 14, of which 7 were waited for; matrix products, arithmetic and copies ran while one was open for 0% of the time, Pallas kernels for 11%

profile of v5, /device:TPU:1, one launch (start us, length us, event | category | flops | bytes accessed | tf_op | source)
XLA Modules:
  0.0 95.1 jit_solution(14467179278552218813)
XLA Ops:
  2.4 2.1 %collective-permute-start = (bf16[64,256]{1,0:T(8,128)(2,1)S(1)}, bf16[64,256]{1,0:T(8,128)(2,1)S(1)}, u32[]{:S(2)}, u32[]{:S(2)}) collective-permute-start(bf16[64,256]{1,0:T(8,128)(2,1)S(1)} %get-tuple-element.43), channel_id=1, source_target_pairs={{0,64},{64,128},{128,192},{192,0},{1,65},{65,129},{129,193},{193,1... | collective-permute-start | bytes 98312 | tf_op jit(solution)/shard_map/ppermute | solution.py:346
  4.5 1.4 %collective-permute-start.1 = (bf16[64,256]{1,0:T(8,128)(2,1)S(1)}, bf16[64,256]{1,0:T(8,128)(2,1)S(1)}, u32[]{:S(2)}, u32[]{:S(2)}) collective-permute-start(bf16[64,256]{1,0:T(8,128)(2,1)S(1)} %get-tuple-element.45), channel_id=1, source_target_pairs={{0,192},{64,0},{128,64},{192,128},{1,193},{65,1},{129,65},{193,129... | collective-permute-start | bytes 98312 | tf_op jit(solution)/shard_map/ppermute | solution.py:347
  6.6 2.5 %mesh_rows.1 = (bf16[2048,256]{1,0:T(8,128)(2,1)S(1)}, bf16[32,256]{1,0:T(8,128)(2,1)S(1)}, f32[1,256]{1,0:T(1,128)S(1)}) custom-call(s32[16,128]{1,0:T(8,128)S(1)} %get-tuple-element.41.live_ref.refs_0_, bf16[2048,256]{1,0:T(8,128)(2,1)S(1)} %copy-done.5, f32[1,256]{1,0:T(1,128)S(1)} %bitcast.12), custom_call_target="tpu_custom_call" | custom-call | flops 2147483648 | tf_op jit(solution)/shard_map/mesh_rows/pallas_call | solution.py:47
  9.1 2.2 %edge_forward.1 = (bf16[2048,256]{1,0:T(8,128)(2,1)S(1)}, bf16[2048,256]{1,0:T(8,128)(2,1)S(1)}) custom-call(s32[16,128]{1,0:T(8,128)S(1)} %bitcast.9, bf16[2048,256]{1,0:T(8,128)(2,1)S(1)} %copy-done.6, bf16[2048,256]{1,0:T(8,128)(2,1)S(1)} %get-tuple-element.42.mesh_rows_ref, bf16[64,256]{1,0:T(8,128)(2,1)S(1)} %collective-permute-done.low_ref, ...), custom_call_target="tpu_custom_call" | custom-call | flops 1342177280 | tf_op jit(solution)/shard_map/edge_forward/pallas_call | solution.py:47
  11.3 1.2 %half_away.2 = bf16[1024,256]{1,0:T(8,128)(2,1)S(1)} custom-call(s32[16,128]{1,0:T(8,128)S(1)} %get-tuple-element.41.live_ref.refs_0_, bf16[2048,256]{1,0:T(8,128)(2,1)S(1)} %get-tuple-element.46.refs_1_.refs_3_), custom_call_target="tpu_custom_call" | custom-call | flops 1073741824 | tf_op jit(solution)/shard_map/half_away/pallas_call | solution.py:47
  12.6 3.2 %collective-permute-start.2 = (bf16[1024,256]{1,0:T(8,128)(2,1)S(1)}, bf16[1024,256]{1,0:T(8,128)(2,1)S(1)}, u32[]{:S(2)}, u32[]{:S(2)}) collective-permute-start(bf16[1024,256]{1,0:T(8,128)(2,1)S(1)} %half_away.2), channel_id=1, source_target_pairs={{0,1},{1,0},{2,3},{3,2},{4,5},{5,4},{6,7},{7,6},{8,9},{9,8},{10,11... | collective-permute-start | bytes 1572872 | tf_op jit(solution)/shard_map/ppermute | solution.py:373
  17.8 1.3 %collective-permute-start.3 = (bf16[256,256]{1,0:T(8,128)(2,1)S(1)}, bf16[256,256]{1,0:T(8,128)(2,1)S(1)}, u32[]{:S(2)}, u32[]{:S(2)}) collective-permute-start(bf16[256,256]{1,0:T(8,128)(2,1)S(1)} %get-tuple-element.49), channel_id=1, source_target_pairs={{0,4},{2,6},{4,0},{6,2},{1,5},{3,7},{5,1},{7,3},{8,12},{10,14},{12... | collective-permute-start | bytes 393224 | tf_op jit(solution)/shard_map/ppermute | solution.py:387
  19.5 2.3 %collective-permute-start.5 = (bf16[256,256]{1,0:T(8,128)(2,1)S(1)}, bf16[256,256]{1,0:T(8,128)(2,1)S(1)}, u32[]{:S(2)}, u32[]{:S(2)}) collective-permute-start(bf16[256,256]{1,0:T(8,128)(2,1)S(1)} %get-tuple-element.51), channel_id=1, source_target_pairs={{0,6},{2,0},{4,2},{6,4},{1,7},{3,1},{5,3},{7,5},{8,14},{10,8},{12,... | collective-permute-start | bytes 393224 | tf_op jit(solution)/shard_map/ppermute | solution.py:387
  21.8 2.8 %collective-permute-done.3.a_ref = bf16[256,256]{1,0:T(8,128)(2,1)S(1)} collective-permute-done((bf16[256,256]{1,0:T(8,128)(2,1)S(1)}, bf16[256,256]{1,0:T(8,128)(2,1)S(1)}, u32[]{:S(2)}, u32[]{:S(2)}) %collective-permute-start.3) | collective-permute-done | bytes 131104 | tf_op jit(solution)/shard_map/ppermute | solution.py:387
  24.5 3.1 %collective-permute-done.4.b_ref = bf16[256,256]{1,0:T(8,128)(2,1)S(1)} collective-permute-done((bf16[256,256]{1,0:T(8,128)(2,1)S(1)}, bf16[256,256]{1,0:T(8,128)(2,1)S(1)}, u32[]{:S(2)}, u32[]{:S(2)}) %collective-permute-start.4) | collective-permute-done | bytes 131104 | tf_op jit(solution)/shard_map/ppermute | solution.py:387
  27.7 14.1 %all_to_all.15.parts_ref = bf16[8,32,256]{2,1,0:T(8,128)(2,1)S(1)} all-to-all(bf16[8,32,256]{2,1,0:T(8,128)(2,1)S(1)} %total.2), channel_id=1, replica_groups=mesh['lon'=4,'z'=8,'y'=4,'core'=2] {'z'}, dimensions={0} | all-to-all | bytes 262144 | tf_op jit(solution)/shard_map/all_to_all | solution.py:394
  42.7 18.5 %all_to_all.16 = bf16[32,32,256]{2,1,0:T(8,128)(2,1)S(1)} all-to-all(bf16[32,32,256]{2,1,0:T(8,128)(2,1)S(1)} %get-tuple-element.56), channel_id=1, replica_groups=mesh['lon'=4,'z'=8,'y'=4,'core'=2] {'z','y'}, dimensions={0} | all-to-all | bytes 1048576 | tf_op jit(solution)/shard_map/all_to_all | solution.py:409
  61.2 4.6 %collective-permute-start.6 = (bf16[1024,256]{1,0:T(8,128)(2,1)S(1)}, bf16[1024,256]{1,0:T(8,128)(2,1)S(1)}, u32[]{:S(2)}, u32[]{:S(2)}) collective-permute-start(bf16[1024,256]{1,0:T(8,128)(2,1)S(1)} %bitcast.7), channel_id=1, source_target_pairs={{0,1},{1,0},{2,3},{3,2},{4,5},{5,4},{6,7},{7,6},{8,9},{9,8},{10,11... | collective-permute-start | bytes 1572872 | tf_op jit(solution)/shard_map/ppermute | solution.py:410
  65.8 1.4 %near_rows.1.refs_1_ = bf16[2048,256]{1,0:T(8,128)(2,1)S(1)} custom-call(s32[16,128]{1,0:T(8,128)S(1)} %get-tuple-element.41.live_ref.refs_0_, bf16[1024,256]{1,0:T(8,128)(2,1)S(1)} %bitcast.8), custom_call_target="tpu_custom_call" | custom-call | flops 1073741824 | tf_op jit(solution)/shard_map/near_rows/pallas_call | solution.py:47
  67.3 2.2 %edge_backward.1.refs_1_.d_first_ref = bf16[2048,256]{1,0:T(8,128)(2,1)S(1)} custom-call(s32[16,128]{1,0:T(8,128)S(1)} %get-tuple-element.41.live_ref.refs_0_, bf16[2048,256]{1,0:T(8,128)(2,1)S(1)} %near_rows.1.refs_1_, bf16[1024,256]{1,0:T(8,128)(2,1)S(1)} %collective-permute-done.6.refs_2_, bf16[2048,256]{1,0:T(8,128)(2,1)S(1)} %get-tuple-element.46.refs_1_.refs_3_, ...), custom_call_target="tpu_custom_call" | custom-call | flops 1342177280 | tf_op jit(solution)/shard_map/edge_backward/pallas_call | solution.py:47
  69.6 1.2 %half_away.3 = bf16[1024,256]{1,0:T(8,128)(2,1)S(1)} custom-call(s32[16,128]{1,0:T(8,128)S(1)} %get-tuple-element.41.live_ref.refs_0_, bf16[2048,256]{1,0:T(8,128)(2,1)S(1)} %edge_backward.1.refs_1_.d_first_ref), custom_call_target="tpu_custom_call" | custom-call | flops 1073741824 | tf_op jit(solution)/shard_map/half_away/pallas_call | solution.py:47
  72.9 1.9 %collective-permute-start.10 = (bf16[256,256]{1,0:T(8,128)(2,1)S(1)}, bf16[256,256]{1,0:T(8,128)(2,1)S(1)}, u32[]{:S(2)}, u32[]{:S(2)}) collective-permute-start(bf16[256,256]{1,0:T(8,128)(2,1)S(1)} %get-tuple-element.72), channel_id=1, source_target_pairs={{0,4},{2,6},{4,0},{6,2},{1,5},{3,7},{5,1},{7,3},{8,12},{10,14},{12... | collective-permute-start | bytes 393224 | tf_op jit(solution)/shard_map/ppermute | solution.py:387
  75.1 2.4 %collective-permute-start.12 = (bf16[256,256]{1,0:T(8,128)(2,1)S(1)}, bf16[256,256]{1,0:T(8,128)(2,1)S(1)}, u32[]{:S(2)}, u32[]{:S(2)}) collective-permute-start(bf16[256,256]{1,0:T(8,128)(2,1)S(1)} %get-tuple-element.74), channel_id=1, source_target_pairs={{0,6},{2,0},{4,2},{6,4},{1,7},{3,1},{5,3},{7,5},{8,14},{10,8},{12,... | collective-permute-start | bytes 393224 | tf_op jit(solution)/shard_map/ppermute | solution.py:387
  78.7 1.5 %edge_grad.1 = bf16[2048,256]{1,0:T(8,128)(2,1)} custom-call(bf16[2048,256]{1,0:T(8,128)(2,1)S(1)} %edge_backward.1.refs_1_.d_first_ref, bf16[768,256]{1,0:T(8,128)(2,1)S(1)} %copy-done), custom_call_target="tpu_custom_call" | custom-call | flops 268435456 | tf_op jit(solution)/shard_map/edge_grad/pallas_call | solution.py:47
  80.2 2.3 %collective-permute-done.11.b_ref = bf16[256,256]{1,0:T(8,128)(2,1)S(1)} collective-permute-done((bf16[256,256]{1,0:T(8,128)(2,1)S(1)}, bf16[256,256]{1,0:T(8,128)(2,1)S(1)}, u32[]{:S(2)}, u32[]{:S(2)}) %collective-permute-start.11) | collective-permute-done | bytes 131104 | tf_op jit(solution)/shard_map/ppermute | solution.py:387
  83.2 3.4 %all-to-all-start.2 = ((bf16[8,32,256]{2,1,0:T(8,128)(2,1)}), bf16[8,32,256]{2,1,0:T(8,128)(2,1)S(1)}, u32[]{:S(2)}, u32[]{:S(2)}) async-start(bf16[8,32,256]{2,1,0:T(8,128)(2,1)} %total.3), calls=%async_computation.2 | async-start | bytes 262144 | tf_op jit(solution)/shard_map/all_to_all | solution.py:394
  86.9 2.5 %collective-permute-start.9 = (bf16[64,256]{1,0:T(8,128)(2,1)S(1)}, bf16[64,256]{1,0:T(8,128)(2,1)S(1)}, u32[]{:S(2)}, u32[]{:S(2)}) collective-permute-start(bf16[64,256]{1,0:T(8,128)(2,1)S(1)} %get-tuple-element.71), channel_id=1, source_target_pairs={{0,192},{64,0},{128,64},{192,128},{1,193},{65,1},{129,65},{193,129... | collective-permute-start | bytes 98312 | tf_op jit(solution)/shard_map/ppermute | solution.py:448
  89.4 1.3 %collective-permute-done.8.low_ref = bf16[64,256]{1,0:T(8,128)(2,1)S(1)} collective-permute-done((bf16[64,256]{1,0:T(8,128)(2,1)S(1)}, bf16[64,256]{1,0:T(8,128)(2,1)S(1)}, u32[]{:S(2)}, u32[]{:S(2)}) %collective-permute-start.8) | collective-permute-done | bytes 32800 | tf_op jit(solution)/shard_map/ppermute | solution.py:447
  91.7 2.6 %all-to-all-done.2.parts_ref = bf16[8,32,256]{2,1,0:T(8,128)(2,1)S(1)} async-done(((bf16[8,32,256]{2,1,0:T(8,128)(2,1)}), bf16[8,32,256]{2,1,0:T(8,128)(2,1)S(1)}, u32[]{:S(2)}, u32[]{:S(2)}) %all-to-all-start.2) | async-done | bytes 131104 | tf_op jit(solution)/shard_map/all_to_all | solution.py:394
  (52 shorter events, 11.6 us)
Async XLA Ops:
  0.6 0.8 copy-start.10
  0.6 1.0 %copy-start.8 = (bf16[768,256]{1,0:T(8,128)(2,1)S(1)}, bf16[768,256]{1,0:T(8,128)(2,1)}, u32[]{:S(2)}) copy-start(bf16[768,256]{1,0:T(8,128)(2,1)} %grid_ref.1) | copy-start | bytes 1179652
  2.1 3.8 %copy-start.5 = (bf16[2048,256]{1,0:T(8,128)(2,1)S(1)}, bf16[2048,256]{1,0:T(8,128)(2,1)}, u32[]{:S(2)}) copy-start(bf16[2048,256]{1,0:T(8,128)(2,1)} %mesh_ref.1) | copy-start | bytes 3145732
  2.4 6.7 %collective-permute-start = (bf16[64,256]{1,0:T(8,128)(2,1)S(1)}, bf16[64,256]{1,0:T(8,128)(2,1)S(1)}, u32[]{:S(2)}, u32[]{:S(2)}) collective-permute-start(bf16[64,256]{1,0:T(8,128)(2,1)S(1)} %get-tuple-element.43), channel_id=1, source_target_pairs={{0,64},{64,128},{128,192},{192,0},{1,65},{65,129},{129,193},{193,1... | collective-permute-start | bytes 98312 | tf_op jit(solution)/shard_map/ppermute | solution.py:346
  4.5 4.6 %collective-permute-start.1 = (bf16[64,256]{1,0:T(8,128)(2,1)S(1)}, bf16[64,256]{1,0:T(8,128)(2,1)S(1)}, u32[]{:S(2)}, u32[]{:S(2)}) collective-permute-start(bf16[64,256]{1,0:T(8,128)(2,1)S(1)} %get-tuple-element.45), channel_id=1, source_target_pairs={{0,192},{64,0},{128,64},{192,128},{1,193},{65,1},{129,65},{193,129... | collective-permute-start | bytes 98312 | tf_op jit(solution)/shard_map/ppermute | solution.py:347
  6.6 2.5 %copy-start = (bf16[768,256]{1,0:T(8,128)(2,1)S(1)}, bf16[768,256]{1,0:T(8,128)(2,1)}, u32[]{:S(2)}) copy-start(bf16[768,256]{1,0:T(8,128)(2,1)} %first_ref.11) | copy-start | bytes 1179652
  6.6 2.5 %copy-start.3 = (s32[2048]{0:T(1024)S(1)}, s32[2048]{0:T(1024)}, u32[]{:S(2)}) copy-start(s32[2048]{0:T(1024)} %param.18) | copy-start | bytes 24580
  6.6 2.5 %copy-start.6 = (bf16[2048,256]{1,0:T(8,128)(2,1)S(1)}, bf16[2048,256]{1,0:T(8,128)(2,1)}, u32[]{:S(2)}) copy-start(bf16[2048,256]{1,0:T(8,128)(2,1)} %edge_ref.1) | copy-start | bytes 3145732
  6.6 2.5 %copy-start.9 = (bf16[256,256]{1,0:T(8,128)(2,1)S(1)}, bf16[256,256]{1,0:T(8,128)(2,1)}, u32[]{:S(2)}) copy-start(bf16[256,256]{1,0:T(8,128)(2,1)} %refs_5_.1) | copy-start | bytes 393220
  11.3 4.4 %copy-start.7 = (bf16[2048,256]{1,0:T(8,128)(2,1)S(1)}, bf16[2048,256]{1,0:T(8,128)(2,1)}, u32[]{:S(2)}) copy-start(bf16[2048,256]{1,0:T(8,128)(2,1)} %refs_2_.1) | copy-start | bytes 3145732
  12.6 5.1 %collective-permute-start.2 = (bf16[1024,256]{1,0:T(8,128)(2,1)S(1)}, bf16[1024,256]{1,0:T(8,128)(2,1)S(1)}, u32[]{:S(2)}, u32[]{:S(2)}) collective-permute-start(bf16[1024,256]{1,0:T(8,128)(2,1)S(1)} %half_away.2), channel_id=1, source_target_pairs={{0,1},{1,0},{2,3},{3,2},{4,5},{5,4},{6,7},{7,6},{8,9},{9,8},{10,11... | collective-permute-start | bytes 1572872 | tf_op jit(solution)/shard_map/ppermute | solution.py:373
  17.8 6.7 %collective-permute-start.3 = (bf16[256,256]{1,0:T(8,128)(2,1)S(1)}, bf16[256,256]{1,0:T(8,128)(2,1)S(1)}, u32[]{:S(2)}, u32[]{:S(2)}) collective-permute-start(bf16[256,256]{1,0:T(8,128)(2,1)S(1)} %get-tuple-element.49), channel_id=1, source_target_pairs={{0,4},{2,6},{4,0},{6,2},{1,5},{3,7},{5,1},{7,3},{8,12},{10,14},{12... | collective-permute-start | bytes 393224 | tf_op jit(solution)/shard_map/ppermute | solution.py:387
  19.1 8.6 %collective-permute-start.4 = (bf16[256,256]{1,0:T(8,128)(2,1)S(1)}, bf16[256,256]{1,0:T(8,128)(2,1)S(1)}, u32[]{:S(2)}, u32[]{:S(2)}) collective-permute-start(bf16[256,256]{1,0:T(8,128)(2,1)S(1)} %get-tuple-element.50), channel_id=1, source_target_pairs={{0,2},{2,4},{4,6},{6,0},{1,3},{3,5},{5,7},{7,1},{8,10},{10,12},{12... | collective-permute-start | bytes 393224 | tf_op jit(solution)/shard_map/ppermute | solution.py:387
  19.5 8.2 %collective-permute-start.5 = (bf16[256,256]{1,0:T(8,128)(2,1)S(1)}, bf16[256,256]{1,0:T(8,128)(2,1)S(1)}, u32[]{:S(2)}, u32[]{:S(2)}) collective-permute-start(bf16[256,256]{1,0:T(8,128)(2,1)S(1)} %get-tuple-element.51), channel_id=1, source_target_pairs={{0,6},{2,0},{4,2},{6,4},{1,7},{3,1},{5,3},{7,5},{8,14},{10,8},{12,... | collective-permute-start | bytes 393224 | tf_op jit(solution)/shard_map/ppermute | solution.py:387
  27.7 14.2 %copy-start.2 = (bf16[256,256]{1,0:T(8,128)(2,1)S(1)}, bf16[256,256]{1,0:T(8,128)(2,1)}, u32[]{:S(2)}) copy-start(bf16[256,256]{1,0:T(8,128)(2,1)} %second_ref.3) | copy-start | bytes 393220
  27.7 14.2 %copy-start.1 = (bf16[512,256]{1,0:T(8,128)(2,1)S(1)}, bf16[512,256]{1,0:T(8,128)(2,1)}, u32[]{:S(2)}) copy-start(bf16[512,256]{1,0:T(8,128)(2,1)} %first_ref.10) | copy-start | bytes 786436
  61.2 6.1 %collective-permute-start.6 = (bf16[1024,256]{1,0:T(8,128)(2,1)S(1)}, bf16[1024,256]{1,0:T(8,128)(2,1)S(1)}, u32[]{:S(2)}, u32[]{:S(2)}) collective-permute-start(bf16[1024,256]{1,0:T(8,128)(2,1)S(1)} %bitcast.7), channel_id=1, source_target_pairs={{0,1},{1,0},{2,3},{3,2},{4,5},{5,4},{6,7},{7,6},{8,9},{9,8},{10,11... | collective-permute-start | bytes 1572872 | tf_op jit(solution)/shard_map/ppermute | solution.py:410
  70.8 2.0 %collective-permute-start.7 = (bf16[1024,256]{1,0:T(8,128)(2,1)S(1)}, bf16[1024,256]{1,0:T(8,128)(2,1)S(1)}, u32[]{:S(2)}, u32[]{:S(2)}) collective-permute-start(bf16[1024,256]{1,0:T(8,128)(2,1)S(1)} %half_away.3), channel_id=1, source_target_pairs={{0,1},{1,0},{2,3},{3,2},{4,5},{5,4},{6,7},{7,6},{8,9},{9,8},{10,11... | collective-permute-start | bytes 1572872 | tf_op jit(solution)/shard_map/ppermute | solution.py:373
  72.9 7.3 %collective-permute-start.10 = (bf16[256,256]{1,0:T(8,128)(2,1)S(1)}, bf16[256,256]{1,0:T(8,128)(2,1)S(1)}, u32[]{:S(2)}, u32[]{:S(2)}) collective-permute-start(bf16[256,256]{1,0:T(8,128)(2,1)S(1)} %get-tuple-element.72), channel_id=1, source_target_pairs={{0,4},{2,6},{4,0},{6,2},{1,5},{3,7},{5,1},{7,3},{8,12},{10,14},{12... | collective-permute-start | bytes 393224 | tf_op jit(solution)/shard_map/ppermute | solution.py:387
  74.8 7.7 %collective-permute-start.11 = (bf16[256,256]{1,0:T(8,128)(2,1)S(1)}, bf16[256,256]{1,0:T(8,128)(2,1)S(1)}, u32[]{:S(2)}, u32[]{:S(2)}) collective-permute-start(bf16[256,256]{1,0:T(8,128)(2,1)S(1)} %get-tuple-element.73), channel_id=1, source_target_pairs={{0,2},{2,4},{4,6},{6,0},{1,3},{3,5},{5,7},{7,1},{8,10},{10,12},{12... | collective-permute-start | bytes 393224 | tf_op jit(solution)/shard_map/ppermute | solution.py:387
  75.1 7.4 %collective-permute-start.12 = (bf16[256,256]{1,0:T(8,128)(2,1)S(1)}, bf16[256,256]{1,0:T(8,128)(2,1)S(1)}, u32[]{:S(2)}, u32[]{:S(2)}) collective-permute-start(bf16[256,256]{1,0:T(8,128)(2,1)S(1)} %get-tuple-element.74), channel_id=1, source_target_pairs={{0,6},{2,0},{4,2},{6,4},{1,7},{3,1},{5,3},{7,5},{8,14},{10,8},{12,... | collective-permute-start | bytes 393224 | tf_op jit(solution)/shard_map/ppermute | solution.py:387
  83.2 11.1 %all-to-all-start.2 = ((bf16[8,32,256]{2,1,0:T(8,128)(2,1)}), bf16[8,32,256]{2,1,0:T(8,128)(2,1)S(1)}, u32[]{:S(2)}, u32[]{:S(2)}) async-start(bf16[8,32,256]{2,1,0:T(8,128)(2,1)} %total.3), calls=%async_computation.2 | async-start | bytes 262144 | tf_op jit(solution)/shard_map/all_to_all | solution.py:394
  86.6 4.1 %collective-permute-start.8 = (bf16[64,256]{1,0:T(8,128)(2,1)S(1)}, bf16[64,256]{1,0:T(8,128)(2,1)S(1)}, u32[]{:S(2)}, u32[]{:S(2)}) collective-permute-start(bf16[64,256]{1,0:T(8,128)(2,1)S(1)} %get-tuple-element.69), channel_id=1, source_target_pairs={{0,64},{64,128},{128,192},{192,0},{1,65},{65,129},{129,193},{193,1... | collective-permute-start | bytes 98312 | tf_op jit(solution)/shard_map/ppermute | solution.py:447
  86.9 3.8 %collective-permute-start.9 = (bf16[64,256]{1,0:T(8,128)(2,1)S(1)}, bf16[64,256]{1,0:T(8,128)(2,1)S(1)}, u32[]{:S(2)}, u32[]{:S(2)}) collective-permute-start(bf16[64,256]{1,0:T(8,128)(2,1)S(1)} %get-tuple-element.71), channel_id=1, source_target_pairs={{0,192},{64,0},{128,64},{192,128},{1,193},{65,1},{129,65},{193,129... | collective-permute-start | bytes 98312 | tf_op jit(solution)/shard_map/ppermute | solution.py:448
  (3 other events, 2.1 us)

commit v6 on v5

--- a/solution.py
+++ b/solution.py
@@ -83,8 +83,11 @@
 
 
 def halo_rows_kernel(
-    index_ref, list_ref, grid_ref, count_ref, recv_ref, low_ref, own_ref, high_ref, live_ref
-):
+    index_ref, list_ref, grid_ref, count_ref, recv_ref, node_gain_ref, edge_gain_ref,
+    low_ref, own_ref, high_ref, live_ref, gains_ref,
+):
+    gains_ref[0:1, :] = node_gain_ref[...]
+    gains_ref[1:2, :] = edge_gain_ref[...]
     rows = dot_tn(one_hot(index_ref[...] == list_ref[...]), grid_ref[...]).astype(bf16)
     side = rows.shape[0] // 3
     low_ref[...] = rows[0:side]
@@ -93,8 +96,7 @@
     live_ref[...] = live_rows(recv_ref, count_ref[...])
 
 
-def mesh_rows_kernel(live_ref, mesh_ref, gain_ref, out_ref, own_ref, gain_out_ref):
-    gain_out_ref[...] = gain_ref[...]
+def mesh_rows_kernel(live_ref, mesh_ref, out_ref, own_ref):
     own = own_ref.shape[0]
     own_ref[...] = mesh_ref[pl.ds(pl.multiple_of(my_block() * own, own), own), :]
     m = mesh_ref.shape[0]
@@ -151,7 +153,7 @@
     return total
 
 
-SHIFTS = (2, 1, 3, 0)
+SHIFTS = (1, 3, 2, 0)
 
 
 def half_sum_kernel(own, here, live_ref, value_ref, out_ref):
@@ -163,13 +165,9 @@
         out_ref[n * size : (n + 1) * size, :] = total.astype(out_ref.dtype)
 
 
-def half_first_kernel(
-    own, live_ref, value_ref, cot_ref, node_gain_ref, edge_gain_ref, out_ref, own_cot_ref, gains_ref
-):
+def half_first_kernel(own, live_ref, value_ref, cot_ref, out_ref, own_cot_ref):
     half_sum_kernel(own, True, live_ref, value_ref, out_ref)
     own_cot_ref[...] = cot_ref[pl.ds(pl.multiple_of(my_block() * own, own), own), :]
-    gains_ref[0:1, :] = node_gain_ref[...]
-    gains_ref[1:2, :] = edge_gain_ref[...]
 
 
 def pieces_kernel(here_ref, away_ref, *out_refs):
@@ -336,19 +334,22 @@
     (index,) = call(
         row_index_kernel, [((grid_rows, listed), i32)], (), flops=2 * big, name="row_index"
     )
-    to_low, stay, to_high, live = call(
+    to_low, stay, to_high, live, gains = call(
         halo_rows_kernel,
-        [((side, width), bf16)] * 3 + [(recv.shape, i32)],
-        (index, send_rows, grid_latent, edge_count.reshape(1, 1), recv),
+        [((side, width), bf16)] * 3 + [(recv.shape, i32), ((2, width), f32)],
+        (
+            index, send_rows, grid_latent, edge_count.reshape(1, 1), recv,
+            node_gain.reshape(1, width), edge_gain.reshape(1, width),
+        ),
         flops=2 * big,
         name="halo_rows",
     )
     from_low = lax.ppermute(to_high, "lon", ring(lon_count, 1))
     from_high = lax.ppermute(to_low, "lon", ring(lon_count, -1))
-    mesh_rows, own_mesh, node_gain_row = call(
+    mesh_rows, own_mesh = call(
         mesh_rows_kernel,
-        [((edges, width), bf16), ((own, width), bf16), ((1, width), f32)],
-        (live, mesh_latent, node_gain.reshape(1, width)),
+        [((edges, width), bf16), ((own, width), bf16)],
+        (live, mesh_latent),
         flops=big,
         name="mesh_rows",
     )
@@ -394,11 +395,7 @@
         parts = lax.all_to_all(both, "z", 0, 0, tiled=True)
         return (parts,) + tuple(here[1:]) + tuple(done)
 
-    parts, own_cot, gains = to_owners(
-        normed,
-        (mesh_cotangent, node_gain_row, edge_gain.reshape(1, width)),
-        (((own, width), bf16), ((2, width), f32)),
-    )
+    parts, own_cot = to_owners(normed, (mesh_cotangent,), (((own, width), bf16),))
     grad_copies, node_normed, d_pre = call(
         node_kernel,
         [((owners, own, width), bf16), ((own, width), f32), ((own, width), bf16)],

time: 95.5 us -> 94 us (0.984); the launches traced: 95.1 us -> 92.2 us
  starting transfers between devices: 26.3 us -> 24.3 us
  local copies, waits for them, and re-layouts: 2.09 us -> 0.75 us
    ppermute x6, starting transfers between devices: 8.52 us -> 6.03 us  [to_owners(): lax.ppermute(total, 'y', ring(lanes, shift))]
    all_to_all x1, blocking collectives: 14.1 us -> 16.4 us  [to_owners(): parts = lax.all_to_all(both, 'z', 0, 0, tiled=True)]
    all_to_all x1, blocking collectives: 18.5 us -> 17 us  [shards(): lax.all_to_all(grad_copies, zy, 0, 0, tiled=True).reshape(half, width)]
    unnamed x26, local copies, waits for them, and re-layouts: 2.09 us -> 0.75 us
  transfers between devices with their start and end apart: 14 -> 14, of which waited for: 7 -> 10; matrix products, arithmetic and copies ran while one was open for 0% -> 0% of each run, Pallas kernels for 11% -> 11%
where the time goes in v6:
time: 94 us; the launch traced here: 92.2 us
  blocking collectives  33.4 us (36%)
  starting transfers between devices  24.3 us (26%)
  Pallas kernels  20 us (21%)
  waiting for transfers between devices  12.3 us (13%)
  between operations  1.6 us (2%)
    pallas_call x20, Pallas kernels, call(): pl.pallas_call(kernel, out_shape=[jax.ShapeDtypeStruct(s, d) for s, d in...  20 us
    all_to_all x1, blocking collectives, shards(): lax.all_to_all(grad_copies, zy, 0, 0, tiled=True).reshape(half, width)  17 us
    all_to_all x1, blocking collectives, to_owners(): parts = lax.all_to_all(both, 'z', 0, 0, tiled=True)  16.4 us
    ppermute x6, waiting for transfers between devices, to_owners(): lax.ppermute(total, 'y', ring(lanes, shift))  7.41 us
    ppermute x6, starting transfers between devices, to_owners(): lax.ppermute(total, 'y', ring(lanes, shift))  6.03 us
    ppermute x1, starting transfers between devices, shards(): far = lax.ppermute(near, 'core', swap)  5.01 us
    ppermute x2, starting transfers between devices, to_owners(): away = lax.ppermute(out, 'core', swap)  3.63 us
    all_to_all x1, starting transfers between devices, to_owners(): parts = lax.all_to_all(both, 'z', 0, 0, tiled=True)  3.37 us
  transfers between devices with their start and end apart: 14, of which 10 were waited for; matrix products, arithmetic and copies ran while one was open for 0% of the time, Pallas kernels for 11%

profile of v6, /device:TPU:1, one launch (start us, length us, event | category | flops | bytes accessed | tf_op | source)
XLA Modules:
  0.0 92.2 jit_solution(4636355422204119550)
XLA Ops:
  2.5 2.1 %collective-permute-start = (bf16[64,256]{1,0:T(8,128)(2,1)S(1)}, bf16[64,256]{1,0:T(8,128)(2,1)S(1)}, u32[]{:S(2)}, u32[]{:S(2)}) collective-permute-start(bf16[64,256]{1,0:T(8,128)(2,1)S(1)} %get-tuple-element.42), channel_id=1, source_target_pairs={{0,64},{64,128},{128,192},{192,0},{1,65},{65,129},{129,193},{193,1... | collective-permute-start | bytes 98312 | tf_op jit(solution)/shard_map/ppermute | solution.py:347
  4.6 1.4 %collective-permute-start.1 = (bf16[64,256]{1,0:T(8,128)(2,1)S(1)}, bf16[64,256]{1,0:T(8,128)(2,1)S(1)}, u32[]{:S(2)}, u32[]{:S(2)}) collective-permute-start(bf16[64,256]{1,0:T(8,128)(2,1)S(1)} %get-tuple-element.44), channel_id=1, source_target_pairs={{0,192},{64,0},{128,64},{192,128},{1,193},{65,1},{129,65},{193,129... | collective-permute-start | bytes 98312 | tf_op jit(solution)/shard_map/ppermute | solution.py:348
  6.0 2.5 %mesh_rows.1 = (bf16[2048,256]{1,0:T(8,128)(2,1)S(1)}, bf16[32,256]{1,0:T(8,128)(2,1)S(1)}) custom-call(s32[16,128]{1,0:T(8,128)S(1)} %get-tuple-element.40.live_ref.refs_0_, bf16[2048,256]{1,0:T(8,128)(2,1)S(1)} %copy-done.5), custom_call_target="tpu_custom_call" | custom-call | flops 2147483648 | tf_op jit(solution)/shard_map/mesh_rows/pallas_call | solution.py:47
  8.5 2.2 %edge_forward.1 = (bf16[2048,256]{1,0:T(8,128)(2,1)S(1)}, bf16[2048,256]{1,0:T(8,128)(2,1)S(1)}) custom-call(s32[16,128]{1,0:T(8,128)S(1)} %bitcast.9, bf16[2048,256]{1,0:T(8,128)(2,1)S(1)} %copy-done.6, bf16[2048,256]{1,0:T(8,128)(2,1)S(1)} %get-tuple-element.41.mesh_rows_ref, bf16[64,256]{1,0:T(8,128)(2,1)S(1)} %collective-permute-done.low_ref, ...), custom_call_target="tpu_custom_call" | custom-call | flops 1342177280 | tf_op jit(solution)/shard_map/edge_forward/pallas_call | solution.py:47
  10.7 1.2 %half_away.2 = bf16[1024,256]{1,0:T(8,128)(2,1)S(1)} custom-call(s32[16,128]{1,0:T(8,128)S(1)} %get-tuple-element.40.live_ref.refs_0_, bf16[2048,256]{1,0:T(8,128)(2,1)S(1)} %get-tuple-element.45.refs_1_.refs_3_), custom_call_target="tpu_custom_call" | custom-call | flops 1073741824 | tf_op jit(solution)/shard_map/half_away/pallas_call | solution.py:47
  12.0 3.2 %collective-permute-start.2 = (bf16[1024,256]{1,0:T(8,128)(2,1)S(1)}, bf16[1024,256]{1,0:T(8,128)(2,1)S(1)}, u32[]{:S(2)}, u32[]{:S(2)}) collective-permute-start(bf16[1024,256]{1,0:T(8,128)(2,1)S(1)} %half_away.2), channel_id=1, source_target_pairs={{0,1},{1,0},{2,3},{3,2},{4,5},{5,4},{6,7},{7,6},{8,9},{9,8},{10,11... | collective-permute-start | bytes 1572872 | tf_op jit(solution)/shard_map/ppermute | solution.py:374
  15.2 1.2 %half_here.2 = (f32[1024,256]{1,0:T(8,128)S(1)}, bf16[32,256]{1,0:T(8,128)(2,1)S(1)}) custom-call(s32[16,128]{1,0:T(8,128)S(1)} %get-tuple-element.40.live_ref.refs_0_, bf16[2048,256]{1,0:T(8,128)(2,1)S(1)} %get-tuple-element.45.refs_1_.refs_3_, bf16[2048,256]{1,0:T(8,128)(2,1)S(1)} %copy-done.7), custom_call_target="tpu_custom_call" | custom-call | flops 1073741824 | tf_op jit(solution)/shard_map/half_here/pallas_call | solution.py:47
  16.9 2.7 %collective-permute-start.4 = (bf16[256,256]{1,0:T(8,128)(2,1)S(1)}, bf16[256,256]{1,0:T(8,128)(2,1)S(1)}, u32[]{:S(2)}, u32[]{:S(2)}) collective-permute-start(bf16[256,256]{1,0:T(8,128)(2,1)S(1)} %get-tuple-element.48), channel_id=1, source_target_pairs={{0,6},{2,0},{4,2},{6,4},{1,7},{3,1},{5,3},{7,5},{8,14},{10,8},{12,... | collective-permute-start | bytes 393224 | tf_op jit(solution)/shard_map/ppermute | solution.py:388
  19.6 3.2 %collective-permute-done.3.a_ref = bf16[256,256]{1,0:T(8,128)(2,1)S(1)} collective-permute-done((bf16[256,256]{1,0:T(8,128)(2,1)S(1)}, bf16[256,256]{1,0:T(8,128)(2,1)S(1)}, u32[]{:S(2)}, u32[]{:S(2)}) %collective-permute-start.3) | collective-permute-done | bytes 131104 | tf_op jit(solution)/shard_map/ppermute | solution.py:388
  22.8 1.9 %collective-permute-done.4.b_ref = bf16[256,256]{1,0:T(8,128)(2,1)S(1)} collective-permute-done((bf16[256,256]{1,0:T(8,128)(2,1)S(1)}, bf16[256,256]{1,0:T(8,128)(2,1)S(1)}, u32[]{:S(2)}, u32[]{:S(2)}) %collective-permute-start.4) | collective-permute-done | bytes 131104 | tf_op jit(solution)/shard_map/ppermute | solution.py:388
  25.0 16.4 %all_to_all.15.parts_ref = bf16[8,32,256]{2,1,0:T(8,128)(2,1)S(1)} all-to-all(bf16[8,32,256]{2,1,0:T(8,128)(2,1)S(1)} %total.2), channel_id=1, replica_groups=mesh['lon'=4,'z'=8,'y'=4,'core'=2] {'z'}, dimensions={0} | all-to-all | bytes 262144 | tf_op jit(solution)/shard_map/all_to_all | solution.py:395
  42.2 17.0 %all_to_all.16 = bf16[32,32,256]{2,1,0:T(8,128)(2,1)S(1)} all-to-all(bf16[32,32,256]{2,1,0:T(8,128)(2,1)S(1)} %get-tuple-element.54), channel_id=1, replica_groups=mesh['lon'=4,'z'=8,'y'=4,'core'=2] {'z','y'}, dimensions={0} | all-to-all | bytes 1048576 | tf_op jit(solution)/shard_map/all_to_all | solution.py:406
  59.2 5.0 %collective-permute-start.6 = (bf16[1024,256]{1,0:T(8,128)(2,1)S(1)}, bf16[1024,256]{1,0:T(8,128)(2,1)S(1)}, u32[]{:S(2)}, u32[]{:S(2)}) collective-permute-start(bf16[1024,256]{1,0:T(8,128)(2,1)S(1)} %bitcast.7), channel_id=1, source_target_pairs={{0,1},{1,0},{2,3},{3,2},{4,5},{5,4},{6,7},{7,6},{8,9},{9,8},{10,11... | collective-permute-start | bytes 1572872 | tf_op jit(solution)/shard_map/ppermute | solution.py:407
  64.2 1.4 %near_rows.1.refs_1_ = bf16[2048,256]{1,0:T(8,128)(2,1)S(1)} custom-call(s32[16,128]{1,0:T(8,128)S(1)} %get-tuple-element.40.live_ref.refs_0_, bf16[1024,256]{1,0:T(8,128)(2,1)S(1)} %bitcast.8), custom_call_target="tpu_custom_call" | custom-call | flops 1073741824 | tf_op jit(solution)/shard_map/near_rows/pallas_call | solution.py:47
  65.8 2.2 %edge_backward.1.refs_1_.d_first_ref = bf16[2048,256]{1,0:T(8,128)(2,1)S(1)} custom-call(s32[16,128]{1,0:T(8,128)S(1)} %get-tuple-element.40.live_ref.refs_0_, bf16[2048,256]{1,0:T(8,128)(2,1)S(1)} %near_rows.1.refs_1_, bf16[1024,256]{1,0:T(8,128)(2,1)S(1)} %collective-permute-done.6.refs_2_, bf16[2048,256]{1,0:T(8,128)(2,1)S(1)} %get-tuple-element.45.refs_1_.refs_3_, ...), custom_call_target="tpu_custom_call" | custom-call | flops 1342177280 | tf_op jit(solution)/shard_map/edge_backward/pallas_call | solution.py:47
  68.0 1.2 %half_away.3 = bf16[1024,256]{1,0:T(8,128)(2,1)S(1)} custom-call(s32[16,128]{1,0:T(8,128)S(1)} %get-tuple-element.40.live_ref.refs_0_, bf16[2048,256]{1,0:T(8,128)(2,1)S(1)} %edge_backward.1.refs_1_.d_first_ref), custom_call_target="tpu_custom_call" | custom-call | flops 1073741824 | tf_op jit(solution)/shard_map/half_away/pallas_call | solution.py:47
  69.7 1.2 %half_here.3.here_ref = f32[1024,256]{1,0:T(8,128)S(1)} custom-call(s32[16,128]{1,0:T(8,128)S(1)} %get-tuple-element.40.live_ref.refs_0_, bf16[2048,256]{1,0:T(8,128)(2,1)S(1)} %edge_backward.1.refs_1_.d_first_ref), custom_call_target="tpu_custom_call" | custom-call | flops 1073741824 | tf_op jit(solution)/shard_map/half_here/pallas_call | solution.py:47
  71.6 2.5 %collective-permute-start.11 = (bf16[256,256]{1,0:T(8,128)(2,1)S(1)}, bf16[256,256]{1,0:T(8,128)(2,1)S(1)}, u32[]{:S(2)}, u32[]{:S(2)}) collective-permute-start(bf16[256,256]{1,0:T(8,128)(2,1)S(1)} %get-tuple-element.71), channel_id=1, source_target_pairs={{0,6},{2,0},{4,2},{6,4},{1,7},{3,1},{5,3},{7,5},{8,14},{10,8},{12,... | collective-permute-start | bytes 393224 | tf_op jit(solution)/shard_map/ppermute | solution.py:388
  75.9 1.5 %edge_grad.1 = bf16[2048,256]{1,0:T(8,128)(2,1)} custom-call(bf16[2048,256]{1,0:T(8,128)(2,1)S(1)} %edge_backward.1.refs_1_.d_first_ref, bf16[768,256]{1,0:T(8,128)(2,1)S(1)} %copy-done), custom_call_target="tpu_custom_call" | custom-call | flops 268435456 | tf_op jit(solution)/shard_map/edge_grad/pallas_call | solution.py:47
  77.3 1.9 %collective-permute-done.11.b_ref = bf16[256,256]{1,0:T(8,128)(2,1)S(1)} collective-permute-done((bf16[256,256]{1,0:T(8,128)(2,1)S(1)}, bf16[256,256]{1,0:T(8,128)(2,1)S(1)}, u32[]{:S(2)}, u32[]{:S(2)}) %collective-permute-start.11) | collective-permute-done | bytes 131104 | tf_op jit(solution)/shard_map/ppermute | solution.py:388
  80.1 3.4 %all-to-all-start.2 = ((bf16[8,32,256]{2,1,0:T(8,128)(2,1)}), bf16[8,32,256]{2,1,0:T(8,128)(2,1)S(1)}, u32[]{:S(2)}, u32[]{:S(2)}) async-start(bf16[8,32,256]{2,1,0:T(8,128)(2,1)} %total.3), calls=%async_computation.2 | async-start | bytes 262144 | tf_op jit(solution)/shard_map/all_to_all | solution.py:395
  84.4 1.9 %collective-permute-start.9 = (bf16[64,256]{1,0:T(8,128)(2,1)S(1)}, bf16[64,256]{1,0:T(8,128)(2,1)S(1)}, u32[]{:S(2)}, u32[]{:S(2)}) collective-permute-start(bf16[64,256]{1,0:T(8,128)(2,1)S(1)} %get-tuple-element.69), channel_id=1, source_target_pairs={{0,192},{64,0},{128,64},{192,128},{1,193},{65,1},{129,65},{193,129... | collective-permute-start | bytes 98312 | tf_op jit(solution)/shard_map/ppermute | solution.py:445
  86.3 1.3 %collective-permute-done.8.low_ref = bf16[64,256]{1,0:T(8,128)(2,1)S(1)} collective-permute-done((bf16[64,256]{1,0:T(8,128)(2,1)S(1)}, bf16[64,256]{1,0:T(8,128)(2,1)S(1)}, u32[]{:S(2)}, u32[]{:S(2)}) %collective-permute-start.8) | collective-permute-done | bytes 32800 | tf_op jit(solution)/shard_map/ppermute | solution.py:444
  88.6 2.9 %all-to-all-done.2.parts_ref = bf16[8,32,256]{2,1,0:T(8,128)(2,1)S(1)} async-done(((bf16[8,32,256]{2,1,0:T(8,128)(2,1)}), bf16[8,32,256]{2,1,0:T(8,128)(2,1)S(1)}, u32[]{:S(2)}, u32[]{:S(2)}) %all-to-all-start.2) | async-done | bytes 131104 | tf_op jit(solution)/shard_map/all_to_all | solution.py:395
  (52 shorter events, 9.3 us)
Async XLA Ops:
  0.6 1.0 %copy-start.8 = (bf16[768,256]{1,0:T(8,128)(2,1)S(1)}, bf16[768,256]{1,0:T(8,128)(2,1)}, u32[]{:S(2)}) copy-start(bf16[768,256]{1,0:T(8,128)(2,1)} %grid_ref.1) | copy-start | bytes 1179652
  0.6 1.0 %copy-start.11 = (f32[256]{0:T(256)S(1)}, f32[256]{0:T(256)}, u32[]{:S(2)}) copy-start(f32[256]{0:T(256)} %param.27) | copy-start | bytes 3076
  2.2 3.8 %copy-start.5 = (bf16[2048,256]{1,0:T(8,128)(2,1)S(1)}, bf16[2048,256]{1,0:T(8,128)(2,1)}, u32[]{:S(2)}) copy-start(bf16[2048,256]{1,0:T(8,128)(2,1)} %mesh_ref.1) | copy-start | bytes 3145732
  2.5 6.0 %collective-permute-start = (bf16[64,256]{1,0:T(8,128)(2,1)S(1)}, bf16[64,256]{1,0:T(8,128)(2,1)S(1)}, u32[]{:S(2)}, u32[]{:S(2)}) collective-permute-start(bf16[64,256]{1,0:T(8,128)(2,1)S(1)} %get-tuple-element.42), channel_id=1, source_target_pairs={{0,64},{64,128},{128,192},{192,0},{1,65},{65,129},{129,193},{193,1... | collective-permute-start | bytes 98312 | tf_op jit(solution)/shard_map/ppermute | solution.py:347
  4.6 3.9 %collective-permute-start.1 = (bf16[64,256]{1,0:T(8,128)(2,1)S(1)}, bf16[64,256]{1,0:T(8,128)(2,1)S(1)}, u32[]{:S(2)}, u32[]{:S(2)}) collective-permute-start(bf16[64,256]{1,0:T(8,128)(2,1)S(1)} %get-tuple-element.44), channel_id=1, source_target_pairs={{0,192},{64,0},{128,64},{192,128},{1,193},{65,1},{129,65},{193,129... | collective-permute-start | bytes 98312 | tf_op jit(solution)/shard_map/ppermute | solution.py:348
  5.9 2.5 %copy-start = (bf16[768,256]{1,0:T(8,128)(2,1)S(1)}, bf16[768,256]{1,0:T(8,128)(2,1)}, u32[]{:S(2)}) copy-start(bf16[768,256]{1,0:T(8,128)(2,1)} %first_ref.11) | copy-start | bytes 1179652
  5.9 2.5 %copy-start.3 = (s32[2048]{0:T(1024)S(1)}, s32[2048]{0:T(1024)}, u32[]{:S(2)}) copy-start(s32[2048]{0:T(1024)} %param.18) | copy-start | bytes 24580
  5.9 2.6 %copy-start.6 = (bf16[2048,256]{1,0:T(8,128)(2,1)S(1)}, bf16[2048,256]{1,0:T(8,128)(2,1)}, u32[]{:S(2)}) copy-start(bf16[2048,256]{1,0:T(8,128)(2,1)} %edge_ref.1) | copy-start | bytes 3145732
  6.0 2.6 %copy-start.9 = (bf16[256,256]{1,0:T(8,128)(2,1)S(1)}, bf16[256,256]{1,0:T(8,128)(2,1)}, u32[]{:S(2)}) copy-start(bf16[256,256]{1,0:T(8,128)(2,1)} %refs_5_.1) | copy-start | bytes 393220
  10.7 4.4 %copy-start.7 = (bf16[2048,256]{1,0:T(8,128)(2,1)S(1)}, bf16[2048,256]{1,0:T(8,128)(2,1)}, u32[]{:S(2)}) copy-start(bf16[2048,256]{1,0:T(8,128)(2,1)} %refs_2_.1) | copy-start | bytes 3145732
  12.0 4.7 %collective-permute-start.2 = (bf16[1024,256]{1,0:T(8,128)(2,1)S(1)}, bf16[1024,256]{1,0:T(8,128)(2,1)S(1)}, u32[]{:S(2)}, u32[]{:S(2)}) collective-permute-start(bf16[1024,256]{1,0:T(8,128)(2,1)S(1)} %half_away.2), channel_id=1, source_target_pairs={{0,1},{1,0},{2,3},{3,2},{4,5},{5,4},{6,7},{7,6},{8,9},{9,8},{10,11... | collective-permute-start | bytes 1572872 | tf_op jit(solution)/shard_map/ppermute | solution.py:374
  16.8 6.0 %collective-permute-start.3 = (bf16[256,256]{1,0:T(8,128)(2,1)S(1)}, bf16[256,256]{1,0:T(8,128)(2,1)S(1)}, u32[]{:S(2)}, u32[]{:S(2)}) collective-permute-start(bf16[256,256]{1,0:T(8,128)(2,1)S(1)} %get-tuple-element.47), channel_id=1, source_target_pairs={{0,2},{2,4},{4,6},{6,0},{1,3},{3,5},{5,7},{7,1},{8,10},{10,12},{12... | collective-permute-start | bytes 393224 | tf_op jit(solution)/shard_map/ppermute | solution.py:388
  16.9 7.8 %collective-permute-start.4 = (bf16[256,256]{1,0:T(8,128)(2,1)S(1)}, bf16[256,256]{1,0:T(8,128)(2,1)S(1)}, u32[]{:S(2)}, u32[]{:S(2)}) collective-permute-start(bf16[256,256]{1,0:T(8,128)(2,1)S(1)} %get-tuple-element.48), channel_id=1, source_target_pairs={{0,6},{2,0},{4,2},{6,4},{1,7},{3,1},{5,3},{7,5},{8,14},{10,8},{12,... | collective-permute-start | bytes 393224 | tf_op jit(solution)/shard_map/ppermute | solution.py:388
  19.6 5.3 %collective-permute-start.5 = (bf16[256,256]{1,0:T(8,128)(2,1)S(1)}, bf16[256,256]{1,0:T(8,128)(2,1)S(1)}, u32[]{:S(2)}, u32[]{:S(2)}) collective-permute-start(bf16[256,256]{1,0:T(8,128)(2,1)S(1)} %get-tuple-element.49), channel_id=1, source_target_pairs={{0,4},{2,6},{4,0},{6,2},{1,5},{3,7},{5,1},{7,3},{8,12},{10,14},{12... | collective-permute-start | bytes 393224 | tf_op jit(solution)/shard_map/ppermute | solution.py:388
  24.9 16.5 %copy-start.2 = (bf16[256,256]{1,0:T(8,128)(2,1)S(1)}, bf16[256,256]{1,0:T(8,128)(2,1)}, u32[]{:S(2)}) copy-start(bf16[256,256]{1,0:T(8,128)(2,1)} %second_ref.3) | copy-start | bytes 393220
  24.9 16.4 %copy-start.1 = (bf16[512,256]{1,0:T(8,128)(2,1)S(1)}, bf16[512,256]{1,0:T(8,128)(2,1)}, u32[]{:S(2)}) copy-start(bf16[512,256]{1,0:T(8,128)(2,1)} %first_ref.10) | copy-start | bytes 786436
  59.2 6.6 %collective-permute-start.6 = (bf16[1024,256]{1,0:T(8,128)(2,1)S(1)}, bf16[1024,256]{1,0:T(8,128)(2,1)S(1)}, u32[]{:S(2)}, u32[]{:S(2)}) collective-permute-start(bf16[1024,256]{1,0:T(8,128)(2,1)S(1)} %bitcast.7), channel_id=1, source_target_pairs={{0,1},{1,0},{2,3},{3,2},{4,5},{5,4},{6,7},{7,6},{8,9},{9,8},{10,11... | collective-permute-start | bytes 1572872 | tf_op jit(solution)/shard_map/ppermute | solution.py:407
  69.3 2.0 %collective-permute-start.7 = (bf16[1024,256]{1,0:T(8,128)(2,1)S(1)}, bf16[1024,256]{1,0:T(8,128)(2,1)S(1)}, u32[]{:S(2)}, u32[]{:S(2)}) collective-permute-start(bf16[1024,256]{1,0:T(8,128)(2,1)S(1)} %half_away.3), channel_id=1, source_target_pairs={{0,1},{1,0},{2,3},{3,2},{4,5},{5,4},{6,7},{7,6},{8,9},{9,8},{10,11... | collective-permute-start | bytes 1572872 | tf_op jit(solution)/shard_map/ppermute | solution.py:374
  71.3 6.0 %collective-permute-start.10 = (bf16[256,256]{1,0:T(8,128)(2,1)S(1)}, bf16[256,256]{1,0:T(8,128)(2,1)S(1)}, u32[]{:S(2)}, u32[]{:S(2)}) collective-permute-start(bf16[256,256]{1,0:T(8,128)(2,1)S(1)} %get-tuple-element.70), channel_id=1, source_target_pairs={{0,2},{2,4},{4,6},{6,0},{1,3},{3,5},{5,7},{7,1},{8,10},{10,12},{12... | collective-permute-start | bytes 393224 | tf_op jit(solution)/shard_map/ppermute | solution.py:388
  71.6 7.6 %collective-permute-start.11 = (bf16[256,256]{1,0:T(8,128)(2,1)S(1)}, bf16[256,256]{1,0:T(8,128)(2,1)S(1)}, u32[]{:S(2)}, u32[]{:S(2)}) collective-permute-start(bf16[256,256]{1,0:T(8,128)(2,1)S(1)} %get-tuple-element.71), channel_id=1, source_target_pairs={{0,6},{2,0},{4,2},{6,4},{1,7},{3,1},{5,3},{7,5},{8,14},{10,8},{12,... | collective-permute-start | bytes 393224 | tf_op jit(solution)/shard_map/ppermute | solution.py:388
  74.1 5.3 %collective-permute-start.12 = (bf16[256,256]{1,0:T(8,128)(2,1)S(1)}, bf16[256,256]{1,0:T(8,128)(2,1)S(1)}, u32[]{:S(2)}, u32[]{:S(2)}) collective-permute-start(bf16[256,256]{1,0:T(8,128)(2,1)S(1)} %get-tuple-element.72), channel_id=1, source_target_pairs={{0,4},{2,6},{4,0},{6,2},{1,5},{3,7},{5,1},{7,3},{8,12},{10,14},{12... | collective-permute-start | bytes 393224 | tf_op jit(solution)/shard_map/ppermute | solution.py:388
  80.1 11.3 %all-to-all-start.2 = ((bf16[8,32,256]{2,1,0:T(8,128)(2,1)}), bf16[8,32,256]{2,1,0:T(8,128)(2,1)S(1)}, u32[]{:S(2)}, u32[]{:S(2)}) async-start(bf16[8,32,256]{2,1,0:T(8,128)(2,1)} %total.3), calls=%async_computation.2 | async-start | bytes 262144 | tf_op jit(solution)/shard_map/all_to_all | solution.py:395
  83.5 4.1 %collective-permute-start.8 = (bf16[64,256]{1,0:T(8,128)(2,1)S(1)}, bf16[64,256]{1,0:T(8,128)(2,1)S(1)}, u32[]{:S(2)}, u32[]{:S(2)}) collective-permute-start(bf16[64,256]{1,0:T(8,128)(2,1)S(1)} %get-tuple-element.67), channel_id=1, source_target_pairs={{0,64},{64,128},{128,192},{192,0},{1,65},{65,129},{129,193},{193,1... | collective-permute-start | bytes 98312 | tf_op jit(solution)/shard_map/ppermute | solution.py:444
  84.4 3.2 %collective-permute-start.9 = (bf16[64,256]{1,0:T(8,128)(2,1)S(1)}, bf16[64,256]{1,0:T(8,128)(2,1)S(1)}, u32[]{:S(2)}, u32[]{:S(2)}) collective-permute-start(bf16[64,256]{1,0:T(8,128)(2,1)S(1)} %get-tuple-element.69), channel_id=1, source_target_pairs={{0,192},{64,0},{128,64},{192,128},{1,193},{65,1},{129,65},{193,129... | collective-permute-start | bytes 98312 | tf_op jit(solution)/shard_map/ppermute | solution.py:445
  (3 other events, 2.6 us)

commit v7 on v6

--- a/solution.py
+++ b/solution.py
@@ -211,7 +211,9 @@
     d_pre = dot_nt(d_post.astype(bf16), second_ref[...]) * (sigma * (1.0 + pre * (1.0 - sigma)))
     d_pre = d_pre.astype(bf16)
     grad = dot_nt(d_pre, first_ref[width : 2 * width, :]).astype(bf16)
-    grad_ref[...] = jnp.broadcast_to(grad[None], grad_ref.shape)
+    gained = grad.astype(f32) * gains_ref[1:2, :]
+    centered = (gained - jnp.mean(gained, axis=-1, keepdims=True)).astype(bf16)
+    grad_ref[...] = jnp.broadcast_to(centered[None], grad_ref.shape)
     d_pre_ref[...] = d_pre
 
 
@@ -239,7 +241,7 @@
 
 def edge_backward_kernel(
     own, live_ref, near_rows_ref, far_ref, normed_ref, slope_ref, second_ref,
-    gains_ref, out_ref, work_ref,
+    out_ref, work_ref,
 ):
     half = far_ref.shape[0]
     place = half_place(own, 1 - my_core(), live_ref[...])
@@ -247,15 +249,11 @@
     for start, at in chunks(out_ref.shape[0], LANES):
         hot = one_hot(lax.broadcasted_iota(i32, (LANES, half), 1) == column(cols, start, LANES))
         work_ref[at, :] = dot(hot, far_ref[...]) + near_rows_ref[at, :].astype(f32)
-    gain = gains_ref[1:2, :]
     for _, at in chunks(out_ref.shape[0], CHUNK):
-        scaled = work_ref[at, :] * gain
+        centered = work_ref[at, :]
         normed = normed_ref[at, :].astype(f32)
-        inner = (
-            scaled
-            - jnp.mean(scaled, axis=-1, keepdims=True)
-            - normed * jnp.mean(scaled * normed, axis=-1, keepdims=True)
-        ).astype(bf16)
+        inner = centered - normed * jnp.mean(centered * normed, axis=-1, keepdims=True)
+        inner = inner.astype(bf16)
         out_ref[at, :] = (dot_nt(inner, second_ref[...]) * slope_ref[at, :].astype(f32)).astype(bf16)
 
 
@@ -414,7 +412,6 @@
         [((edges, width), bf16)],
         (
             live, near_rows, far, normed, slope, edge_second,
-            gains,
         ),
         scratch=[vm((edges, width), f32)],
         flops=big // 2 + dense,

time: 94 us -> 94 us (level)
  no operation moved by 1% of the time
where the time goes in v7:
time: 94 us; the launch traced here: 92.2 us
  blocking collectives  33.4 us (36%)
  starting transfers between devices  24.3 us (26%)
  Pallas kernels  20 us (21%)
  waiting for transfers between devices  12.3 us (13%)
  between operations  1.6 us (2%)
    pallas_call x20, Pallas kernels, call(): pl.pallas_call(kernel, out_shape=[jax.ShapeDtypeStruct(s, d) for s, d in...  20 us
    all_to_all x1, blocking collectives, shards(): lax.all_to_all(grad_copies, zy, 0, 0, tiled=True).reshape(half, width)  17 us
    all_to_all x1, blocking collectives, to_owners(): parts = lax.all_to_all(both, 'z', 0, 0, tiled=True)  16.4 us
    ppermute x6, waiting for transfers between devices, to_owners(): lax.ppermute(total, 'y', ring(lanes, shift))  7.41 us
    ppermute x6, starting transfers between devices, to_owners(): lax.ppermute(total, 'y', ring(lanes, shift))  6.03 us
    ppermute x1, starting transfers between devices, shards(): far = lax.ppermute(near, 'core', swap)  5.01 us
    ppermute x2, starting transfers between devices, to_owners(): away = lax.ppermute(out, 'core', swap)  3.63 us
    all_to_all x1, starting transfers between devices, to_owners(): parts = lax.all_to_all(both, 'z', 0, 0, tiled=True)  3.37 us
  transfers between devices with their start and end apart: 14, of which 10 were waited for; matrix products, arithmetic and copies ran while one was open for 0% of the time, Pallas kernels for 11%

profile of v7, /device:TPU:1, one launch (start us, length us, event | category | flops | bytes accessed | tf_op | source)
XLA Modules:
  0.0 92.2 jit_solution(3460596759270040618)
XLA Ops:
  2.5 2.1 %collective-permute-start = (bf16[64,256]{1,0:T(8,128)(2,1)S(1)}, bf16[64,256]{1,0:T(8,128)(2,1)S(1)}, u32[]{:S(2)}, u32[]{:S(2)}) collective-permute-start(bf16[64,256]{1,0:T(8,128)(2,1)S(1)} %get-tuple-element.42), channel_id=1, source_target_pairs={{0,64},{64,128},{128,192},{192,0},{1,65},{65,129},{129,193},{193,1... | collective-permute-start | bytes 98312 | tf_op jit(solution)/shard_map/ppermute | solution.py:345
  4.6 1.4 %collective-permute-start.1 = (bf16[64,256]{1,0:T(8,128)(2,1)S(1)}, bf16[64,256]{1,0:T(8,128)(2,1)S(1)}, u32[]{:S(2)}, u32[]{:S(2)}) collective-permute-start(bf16[64,256]{1,0:T(8,128)(2,1)S(1)} %get-tuple-element.44), channel_id=1, source_target_pairs={{0,192},{64,0},{128,64},{192,128},{1,193},{65,1},{129,65},{193,129... | collective-permute-start | bytes 98312 | tf_op jit(solution)/shard_map/ppermute | solution.py:346
  6.0 2.5 %mesh_rows.1 = (bf16[2048,256]{1,0:T(8,128)(2,1)S(1)}, bf16[32,256]{1,0:T(8,128)(2,1)S(1)}) custom-call(s32[16,128]{1,0:T(8,128)S(1)} %get-tuple-element.40.live_ref.refs_0_, bf16[2048,256]{1,0:T(8,128)(2,1)S(1)} %copy-done.5), custom_call_target="tpu_custom_call" | custom-call | flops 2147483648 | tf_op jit(solution)/shard_map/mesh_rows/pallas_call | solution.py:47
  8.5 2.2 %edge_forward.1 = (bf16[2048,256]{1,0:T(8,128)(2,1)S(1)}, bf16[2048,256]{1,0:T(8,128)(2,1)S(1)}) custom-call(s32[16,128]{1,0:T(8,128)S(1)} %bitcast.9, bf16[2048,256]{1,0:T(8,128)(2,1)S(1)} %copy-done.6, bf16[2048,256]{1,0:T(8,128)(2,1)S(1)} %get-tuple-element.41.mesh_rows_ref, bf16[64,256]{1,0:T(8,128)(2,1)S(1)} %collective-permute-done.low_ref, ...), custom_call_target="tpu_custom_call" | custom-call | flops 1342177280 | tf_op jit(solution)/shard_map/edge_forward/pallas_call | solution.py:47
  10.7 1.2 %half_away.2 = bf16[1024,256]{1,0:T(8,128)(2,1)S(1)} custom-call(s32[16,128]{1,0:T(8,128)S(1)} %get-tuple-element.40.live_ref.refs_0_, bf16[2048,256]{1,0:T(8,128)(2,1)S(1)} %get-tuple-element.45.refs_1_.refs_3_), custom_call_target="tpu_custom_call" | custom-call | flops 1073741824 | tf_op jit(solution)/shard_map/half_away/pallas_call | solution.py:47
  12.0 3.2 %collective-permute-start.2 = (bf16[1024,256]{1,0:T(8,128)(2,1)S(1)}, bf16[1024,256]{1,0:T(8,128)(2,1)S(1)}, u32[]{:S(2)}, u32[]{:S(2)}) collective-permute-start(bf16[1024,256]{1,0:T(8,128)(2,1)S(1)} %half_away.2), channel_id=1, source_target_pairs={{0,1},{1,0},{2,3},{3,2},{4,5},{5,4},{6,7},{7,6},{8,9},{9,8},{10,11... | collective-permute-start | bytes 1572872 | tf_op jit(solution)/shard_map/ppermute | solution.py:372
  15.2 1.2 %half_here.2 = (f32[1024,256]{1,0:T(8,128)S(1)}, bf16[32,256]{1,0:T(8,128)(2,1)S(1)}) custom-call(s32[16,128]{1,0:T(8,128)S(1)} %get-tuple-element.40.live_ref.refs_0_, bf16[2048,256]{1,0:T(8,128)(2,1)S(1)} %get-tuple-element.45.refs_1_.refs_3_, bf16[2048,256]{1,0:T(8,128)(2,1)S(1)} %copy-done.7), custom_call_target="tpu_custom_call" | custom-call | flops 1073741824 | tf_op jit(solution)/shard_map/half_here/pallas_call | solution.py:47
  16.9 2.7 %collective-permute-start.4 = (bf16[256,256]{1,0:T(8,128)(2,1)S(1)}, bf16[256,256]{1,0:T(8,128)(2,1)S(1)}, u32[]{:S(2)}, u32[]{:S(2)}) collective-permute-start(bf16[256,256]{1,0:T(8,128)(2,1)S(1)} %get-tuple-element.48), channel_id=1, source_target_pairs={{0,6},{2,0},{4,2},{6,4},{1,7},{3,1},{5,3},{7,5},{8,14},{10,8},{12,... | collective-permute-start | bytes 393224 | tf_op jit(solution)/shard_map/ppermute | solution.py:386
  19.6 3.2 %collective-permute-done.3.a_ref = bf16[256,256]{1,0:T(8,128)(2,1)S(1)} collective-permute-done((bf16[256,256]{1,0:T(8,128)(2,1)S(1)}, bf16[256,256]{1,0:T(8,128)(2,1)S(1)}, u32[]{:S(2)}, u32[]{:S(2)}) %collective-permute-start.3) | collective-permute-done | bytes 131104 | tf_op jit(solution)/shard_map/ppermute | solution.py:386
  22.8 1.9 %collective-permute-done.4.b_ref = bf16[256,256]{1,0:T(8,128)(2,1)S(1)} collective-permute-done((bf16[256,256]{1,0:T(8,128)(2,1)S(1)}, bf16[256,256]{1,0:T(8,128)(2,1)S(1)}, u32[]{:S(2)}, u32[]{:S(2)}) %collective-permute-start.4) | collective-permute-done | bytes 131104 | tf_op jit(solution)/shard_map/ppermute | solution.py:386
  25.0 16.4 %all_to_all.15.parts_ref = bf16[8,32,256]{2,1,0:T(8,128)(2,1)S(1)} all-to-all(bf16[8,32,256]{2,1,0:T(8,128)(2,1)S(1)} %total.2), channel_id=1, replica_groups=mesh['lon'=4,'z'=8,'y'=4,'core'=2] {'z'}, dimensions={0} | all-to-all | bytes 262144 | tf_op jit(solution)/shard_map/all_to_all | solution.py:393
  42.3 17.0 %all_to_all.16 = bf16[32,32,256]{2,1,0:T(8,128)(2,1)S(1)} all-to-all(bf16[32,32,256]{2,1,0:T(8,128)(2,1)S(1)} %get-tuple-element.54), channel_id=1, replica_groups=mesh['lon'=4,'z'=8,'y'=4,'core'=2] {'z','y'}, dimensions={0} | all-to-all | bytes 1048576 | tf_op jit(solution)/shard_map/all_to_all | solution.py:404
  59.3 5.0 %collective-permute-start.6 = (bf16[1024,256]{1,0:T(8,128)(2,1)S(1)}, bf16[1024,256]{1,0:T(8,128)(2,1)S(1)}, u32[]{:S(2)}, u32[]{:S(2)}) collective-permute-start(bf16[1024,256]{1,0:T(8,128)(2,1)S(1)} %bitcast.7), channel_id=1, source_target_pairs={{0,1},{1,0},{2,3},{3,2},{4,5},{5,4},{6,7},{7,6},{8,9},{9,8},{10,11... | collective-permute-start | bytes 1572872 | tf_op jit(solution)/shard_map/ppermute | solution.py:405
  64.3 1.4 %near_rows.1.refs_1_ = bf16[2048,256]{1,0:T(8,128)(2,1)S(1)} custom-call(s32[16,128]{1,0:T(8,128)S(1)} %get-tuple-element.40.live_ref.refs_0_, bf16[1024,256]{1,0:T(8,128)(2,1)S(1)} %bitcast.8), custom_call_target="tpu_custom_call" | custom-call | flops 1073741824 | tf_op jit(solution)/shard_map/near_rows/pallas_call | solution.py:47
  65.8 2.1 %edge_backward.1.refs_1_.d_first_ref = bf16[2048,256]{1,0:T(8,128)(2,1)S(1)} custom-call(s32[16,128]{1,0:T(8,128)S(1)} %get-tuple-element.40.live_ref.refs_0_, bf16[2048,256]{1,0:T(8,128)(2,1)S(1)} %near_rows.1.refs_1_, bf16[1024,256]{1,0:T(8,128)(2,1)S(1)} %collective-permute-done.6.refs_2_, bf16[2048,256]{1,0:T(8,128)(2,1)S(1)} %get-tuple-element.45.refs_1_.refs_3_, ...), custom_call_target="tpu_custom_call" | custom-call | flops 1342177280 | tf_op jit(solution)/shard_map/edge_backward/pallas_call | solution.py:47
  68.0 1.2 %half_away.3 = bf16[1024,256]{1,0:T(8,128)(2,1)S(1)} custom-call(s32[16,128]{1,0:T(8,128)S(1)} %get-tuple-element.40.live_ref.refs_0_, bf16[2048,256]{1,0:T(8,128)(2,1)S(1)} %edge_backward.1.refs_1_.d_first_ref), custom_call_target="tpu_custom_call" | custom-call | flops 1073741824 | tf_op jit(solution)/shard_map/half_away/pallas_call | solution.py:47
  69.7 1.2 %half_here.3.here_ref = f32[1024,256]{1,0:T(8,128)S(1)} custom-call(s32[16,128]{1,0:T(8,128)S(1)} %get-tuple-element.40.live_ref.refs_0_, bf16[2048,256]{1,0:T(8,128)(2,1)S(1)} %edge_backward.1.refs_1_.d_first_ref), custom_call_target="tpu_custom_call" | custom-call | flops 1073741824 | tf_op jit(solution)/shard_map/half_here/pallas_call | solution.py:47
  71.6 2.4 %collective-permute-start.11 = (bf16[256,256]{1,0:T(8,128)(2,1)S(1)}, bf16[256,256]{1,0:T(8,128)(2,1)S(1)}, u32[]{:S(2)}, u32[]{:S(2)}) collective-permute-start(bf16[256,256]{1,0:T(8,128)(2,1)S(1)} %get-tuple-element.71), channel_id=1, source_target_pairs={{0,6},{2,0},{4,2},{6,4},{1,7},{3,1},{5,3},{7,5},{8,14},{10,8},{12,... | collective-permute-start | bytes 393224 | tf_op jit(solution)/shard_map/ppermute | solution.py:386
  75.9 1.5 %edge_grad.1 = bf16[2048,256]{1,0:T(8,128)(2,1)} custom-call(bf16[2048,256]{1,0:T(8,128)(2,1)S(1)} %edge_backward.1.refs_1_.d_first_ref, bf16[768,256]{1,0:T(8,128)(2,1)S(1)} %copy-done), custom_call_target="tpu_custom_call" | custom-call | flops 268435456 | tf_op jit(solution)/shard_map/edge_grad/pallas_call | solution.py:47
  77.3 1.9 %collective-permute-done.11.b_ref = bf16[256,256]{1,0:T(8,128)(2,1)S(1)} collective-permute-done((bf16[256,256]{1,0:T(8,128)(2,1)S(1)}, bf16[256,256]{1,0:T(8,128)(2,1)S(1)}, u32[]{:S(2)}, u32[]{:S(2)}) %collective-permute-start.11) | collective-permute-done | bytes 131104 | tf_op jit(solution)/shard_map/ppermute | solution.py:386
  80.1 3.4 %all-to-all-start.2 = ((bf16[8,32,256]{2,1,0:T(8,128)(2,1)}), bf16[8,32,256]{2,1,0:T(8,128)(2,1)S(1)}, u32[]{:S(2)}, u32[]{:S(2)}) async-start(bf16[8,32,256]{2,1,0:T(8,128)(2,1)} %total.3), calls=%async_computation.2 | async-start | bytes 262144 | tf_op jit(solution)/shard_map/all_to_all | solution.py:393
  84.4 1.9 %collective-permute-start.9 = (bf16[64,256]{1,0:T(8,128)(2,1)S(1)}, bf16[64,256]{1,0:T(8,128)(2,1)S(1)}, u32[]{:S(2)}, u32[]{:S(2)}) collective-permute-start(bf16[64,256]{1,0:T(8,128)(2,1)S(1)} %get-tuple-element.69), channel_id=1, source_target_pairs={{0,192},{64,0},{128,64},{192,128},{1,193},{65,1},{129,65},{193,129... | collective-permute-start | bytes 98312 | tf_op jit(solution)/shard_map/ppermute | solution.py:442
  86.3 1.3 %collective-permute-done.8.low_ref = bf16[64,256]{1,0:T(8,128)(2,1)S(1)} collective-permute-done((bf16[64,256]{1,0:T(8,128)(2,1)S(1)}, bf16[64,256]{1,0:T(8,128)(2,1)S(1)}, u32[]{:S(2)}, u32[]{:S(2)}) %collective-permute-start.8) | collective-permute-done | bytes 32800 | tf_op jit(solution)/shard_map/ppermute | solution.py:441
  88.6 2.9 %all-to-all-done.2.parts_ref = bf16[8,32,256]{2,1,0:T(8,128)(2,1)S(1)} async-done(((bf16[8,32,256]{2,1,0:T(8,128)(2,1)}), bf16[8,32,256]{2,1,0:T(8,128)(2,1)S(1)}, u32[]{:S(2)}, u32[]{:S(2)}) %all-to-all-start.2) | async-done | bytes 131104 | tf_op jit(solution)/shard_map/all_to_all | solution.py:393
  (52 shorter events, 9.4 us)
Async XLA Ops:
  0.6 1.0 %copy-start.8 = (bf16[768,256]{1,0:T(8,128)(2,1)S(1)}, bf16[768,256]{1,0:T(8,128)(2,1)}, u32[]{:S(2)}) copy-start(bf16[768,256]{1,0:T(8,128)(2,1)} %grid_ref.1) | copy-start | bytes 1179652
  0.6 1.0 %copy-start.11 = (f32[256]{0:T(256)S(1)}, f32[256]{0:T(256)}, u32[]{:S(2)}) copy-start(f32[256]{0:T(256)} %param.27) | copy-start | bytes 3076
  2.2 3.8 %copy-start.5 = (bf16[2048,256]{1,0:T(8,128)(2,1)S(1)}, bf16[2048,256]{1,0:T(8,128)(2,1)}, u32[]{:S(2)}) copy-start(bf16[2048,256]{1,0:T(8,128)(2,1)} %mesh_ref.1) | copy-start | bytes 3145732
  2.5 6.0 %collective-permute-start = (bf16[64,256]{1,0:T(8,128)(2,1)S(1)}, bf16[64,256]{1,0:T(8,128)(2,1)S(1)}, u32[]{:S(2)}, u32[]{:S(2)}) collective-permute-start(bf16[64,256]{1,0:T(8,128)(2,1)S(1)} %get-tuple-element.42), channel_id=1, source_target_pairs={{0,64},{64,128},{128,192},{192,0},{1,65},{65,129},{129,193},{193,1... | collective-permute-start | bytes 98312 | tf_op jit(solution)/shard_map/ppermute | solution.py:345
  4.6 3.9 %collective-permute-start.1 = (bf16[64,256]{1,0:T(8,128)(2,1)S(1)}, bf16[64,256]{1,0:T(8,128)(2,1)S(1)}, u32[]{:S(2)}, u32[]{:S(2)}) collective-permute-start(bf16[64,256]{1,0:T(8,128)(2,1)S(1)} %get-tuple-element.44), channel_id=1, source_target_pairs={{0,192},{64,0},{128,64},{192,128},{1,193},{65,1},{129,65},{193,129... | collective-permute-start | bytes 98312 | tf_op jit(solution)/shard_map/ppermute | solution.py:346
  5.9 2.5 %copy-start = (bf16[768,256]{1,0:T(8,128)(2,1)S(1)}, bf16[768,256]{1,0:T(8,128)(2,1)}, u32[]{:S(2)}) copy-start(bf16[768,256]{1,0:T(8,128)(2,1)} %first_ref.11) | copy-start | bytes 1179652
  5.9 2.5 %copy-start.3 = (s32[2048]{0:T(1024)S(1)}, s32[2048]{0:T(1024)}, u32[]{:S(2)}) copy-start(s32[2048]{0:T(1024)} %param.18) | copy-start | bytes 24580
  5.9 2.6 %copy-start.6 = (bf16[2048,256]{1,0:T(8,128)(2,1)S(1)}, bf16[2048,256]{1,0:T(8,128)(2,1)}, u32[]{:S(2)}) copy-start(bf16[2048,256]{1,0:T(8,128)(2,1)} %edge_ref.1) | copy-start | bytes 3145732
  6.0 2.6 %copy-start.9 = (bf16[256,256]{1,0:T(8,128)(2,1)S(1)}, bf16[256,256]{1,0:T(8,128)(2,1)}, u32[]{:S(2)}) copy-start(bf16[256,256]{1,0:T(8,128)(2,1)} %refs_5_.1) | copy-start | bytes 393220
  10.7 4.4 %copy-start.7 = (bf16[2048,256]{1,0:T(8,128)(2,1)S(1)}, bf16[2048,256]{1,0:T(8,128)(2,1)}, u32[]{:S(2)}) copy-start(bf16[2048,256]{1,0:T(8,128)(2,1)} %refs_2_.1) | copy-start | bytes 3145732
  12.0 4.7 %collective-permute-start.2 = (bf16[1024,256]{1,0:T(8,128)(2,1)S(1)}, bf16[1024,256]{1,0:T(8,128)(2,1)S(1)}, u32[]{:S(2)}, u32[]{:S(2)}) collective-permute-start(bf16[1024,256]{1,0:T(8,128)(2,1)S(1)} %half_away.2), channel_id=1, source_target_pairs={{0,1},{1,0},{2,3},{3,2},{4,5},{5,4},{6,7},{7,6},{8,9},{9,8},{10,11... | collective-permute-start | bytes 1572872 | tf_op jit(solution)/shard_map/ppermute | solution.py:372
  16.8 6.0 %collective-permute-start.3 = (bf16[256,256]{1,0:T(8,128)(2,1)S(1)}, bf16[256,256]{1,0:T(8,128)(2,1)S(1)}, u32[]{:S(2)}, u32[]{:S(2)}) collective-permute-start(bf16[256,256]{1,0:T(8,128)(2,1)S(1)} %get-tuple-element.47), channel_id=1, source_target_pairs={{0,2},{2,4},{4,6},{6,0},{1,3},{3,5},{5,7},{7,1},{8,10},{10,12},{12... | collective-permute-start | bytes 393224 | tf_op jit(solution)/shard_map/ppermute | solution.py:386
  16.9 7.8 %collective-permute-start.4 = (bf16[256,256]{1,0:T(8,128)(2,1)S(1)}, bf16[256,256]{1,0:T(8,128)(2,1)S(1)}, u32[]{:S(2)}, u32[]{:S(2)}) collective-permute-start(bf16[256,256]{1,0:T(8,128)(2,1)S(1)} %get-tuple-element.48), channel_id=1, source_target_pairs={{0,6},{2,0},{4,2},{6,4},{1,7},{3,1},{5,3},{7,5},{8,14},{10,8},{12,... | collective-permute-start | bytes 393224 | tf_op jit(solution)/shard_map/ppermute | solution.py:386
  19.6 5.3 %collective-permute-start.5 = (bf16[256,256]{1,0:T(8,128)(2,1)S(1)}, bf16[256,256]{1,0:T(8,128)(2,1)S(1)}, u32[]{:S(2)}, u32[]{:S(2)}) collective-permute-start(bf16[256,256]{1,0:T(8,128)(2,1)S(1)} %get-tuple-element.49), channel_id=1, source_target_pairs={{0,4},{2,6},{4,0},{6,2},{1,5},{3,7},{5,1},{7,3},{8,12},{10,14},{12... | collective-permute-start | bytes 393224 | tf_op jit(solution)/shard_map/ppermute | solution.py:386
  24.9 16.5 %copy-start.2 = (bf16[256,256]{1,0:T(8,128)(2,1)S(1)}, bf16[256,256]{1,0:T(8,128)(2,1)}, u32[]{:S(2)}) copy-start(bf16[256,256]{1,0:T(8,128)(2,1)} %second_ref.3) | copy-start | bytes 393220
  24.9 16.4 %copy-start.1 = (bf16[512,256]{1,0:T(8,128)(2,1)S(1)}, bf16[512,256]{1,0:T(8,128)(2,1)}, u32[]{:S(2)}) copy-start(bf16[512,256]{1,0:T(8,128)(2,1)} %first_ref.10) | copy-start | bytes 786436
  59.3 6.6 %collective-permute-start.6 = (bf16[1024,256]{1,0:T(8,128)(2,1)S(1)}, bf16[1024,256]{1,0:T(8,128)(2,1)S(1)}, u32[]{:S(2)}, u32[]{:S(2)}) collective-permute-start(bf16[1024,256]{1,0:T(8,128)(2,1)S(1)} %bitcast.7), channel_id=1, source_target_pairs={{0,1},{1,0},{2,3},{3,2},{4,5},{5,4},{6,7},{7,6},{8,9},{9,8},{10,11... | collective-permute-start | bytes 1572872 | tf_op jit(solution)/shard_map/ppermute | solution.py:405
  69.3 2.0 %collective-permute-start.7 = (bf16[1024,256]{1,0:T(8,128)(2,1)S(1)}, bf16[1024,256]{1,0:T(8,128)(2,1)S(1)}, u32[]{:S(2)}, u32[]{:S(2)}) collective-permute-start(bf16[1024,256]{1,0:T(8,128)(2,1)S(1)} %half_away.3), channel_id=1, source_target_pairs={{0,1},{1,0},{2,3},{3,2},{4,5},{5,4},{6,7},{7,6},{8,9},{9,8},{10,11... | collective-permute-start | bytes 1572872 | tf_op jit(solution)/shard_map/ppermute | solution.py:372
  71.3 6.0 %collective-permute-start.10 = (bf16[256,256]{1,0:T(8,128)(2,1)S(1)}, bf16[256,256]{1,0:T(8,128)(2,1)S(1)}, u32[]{:S(2)}, u32[]{:S(2)}) collective-permute-start(bf16[256,256]{1,0:T(8,128)(2,1)S(1)} %get-tuple-element.70), channel_id=1, source_target_pairs={{0,2},{2,4},{4,6},{6,0},{1,3},{3,5},{5,7},{7,1},{8,10},{10,12},{12... | collective-permute-start | bytes 393224 | tf_op jit(solution)/shard_map/ppermute | solution.py:386
  71.6 7.6 %collective-permute-start.11 = (bf16[256,256]{1,0:T(8,128)(2,1)S(1)}, bf16[256,256]{1,0:T(8,128)(2,1)S(1)}, u32[]{:S(2)}, u32[]{:S(2)}) collective-permute-start(bf16[256,256]{1,0:T(8,128)(2,1)S(1)} %get-tuple-element.71), channel_id=1, source_target_pairs={{0,6},{2,0},{4,2},{6,4},{1,7},{3,1},{5,3},{7,5},{8,14},{10,8},{12,... | collective-permute-start | bytes 393224 | tf_op jit(solution)/shard_map/ppermute | solution.py:386
  74.1 5.3 %collective-permute-start.12 = (bf16[256,256]{1,0:T(8,128)(2,1)S(1)}, bf16[256,256]{1,0:T(8,128)(2,1)S(1)}, u32[]{:S(2)}, u32[]{:S(2)}) collective-permute-start(bf16[256,256]{1,0:T(8,128)(2,1)S(1)} %get-tuple-element.72), channel_id=1, source_target_pairs={{0,4},{2,6},{4,0},{6,2},{1,5},{3,7},{5,1},{7,3},{8,12},{10,14},{12... | collective-permute-start | bytes 393224 | tf_op jit(solution)/shard_map/ppermute | solution.py:386
  80.1 11.3 %all-to-all-start.2 = ((bf16[8,32,256]{2,1,0:T(8,128)(2,1)}), bf16[8,32,256]{2,1,0:T(8,128)(2,1)S(1)}, u32[]{:S(2)}, u32[]{:S(2)}) async-start(bf16[8,32,256]{2,1,0:T(8,128)(2,1)} %total.3), calls=%async_computation.2 | async-start | bytes 262144 | tf_op jit(solution)/shard_map/all_to_all | solution.py:393
  83.5 4.1 %collective-permute-start.8 = (bf16[64,256]{1,0:T(8,128)(2,1)S(1)}, bf16[64,256]{1,0:T(8,128)(2,1)S(1)}, u32[]{:S(2)}, u32[]{:S(2)}) collective-permute-start(bf16[64,256]{1,0:T(8,128)(2,1)S(1)} %get-tuple-element.67), channel_id=1, source_target_pairs={{0,64},{64,128},{128,192},{192,0},{1,65},{65,129},{129,193},{193,1... | collective-permute-start | bytes 98312 | tf_op jit(solution)/shard_map/ppermute | solution.py:441
  84.4 3.2 %collective-permute-start.9 = (bf16[64,256]{1,0:T(8,128)(2,1)S(1)}, bf16[64,256]{1,0:T(8,128)(2,1)S(1)}, u32[]{:S(2)}, u32[]{:S(2)}) collective-permute-start(bf16[64,256]{1,0:T(8,128)(2,1)S(1)} %get-tuple-element.69), channel_id=1, source_target_pairs={{0,192},{64,0},{128,64},{192,128},{1,193},{65,1},{129,65},{193,129... | collective-permute-start | bytes 98312 | tf_op jit(solution)/shard_map/ppermute | solution.py:442
  (3 other events, 2.6 us)

commit v8 on v6

--- a/solution.py
+++ b/solution.py
@@ -425,10 +425,6 @@
             slot_sum_kernel, [((side, width), bf16)] * 3, (send, d_first, edge_first),
             flops=dense, name="slot_sum",
         )
-        grads = call(
-            edge_grad_kernel, [((edges, width), bf16)], (d_first, edge_first),
-            flops=dense, name="edge_grad",
-        )
         late_normed, late_d_pre, _ = lax.optimization_barrier((node_normed, d_pre, d_first))
         node_outs = call(
             mesh_out_kernel,
@@ -436,13 +432,18 @@
             (own_mesh, own_cot, late_normed, late_d_pre, node_first, gains),
             flops=2 * own * width * width, name="mesh_out",
         )
-        return (*slots, *grads, *node_outs)
-
-    mesh_parts, back_low, back_own, back_high, edge_grad, mesh_out, direct = to_owners(
+        return (*slots, *node_outs)
+
+    mesh_parts, back_low, back_own, back_high, mesh_out, direct = to_owners(
         d_first, beside=other_work
     )
     got_low = lax.ppermute(back_high, "lon", ring(lon_count, 1))
     got_high = lax.ppermute(back_low, "lon", ring(lon_count, -1))
+    late_first, _ = lax.optimization_barrier((d_first, back_own))
+    (edge_grad,) = call(
+        edge_grad_kernel, [((edges, width), bf16)], (late_first, edge_first),
+        flops=dense, name="edge_grad",
+    )
     (grid_grad,) = call(
         grid_grad_kernel,
         [((grid_rows, width), bf16)],

time: 94 us -> 94.1 us (level)
    ppermute x6, waiting for transfers between devices: 7.41 us -> 8.87 us  [to_owners(): lax.ppermute(total, 'y', ring(lanes, shift))]
    ppermute x1, waiting for transfers between devices: 1.3 us -> 0.01 us  [shards(): got_low = lax.ppermute(back_high, 'lon', ring(lon_count, 1))]
where the time goes in v8:
time: 94.1 us; the launch traced here: 92.3 us
  blocking collectives  33.4 us (35%)
  starting transfers between devices  24.3 us (26%)
  Pallas kernels  20 us (21%)
  waiting for transfers between devices  12.3 us (13%)
  between operations  1.6 us (2%)
    pallas_call x20, Pallas kernels, call(): pl.pallas_call(kernel, out_shape=[jax.ShapeDtypeStruct(s, d) for s, d in...  20 us
    all_to_all x1, blocking collectives, shards(): lax.all_to_all(grad_copies, zy, 0, 0, tiled=True).reshape(half, width)  17 us
    all_to_all x1, blocking collectives, to_owners(): parts = lax.all_to_all(both, 'z', 0, 0, tiled=True)  16.4 us
    ppermute x6, waiting for transfers between devices, to_owners(): lax.ppermute(total, 'y', ring(lanes, shift))  8.87 us
    ppermute x6, starting transfers between devices, to_owners(): lax.ppermute(total, 'y', ring(lanes, shift))  6.03 us
    ppermute x1, starting transfers between devices, shards(): far = lax.ppermute(near, 'core', swap)  5.01 us
    ppermute x2, starting transfers between devices, to_owners(): away = lax.ppermute(out, 'core', swap)  3.63 us
    all_to_all x1, starting transfers between devices, to_owners(): parts = lax.all_to_all(both, 'z', 0, 0, tiled=True)  3.37 us
  transfers between devices with their start and end apart: 14, of which 10 were waited for; matrix products, arithmetic and copies ran while one was open for 0% of the time, Pallas kernels for 11%

profile of v8, /device:TPU:1, one launch (start us, length us, event | category | flops | bytes accessed | tf_op | source)
XLA Modules:
  0.0 92.3 jit_solution(11930144804152859155)
XLA Ops:
  2.5 2.1 %collective-permute-start = (bf16[64,256]{1,0:T(8,128)(2,1)S(1)}, bf16[64,256]{1,0:T(8,128)(2,1)S(1)}, u32[]{:S(2)}, u32[]{:S(2)}) collective-permute-start(bf16[64,256]{1,0:T(8,128)(2,1)S(1)} %get-tuple-element.42), channel_id=1, source_target_pairs={{0,64},{64,128},{128,192},{192,0},{1,65},{65,129},{129,193},{193,1... | collective-permute-start | bytes 98312 | tf_op jit(solution)/shard_map/ppermute | solution.py:347
  4.6 1.4 %collective-permute-start.1 = (bf16[64,256]{1,0:T(8,128)(2,1)S(1)}, bf16[64,256]{1,0:T(8,128)(2,1)S(1)}, u32[]{:S(2)}, u32[]{:S(2)}) collective-permute-start(bf16[64,256]{1,0:T(8,128)(2,1)S(1)} %get-tuple-element.44), channel_id=1, source_target_pairs={{0,192},{64,0},{128,64},{192,128},{1,193},{65,1},{129,65},{193,129... | collective-permute-start | bytes 98312 | tf_op jit(solution)/shard_map/ppermute | solution.py:348
  6.0 2.5 %mesh_rows.1 = (bf16[2048,256]{1,0:T(8,128)(2,1)S(1)}, bf16[32,256]{1,0:T(8,128)(2,1)S(1)}) custom-call(s32[16,128]{1,0:T(8,128)S(1)} %get-tuple-element.40.live_ref.refs_0_, bf16[2048,256]{1,0:T(8,128)(2,1)S(1)} %copy-done.5), custom_call_target="tpu_custom_call" | custom-call | flops 2147483648 | tf_op jit(solution)/shard_map/mesh_rows/pallas_call | solution.py:47
  8.5 2.2 %edge_forward.1 = (bf16[2048,256]{1,0:T(8,128)(2,1)S(1)}, bf16[2048,256]{1,0:T(8,128)(2,1)S(1)}) custom-call(s32[16,128]{1,0:T(8,128)S(1)} %bitcast.9, bf16[2048,256]{1,0:T(8,128)(2,1)S(1)} %copy-done.6, bf16[2048,256]{1,0:T(8,128)(2,1)S(1)} %get-tuple-element.41.mesh_rows_ref, bf16[64,256]{1,0:T(8,128)(2,1)S(1)} %collective-permute-done.low_ref, ...), custom_call_target="tpu_custom_call" | custom-call | flops 1342177280 | tf_op jit(solution)/shard_map/edge_forward/pallas_call | solution.py:47
  10.7 1.2 %half_away.2 = bf16[1024,256]{1,0:T(8,128)(2,1)S(1)} custom-call(s32[16,128]{1,0:T(8,128)S(1)} %get-tuple-element.40.live_ref.refs_0_, bf16[2048,256]{1,0:T(8,128)(2,1)S(1)} %get-tuple-element.45.refs_1_.refs_3_), custom_call_target="tpu_custom_call" | custom-call | flops 1073741824 | tf_op jit(solution)/shard_map/half_away/pallas_call | solution.py:47
  12.0 3.2 %collective-permute-start.2 = (bf16[1024,256]{1,0:T(8,128)(2,1)S(1)}, bf16[1024,256]{1,0:T(8,128)(2,1)S(1)}, u32[]{:S(2)}, u32[]{:S(2)}) collective-permute-start(bf16[1024,256]{1,0:T(8,128)(2,1)S(1)} %half_away.2), channel_id=1, source_target_pairs={{0,1},{1,0},{2,3},{3,2},{4,5},{5,4},{6,7},{7,6},{8,9},{9,8},{10,11... | collective-permute-start | bytes 1572872 | tf_op jit(solution)/shard_map/ppermute | solution.py:374
  15.2 1.2 %half_here.2 = (f32[1024,256]{1,0:T(8,128)S(1)}, bf16[32,256]{1,0:T(8,128)(2,1)S(1)}) custom-call(s32[16,128]{1,0:T(8,128)S(1)} %get-tuple-element.40.live_ref.refs_0_, bf16[2048,256]{1,0:T(8,128)(2,1)S(1)} %get-tuple-element.45.refs_1_.refs_3_, bf16[2048,256]{1,0:T(8,128)(2,1)S(1)} %copy-done.7), custom_call_target="tpu_custom_call" | custom-call | flops 1073741824 | tf_op jit(solution)/shard_map/half_here/pallas_call | solution.py:47
  16.9 2.7 %collective-permute-start.4 = (bf16[256,256]{1,0:T(8,128)(2,1)S(1)}, bf16[256,256]{1,0:T(8,128)(2,1)S(1)}, u32[]{:S(2)}, u32[]{:S(2)}) collective-permute-start(bf16[256,256]{1,0:T(8,128)(2,1)S(1)} %get-tuple-element.48), channel_id=1, source_target_pairs={{0,6},{2,0},{4,2},{6,4},{1,7},{3,1},{5,3},{7,5},{8,14},{10,8},{12,... | collective-permute-start | bytes 393224 | tf_op jit(solution)/shard_map/ppermute | solution.py:388
  19.6 3.2 %collective-permute-done.3.a_ref = bf16[256,256]{1,0:T(8,128)(2,1)S(1)} collective-permute-done((bf16[256,256]{1,0:T(8,128)(2,1)S(1)}, bf16[256,256]{1,0:T(8,128)(2,1)S(1)}, u32[]{:S(2)}, u32[]{:S(2)}) %collective-permute-start.3) | collective-permute-done | bytes 131104 | tf_op jit(solution)/shard_map/ppermute | solution.py:388
  22.8 1.9 %collective-permute-done.4.b_ref = bf16[256,256]{1,0:T(8,128)(2,1)S(1)} collective-permute-done((bf16[256,256]{1,0:T(8,128)(2,1)S(1)}, bf16[256,256]{1,0:T(8,128)(2,1)S(1)}, u32[]{:S(2)}, u32[]{:S(2)}) %collective-permute-start.4) | collective-permute-done | bytes 131104 | tf_op jit(solution)/shard_map/ppermute | solution.py:388
  25.0 16.4 %all_to_all.15.parts_ref = bf16[8,32,256]{2,1,0:T(8,128)(2,1)S(1)} all-to-all(bf16[8,32,256]{2,1,0:T(8,128)(2,1)S(1)} %total.2), channel_id=1, replica_groups=mesh['lon'=4,'z'=8,'y'=4,'core'=2] {'z'}, dimensions={0} | all-to-all | bytes 262144 | tf_op jit(solution)/shard_map/all_to_all | solution.py:395
  42.2 17.0 %all_to_all.16 = bf16[32,32,256]{2,1,0:T(8,128)(2,1)S(1)} all-to-all(bf16[32,32,256]{2,1,0:T(8,128)(2,1)S(1)} %get-tuple-element.54), channel_id=1, replica_groups=mesh['lon'=4,'z'=8,'y'=4,'core'=2] {'z','y'}, dimensions={0} | all-to-all | bytes 1048576 | tf_op jit(solution)/shard_map/all_to_all | solution.py:406
  59.2 5.0 %collective-permute-start.6 = (bf16[1024,256]{1,0:T(8,128)(2,1)S(1)}, bf16[1024,256]{1,0:T(8,128)(2,1)S(1)}, u32[]{:S(2)}, u32[]{:S(2)}) collective-permute-start(bf16[1024,256]{1,0:T(8,128)(2,1)S(1)} %bitcast.7), channel_id=1, source_target_pairs={{0,1},{1,0},{2,3},{3,2},{4,5},{5,4},{6,7},{7,6},{8,9},{9,8},{10,11... | collective-permute-start | bytes 1572872 | tf_op jit(solution)/shard_map/ppermute | solution.py:407
  64.2 1.4 %near_rows.1.refs_1_ = bf16[2048,256]{1,0:T(8,128)(2,1)S(1)} custom-call(s32[16,128]{1,0:T(8,128)S(1)} %get-tuple-element.40.live_ref.refs_0_, bf16[1024,256]{1,0:T(8,128)(2,1)S(1)} %bitcast.8), custom_call_target="tpu_custom_call" | custom-call | flops 1073741824 | tf_op jit(solution)/shard_map/near_rows/pallas_call | solution.py:47
  65.8 2.3 %edge_backward.1.refs_1_.d_first_ref = bf16[2048,256]{1,0:T(8,128)(2,1)S(1)} custom-call(s32[16,128]{1,0:T(8,128)S(1)} %get-tuple-element.40.live_ref.refs_0_, bf16[2048,256]{1,0:T(8,128)(2,1)S(1)} %near_rows.1.refs_1_, bf16[1024,256]{1,0:T(8,128)(2,1)S(1)} %collective-permute-done.6.refs_2_, bf16[2048,256]{1,0:T(8,128)(2,1)S(1)} %get-tuple-element.45.refs_1_.refs_3_, ...), custom_call_target="tpu_custom_call" | custom-call | flops 1342177280 | tf_op jit(solution)/shard_map/edge_backward/pallas_call | solution.py:47
  68.1 1.2 %half_away.3 = bf16[1024,256]{1,0:T(8,128)(2,1)S(1)} custom-call(s32[16,128]{1,0:T(8,128)S(1)} %get-tuple-element.40.live_ref.refs_0_, bf16[2048,256]{1,0:T(8,128)(2,1)S(1)} %edge_backward.1.refs_1_.d_first_ref), custom_call_target="tpu_custom_call" | custom-call | flops 1073741824 | tf_op jit(solution)/shard_map/half_away/pallas_call | solution.py:47
  69.8 1.2 %half_here.3.here_ref = f32[1024,256]{1,0:T(8,128)S(1)} custom-call(s32[16,128]{1,0:T(8,128)S(1)} %get-tuple-element.40.live_ref.refs_0_, bf16[2048,256]{1,0:T(8,128)(2,1)S(1)} %edge_backward.1.refs_1_.d_first_ref), custom_call_target="tpu_custom_call" | custom-call | flops 1073741824 | tf_op jit(solution)/shard_map/half_here/pallas_call | solution.py:47
  71.7 2.5 %collective-permute-start.11 = (bf16[256,256]{1,0:T(8,128)(2,1)S(1)}, bf16[256,256]{1,0:T(8,128)(2,1)S(1)}, u32[]{:S(2)}, u32[]{:S(2)}) collective-permute-start(bf16[256,256]{1,0:T(8,128)(2,1)S(1)} %get-tuple-element.71), channel_id=1, source_target_pairs={{0,6},{2,0},{4,2},{6,4},{1,7},{3,1},{5,3},{7,5},{8,14},{10,8},{12,... | collective-permute-start | bytes 393224 | tf_op jit(solution)/shard_map/ppermute | solution.py:388
  75.9 1.5 %collective-permute-done.10.a_ref = bf16[256,256]{1,0:T(8,128)(2,1)S(1)} collective-permute-done((bf16[256,256]{1,0:T(8,128)(2,1)S(1)}, bf16[256,256]{1,0:T(8,128)(2,1)S(1)}, u32[]{:S(2)}, u32[]{:S(2)}) %collective-permute-start.10) | collective-permute-done | bytes 131104 | tf_op jit(solution)/shard_map/ppermute | solution.py:388
  77.4 1.9 %collective-permute-done.11.b_ref = bf16[256,256]{1,0:T(8,128)(2,1)S(1)} collective-permute-done((bf16[256,256]{1,0:T(8,128)(2,1)S(1)}, bf16[256,256]{1,0:T(8,128)(2,1)S(1)}, u32[]{:S(2)}, u32[]{:S(2)}) %collective-permute-start.11) | collective-permute-done | bytes 131104 | tf_op jit(solution)/shard_map/ppermute | solution.py:388
  80.2 3.4 %all-to-all-start.2 = ((bf16[8,32,256]{2,1,0:T(8,128)(2,1)}), bf16[8,32,256]{2,1,0:T(8,128)(2,1)S(1)}, u32[]{:S(2)}, u32[]{:S(2)}) async-start(bf16[8,32,256]{2,1,0:T(8,128)(2,1)} %total.3), calls=%async_computation.2 | async-start | bytes 262144 | tf_op jit(solution)/shard_map/all_to_all | solution.py:395
  84.5 1.9 %collective-permute-start.9 = (bf16[64,256]{1,0:T(8,128)(2,1)S(1)}, bf16[64,256]{1,0:T(8,128)(2,1)S(1)}, u32[]{:S(2)}, u32[]{:S(2)}) collective-permute-start(bf16[64,256]{1,0:T(8,128)(2,1)S(1)} %get-tuple-element.69), channel_id=1, source_target_pairs={{0,192},{64,0},{128,64},{192,128},{1,193},{65,1},{129,65},{193,129... | collective-permute-start | bytes 98312 | tf_op jit(solution)/shard_map/ppermute | solution.py:441
  86.3 1.4 %edge_grad.1 = bf16[2048,256]{1,0:T(8,128)(2,1)} custom-call(bf16[2048,256]{1,0:T(8,128)(2,1)S(1)} %edge_backward.1.refs_1_.d_first_ref, bf16[768,256]{1,0:T(8,128)(2,1)S(1)} %copy-done), custom_call_target="tpu_custom_call" | custom-call | flops 268435456 | tf_op jit(solution)/shard_map/edge_grad/pallas_call | solution.py:47
  88.8 2.7 %all-to-all-done.2.parts_ref = bf16[8,32,256]{2,1,0:T(8,128)(2,1)S(1)} async-done(((bf16[8,32,256]{2,1,0:T(8,128)(2,1)}), bf16[8,32,256]{2,1,0:T(8,128)(2,1)S(1)}, u32[]{:S(2)}, u32[]{:S(2)}) %all-to-all-start.2) | async-done | bytes 131104 | tf_op jit(solution)/shard_map/all_to_all | solution.py:395
  (52 shorter events, 9.3 us)
Async XLA Ops:
  0.6 1.0 %copy-start.8 = (bf16[768,256]{1,0:T(8,128)(2,1)S(1)}, bf16[768,256]{1,0:T(8,128)(2,1)}, u32[]{:S(2)}) copy-start(bf16[768,256]{1,0:T(8,128)(2,1)} %grid_ref.1) | copy-start | bytes 1179652
  0.6 1.0 %copy-start.11 = (f32[256]{0:T(256)S(1)}, f32[256]{0:T(256)}, u32[]{:S(2)}) copy-start(f32[256]{0:T(256)} %param.27) | copy-start | bytes 3076
  2.2 3.8 %copy-start.5 = (bf16[2048,256]{1,0:T(8,128)(2,1)S(1)}, bf16[2048,256]{1,0:T(8,128)(2,1)}, u32[]{:S(2)}) copy-start(bf16[2048,256]{1,0:T(8,128)(2,1)} %mesh_ref.1) | copy-start | bytes 3145732
  2.5 6.0 %collective-permute-start = (bf16[64,256]{1,0:T(8,128)(2,1)S(1)}, bf16[64,256]{1,0:T(8,128)(2,1)S(1)}, u32[]{:S(2)}, u32[]{:S(2)}) collective-permute-start(bf16[64,256]{1,0:T(8,128)(2,1)S(1)} %get-tuple-element.42), channel_id=1, source_target_pairs={{0,64},{64,128},{128,192},{192,0},{1,65},{65,129},{129,193},{193,1... | collective-permute-start | bytes 98312 | tf_op jit(solution)/shard_map/ppermute | solution.py:347
  4.6 3.9 %collective-permute-start.1 = (bf16[64,256]{1,0:T(8,128)(2,1)S(1)}, bf16[64,256]{1,0:T(8,128)(2,1)S(1)}, u32[]{:S(2)}, u32[]{:S(2)}) collective-permute-start(bf16[64,256]{1,0:T(8,128)(2,1)S(1)} %get-tuple-element.44), channel_id=1, source_target_pairs={{0,192},{64,0},{128,64},{192,128},{1,193},{65,1},{129,65},{193,129... | collective-permute-start | bytes 98312 | tf_op jit(solution)/shard_map/ppermute | solution.py:348
  5.9 2.5 %copy-start = (bf16[768,256]{1,0:T(8,128)(2,1)S(1)}, bf16[768,256]{1,0:T(8,128)(2,1)}, u32[]{:S(2)}) copy-start(bf16[768,256]{1,0:T(8,128)(2,1)} %first_ref.11) | copy-start | bytes 1179652
  5.9 2.5 %copy-start.3 = (s32[2048]{0:T(1024)S(1)}, s32[2048]{0:T(1024)}, u32[]{:S(2)}) copy-start(s32[2048]{0:T(1024)} %param.18) | copy-start | bytes 24580
  5.9 2.6 %copy-start.6 = (bf16[2048,256]{1,0:T(8,128)(2,1)S(1)}, bf16[2048,256]{1,0:T(8,128)(2,1)}, u32[]{:S(2)}) copy-start(bf16[2048,256]{1,0:T(8,128)(2,1)} %edge_ref.1) | copy-start | bytes 3145732
  6.0 2.6 %copy-start.9 = (bf16[256,256]{1,0:T(8,128)(2,1)S(1)}, bf16[256,256]{1,0:T(8,128)(2,1)}, u32[]{:S(2)}) copy-start(bf16[256,256]{1,0:T(8,128)(2,1)} %refs_5_.1) | copy-start | bytes 393220
  10.7 4.4 %copy-start.7 = (bf16[2048,256]{1,0:T(8,128)(2,1)S(1)}, bf16[2048,256]{1,0:T(8,128)(2,1)}, u32[]{:S(2)}) copy-start(bf16[2048,256]{1,0:T(8,128)(2,1)} %refs_2_.1) | copy-start | bytes 3145732
  12.0 4.7 %collective-permute-start.2 = (bf16[1024,256]{1,0:T(8,128)(2,1)S(1)}, bf16[1024,256]{1,0:T(8,128)(2,1)S(1)}, u32[]{:S(2)}, u32[]{:S(2)}) collective-permute-start(bf16[1024,256]{1,0:T(8,128)(2,1)S(1)} %half_away.2), channel_id=1, source_target_pairs={{0,1},{1,0},{2,3},{3,2},{4,5},{5,4},{6,7},{7,6},{8,9},{9,8},{10,11... | collective-permute-start | bytes 1572872 | tf_op jit(solution)/shard_map/ppermute | solution.py:374
  16.8 6.0 %collective-permute-start.3 = (bf16[256,256]{1,0:T(8,128)(2,1)S(1)}, bf16[256,256]{1,0:T(8,128)(2,1)S(1)}, u32[]{:S(2)}, u32[]{:S(2)}) collective-permute-start(bf16[256,256]{1,0:T(8,128)(2,1)S(1)} %get-tuple-element.47), channel_id=1, source_target_pairs={{0,2},{2,4},{4,6},{6,0},{1,3},{3,5},{5,7},{7,1},{8,10},{10,12},{12... | collective-permute-start | bytes 393224 | tf_op jit(solution)/shard_map/ppermute | solution.py:388
  16.9 7.8 %collective-permute-start.4 = (bf16[256,256]{1,0:T(8,128)(2,1)S(1)}, bf16[256,256]{1,0:T(8,128)(2,1)S(1)}, u32[]{:S(2)}, u32[]{:S(2)}) collective-permute-start(bf16[256,256]{1,0:T(8,128)(2,1)S(1)} %get-tuple-element.48), channel_id=1, source_target_pairs={{0,6},{2,0},{4,2},{6,4},{1,7},{3,1},{5,3},{7,5},{8,14},{10,8},{12,... | collective-permute-start | bytes 393224 | tf_op jit(solution)/shard_map/ppermute | solution.py:388
  19.6 5.3 %collective-permute-start.5 = (bf16[256,256]{1,0:T(8,128)(2,1)S(1)}, bf16[256,256]{1,0:T(8,128)(2,1)S(1)}, u32[]{:S(2)}, u32[]{:S(2)}) collective-permute-start(bf16[256,256]{1,0:T(8,128)(2,1)S(1)} %get-tuple-element.49), channel_id=1, source_target_pairs={{0,4},{2,6},{4,0},{6,2},{1,5},{3,7},{5,1},{7,3},{8,12},{10,14},{12... | collective-permute-start | bytes 393224 | tf_op jit(solution)/shard_map/ppermute | solution.py:388
  24.9 16.5 %copy-start.2 = (bf16[256,256]{1,0:T(8,128)(2,1)S(1)}, bf16[256,256]{1,0:T(8,128)(2,1)}, u32[]{:S(2)}) copy-start(bf16[256,256]{1,0:T(8,128)(2,1)} %second_ref.3) | copy-start | bytes 393220
  25.0 16.4 %copy-start.1 = (bf16[512,256]{1,0:T(8,128)(2,1)S(1)}, bf16[512,256]{1,0:T(8,128)(2,1)}, u32[]{:S(2)}) copy-start(bf16[512,256]{1,0:T(8,128)(2,1)} %first_ref.9) | copy-start | bytes 786436
  59.2 6.6 %collective-permute-start.6 = (bf16[1024,256]{1,0:T(8,128)(2,1)S(1)}, bf16[1024,256]{1,0:T(8,128)(2,1)S(1)}, u32[]{:S(2)}, u32[]{:S(2)}) collective-permute-start(bf16[1024,256]{1,0:T(8,128)(2,1)S(1)} %bitcast.7), channel_id=1, source_target_pairs={{0,1},{1,0},{2,3},{3,2},{4,5},{5,4},{6,7},{7,6},{8,9},{9,8},{10,11... | collective-permute-start | bytes 1572872 | tf_op jit(solution)/shard_map/ppermute | solution.py:407
  69.3 2.0 %collective-permute-start.7 = (bf16[1024,256]{1,0:T(8,128)(2,1)S(1)}, bf16[1024,256]{1,0:T(8,128)(2,1)S(1)}, u32[]{:S(2)}, u32[]{:S(2)}) collective-permute-start(bf16[1024,256]{1,0:T(8,128)(2,1)S(1)} %half_away.3), channel_id=1, source_target_pairs={{0,1},{1,0},{2,3},{3,2},{4,5},{5,4},{6,7},{7,6},{8,9},{9,8},{10,11... | collective-permute-start | bytes 1572872 | tf_op jit(solution)/shard_map/ppermute | solution.py:374
  71.4 6.0 %collective-permute-start.10 = (bf16[256,256]{1,0:T(8,128)(2,1)S(1)}, bf16[256,256]{1,0:T(8,128)(2,1)S(1)}, u32[]{:S(2)}, u32[]{:S(2)}) collective-permute-start(bf16[256,256]{1,0:T(8,128)(2,1)S(1)} %get-tuple-element.70), channel_id=1, source_target_pairs={{0,2},{2,4},{4,6},{6,0},{1,3},{3,5},{5,7},{7,1},{8,10},{10,12},{12... | collective-permute-start | bytes 393224 | tf_op jit(solution)/shard_map/ppermute | solution.py:388
  71.7 7.6 %collective-permute-start.11 = (bf16[256,256]{1,0:T(8,128)(2,1)S(1)}, bf16[256,256]{1,0:T(8,128)(2,1)S(1)}, u32[]{:S(2)}, u32[]{:S(2)}) collective-permute-start(bf16[256,256]{1,0:T(8,128)(2,1)S(1)} %get-tuple-element.71), channel_id=1, source_target_pairs={{0,6},{2,0},{4,2},{6,4},{1,7},{3,1},{5,3},{7,5},{8,14},{10,8},{12,... | collective-permute-start | bytes 393224 | tf_op jit(solution)/shard_map/ppermute | solution.py:388
  74.1 5.3 %collective-permute-start.12 = (bf16[256,256]{1,0:T(8,128)(2,1)S(1)}, bf16[256,256]{1,0:T(8,128)(2,1)S(1)}, u32[]{:S(2)}, u32[]{:S(2)}) collective-permute-start(bf16[256,256]{1,0:T(8,128)(2,1)S(1)} %get-tuple-element.72), channel_id=1, source_target_pairs={{0,4},{2,6},{4,0},{6,2},{1,5},{3,7},{5,1},{7,3},{8,12},{10,14},{12... | collective-permute-start | bytes 393224 | tf_op jit(solution)/shard_map/ppermute | solution.py:388
  80.2 11.3 %all-to-all-start.2 = ((bf16[8,32,256]{2,1,0:T(8,128)(2,1)}), bf16[8,32,256]{2,1,0:T(8,128)(2,1)S(1)}, u32[]{:S(2)}, u32[]{:S(2)}) async-start(bf16[8,32,256]{2,1,0:T(8,128)(2,1)} %total.3), calls=%async_computation.2 | async-start | bytes 262144 | tf_op jit(solution)/shard_map/all_to_all | solution.py:395
  83.6 4.2 %collective-permute-start.8 = (bf16[64,256]{1,0:T(8,128)(2,1)S(1)}, bf16[64,256]{1,0:T(8,128)(2,1)S(1)}, u32[]{:S(2)}, u32[]{:S(2)}) collective-permute-start(bf16[64,256]{1,0:T(8,128)(2,1)S(1)} %get-tuple-element.67), channel_id=1, source_target_pairs={{0,64},{64,128},{128,192},{192,0},{1,65},{65,129},{129,193},{193,1... | collective-permute-start | bytes 98312 | tf_op jit(solution)/shard_map/ppermute | solution.py:440
  84.5 3.3 %collective-permute-start.9 = (bf16[64,256]{1,0:T(8,128)(2,1)S(1)}, bf16[64,256]{1,0:T(8,128)(2,1)S(1)}, u32[]{:S(2)}, u32[]{:S(2)}) collective-permute-start(bf16[64,256]{1,0:T(8,128)(2,1)S(1)} %get-tuple-element.69), channel_id=1, source_target_pairs={{0,192},{64,0},{128,64},{192,128},{1,193},{65,1},{129,65},{193,129... | collective-permute-start | bytes 98312 | tf_op jit(solution)/shard_map/ppermute | solution.py:441
  (3 other events, 2.6 us)
